TPU v7x, 256 devices: a whole 4x4x8 slice. The times are simulated.
256 devices in a mesh: row: 16 (over z, x_hi), col: 4 (over y), grp: 4 (over x_lo, core).
Axes of the slice: x: 4 (x_hi: 2, x_lo: 2; x = x_hi * 2 + x_lo), y: 4, z: 8, core: 2. Of those that a mesh axis runs over, the one named last changes fastest.
Arguments:
- act: bfloat16 [32, 1024, 768], P('grp', 'row'), may hold values from -6 to 6
- cond: bfloat16 [32, 1024, 384], P('grp', 'row'), may hold values from -6 to 6
- pair: bfloat16 [1024, 1024, 128], P('row', ('col', 'grp')), may hold values from -6 to 6
- pair_gain: float32 [128], replicated, may hold values from 0.5 to 2
- chain_ids: int32 [1024], replicated, may hold values from 0 to 2, as said below
- bias_proj: bfloat16 [128, 16], replicated, may hold values from -24 to 24
- chain_bias: float32 [2, 16], replicated, may hold values from -4 to 4
- cond_gain: float32 [384], replicated, may hold values from 0.5 to 2
- ada_scale: bfloat16 [2, 384, 768], replicated, may hold values from -0.3125 to 0.3125
- ada_shift: bfloat16 [2, 384, 768], replicated, may hold values from -0.3125 to 0.3125
- qkvg: bfloat16 [768, 4, 768], P(None, None, 'col'), may hold values from -0.21875 to 0.21875
- attn_out: bfloat16 [768, 768], P('col'), may hold values from -0.21875 to 0.21875
- out_gate: bfloat16 [2, 384, 768], replicated, may hold values from -0.3125 to 0.3125
- trans_in: bfloat16 [768, 2, 1536], P(None, None, 'col'), may hold values from -0.21875 to 0.21875
- trans_out: bfloat16 [1536, 768], P('col'), may hold values from -0.15625 to 0.15625
Outputs:
- updated: bfloat16 [32, 1024, 768], P('grp', 'row')
Inputs may be any that keep to these rules, and one draw needn't show every extreme that they name: `chain_ids`: chain numbers never fall along the tokens; each of the three chains holds at least one token.
All inputs are finite; a program needn't handle non-finite values.
Results may differ from a plain program's by a relative error of at most 0.017.
The roundings to bfloat16 on the way count: a program that leaves them out, or rounds other values in their place, can miss the bound.
Values may be sent and summed in bfloat16 or wider, within the bound.
No kernel may reach another device: no remote copies, remote signals or barrier semaphores. Data moves between devices by JAX's collectives and lax.ppermute only.
A program may use at most 128 MiB of HBM per device.

v0:
```python
import jax
import jax.numpy as jnp
from jax import lax
from jax.sharding import PartitionSpec as P

HD = 48


def norm_last(values_in):
    center = values_in - jnp.mean(values_in, axis=-1, keepdims=True)
    spread = jnp.mean(center * center, axis=-1, keepdims=True)
    return center * lax.rsqrt(spread + 1e-05)


def body(
    act,
    cond,
    pair,
    pair_gain,
    chain_ids,
    bias_proj,
    chain_bias,
    cond_gain,
    ada_scale,
    ada_shift,
    qkvg,
    attn_out,
    out_gate,
    trans_in,
    trans_out,
):
    sample_count, row_count, model_width = act.shape
    flat_rows = sample_count * row_count
    heads_local = qkvg.shape[2] // HD
    col_index = lax.axis_index("col")
    row_index = lax.axis_index("row")
    cond_norm = (norm_last(cond.astype(jnp.float32).reshape(flat_rows, -1)) * cond_gain).astype(
        jnp.bfloat16
    )
    act_norm = norm_last(act.astype(jnp.float32).reshape(flat_rows, model_width))

    def condition(weight):
        return jnp.dot(cond_norm, weight, preferred_element_type=jnp.float32)

    att_input = (
        jax.nn.sigmoid(condition(ada_scale[0])) * act_norm + condition(ada_shift[0])
    ).astype(jnp.bfloat16)
    trans_input = (
        jax.nn.sigmoid(condition(ada_scale[1])) * act_norm + condition(ada_shift[1])
    ).astype(jnp.bfloat16)
    projected = jnp.dot(
        att_input, qkvg.reshape(model_width, -1), preferred_element_type=jnp.float32
    ).reshape(flat_rows, 4, -1)
    queries = projected[:, 0].astype(jnp.bfloat16).reshape(sample_count, row_count, heads_local, HD)
    keys_local = projected[:, 1].astype(jnp.bfloat16).reshape(sample_count, row_count, -1)
    values_local = projected[:, 2].astype(jnp.bfloat16).reshape(sample_count, row_count, -1)
    gates = jax.nn.sigmoid(projected[:, 3])
    query_chain = lax.dynamic_slice_in_dim(chain_ids, row_index * row_count, row_count)
    same_chain = (query_chain[:, None] == chain_ids[None, :]).astype(jnp.float32)
    local_chain = lax.dynamic_slice_in_dim(chain_bias, col_index * heads_local, heads_local, 1)
    chain_term = (
        local_chain[0][:, None, None]
        + (local_chain[1] - local_chain[0])[:, None, None] * same_chain[None]
    )
    normed = (norm_last(pair.astype(jnp.float32)) * pair_gain).astype(jnp.bfloat16)
    flat_tile = normed.reshape(pair.shape[0] * pair.shape[1], pair.shape[2])
    tile_bias = jnp.dot(flat_tile, bias_proj, preferred_element_type=jnp.float32).astype(
        jnp.bfloat16
    )
    tile_bias = jnp.transpose(tile_bias.reshape(pair.shape[0], pair.shape[1], -1), (2, 0, 1))
    tile_bias = lax.all_gather(tile_bias, "grp", axis=2, tiled=True)
    pair_bias = lax.all_to_all(tile_bias, "col", split_axis=0, concat_axis=2, tiled=True)
    total_bias = pair_bias.astype(jnp.float32) + chain_term
    scale = HD ** (-0.5)
    start_max = jnp.full((sample_count, heads_local, row_count), -1e30, jnp.float32)
    pieces = (
        lax.all_gather(keys_local, "row", axis=1, tiled=True),
        lax.all_gather(values_local, "row", axis=1, tiled=True),
    )
    key_piece = pieces[0].reshape(sample_count, pieces[0].shape[1], heads_local, HD)
    value_piece = pieces[1].reshape(sample_count, pieces[1].shape[1], heads_local, HD)
    scores = (
        jnp.einsum("sqhd,skhd->shqk", queries, key_piece, preferred_element_type=jnp.float32)
        * scale
        + total_bias[None]
    )
    new_max = jnp.maximum(start_max, jnp.max(scores, axis=-1))
    weights = jnp.exp(scores - new_max[..., None])
    new_sum = jnp.sum(weights, axis=-1)
    product = jnp.einsum(
        "shqk,skhd->shqd",
        weights.astype(jnp.bfloat16),
        value_piece,
        preferred_element_type=jnp.float32,
    )
    attended = jnp.transpose(product / new_sum[..., None], (0, 2, 1, 3)).reshape(flat_rows, -1)
    mixed = (gates * attended).astype(jnp.bfloat16)
    attn_part = jnp.dot(mixed, attn_out, preferred_element_type=jnp.float32)
    inner = jnp.dot(
        trans_input, trans_in.reshape(model_width, -1), preferred_element_type=jnp.float32
    ).reshape(flat_rows, 2, -1)
    hidden = (jax.nn.silu(inner[:, 0]) * inner[:, 1]).astype(jnp.bfloat16)
    trans_part = jnp.dot(hidden, trans_out, preferred_element_type=jnp.float32)
    attn_gate = jax.nn.sigmoid(condition(out_gate[0]))
    trans_gate = jax.nn.sigmoid(condition(out_gate[1]))
    attn_total, trans_total = (
        lax.psum(attn_part.astype(jnp.bfloat16), "col").astype(jnp.float32),
        lax.psum(trans_part.astype(jnp.bfloat16), "col").astype(jnp.float32),
    )
    updated = attn_gate * attn_total + trans_gate * trans_total
    return updated.reshape(sample_count, row_count, model_width).astype(jnp.bfloat16)


def solution(mesh):
    in_specs = (
        P("grp", "row", None),
        P("grp", "row", None),
        P("row", ("col", "grp"), None),
        P(),
        P(),
        P(),
        P(),
        P(),
        P(),
        P(),
        P(None, None, "col"),
        P("col", None),
        P(),
        P(None, None, "col"),
        P("col", None),
    )
    out_specs = P("grp", "row", None)
    return jax.shard_map(body, mesh=mesh, in_specs=in_specs, out_specs=out_specs, check_vma=False)
```

profile of v0, /device:TPU:1, one launch (start us, length us, event | category | flops | bytes accessed | tf_op | source)
XLA Modules:
  0.0 302.3 jit_solution(10379321636345688175)
XLA Ops:
  6.5 0.0 all-gather.3.cloned.1.call-start
  6.6 1.5 convert_reduce_fusion.2
  8.1 1.5 multiply_reduce_fusion
  9.5 0.1 div.58
  9.6 0.1 convert_reduce_fusion.1
  9.8 0.3 fusion.27
  10.1 0.1 rsqrt.29
  10.2 0.0 copy-done.10
  10.2 0.2 fusion.29
  10.4 0.0 copy-done.3
  10.4 1.5 fusion.13
  11.9 1.7 fusion.39
  13.6 4.2 %fusion.71 = (bf16[512,4,192]{0,2,1:T(8,128)(2,1)}, f32[512,4,192]{0,2,1:T(8,128)}) fusion(bf16[768,4,192]{0,2,1:T(8,128)(2,1)S(1)} %copy-done, f32[512,768]{1,0:T(8,128)} %fusion.39, f32[512,768]{1,0:T(8,128)S(1)} %copy-done.5, bf16[512,384]{1,0:T(8,128)(2,1)S(1)} %bitcast.117, bf16[2,384,768]{2,1,0:T(8,128)(2,1)} %param.23), kind=kOutput, calls=%fused_computation.91 | convolution fusion | flops 908722176 | bytes 7667712 | tf_op jit(solution)/shard_map/dot_general | solution.py:51
  17.9 1.9 fusion.70
  19.8 0.8 copy.39
  20.6 0.0 all-gather.3.cloned.1.call-update
  20.6 0.0 copy-start.12
  20.6 0.0 all-gather.5.cloned.1.call-start
  20.7 0.8 copy.45
  21.5 0.0 all-gather.5.cloned.1.call-update
  21.6 0.6 convert_reduce_fusion
  22.2 0.0 copy-start.8
  22.2 1.3 fusion.10
  23.5 1.3 fusion.12
  24.8 0.4 convolution_convert_fusion
  25.2 0.3 reshape.264
  25.5 0.3 copy.42
  25.7 11.4 %all_gather.10 = bf16[16,64,256]{1,0,2:T(8,128)(2,1)S(1)} all-gather(bf16[16,64,64]{1,0,2:T(8,128)(2,1)S(1)} %bitcast.129), channel_id=1, replica_groups=mesh['row'=16,'col'=4,'grp'=4] {'grp'}, dimensions={2}, use_global_device_ids=true | all-gather | bytes 655360 | tf_op jit(solution)/shard_map/all_gather | solution.py:71
  37.1 1.6 copy.43
  38.7 4.2 %all-to-all-start = ((bf16[16,64,256]{2,1,0:T(8,128)(2,1)}), bf16[16,64,256]{2,1,0:T(8,128)(2,1)S(1)}, u32[]{:S(2)}, u32[]{:S(2)}) async-start(bf16[16,64,256]{2,1,0:T(8,128)(2,1)} %copy.43), calls=%async_computation | async-start | bytes 1048576 | tf_op jit(solution)/shard_map/all_to_all | solution.py:72
  42.9 0.0 all-reduce.3.cloned.1.call-start
  42.9 1.5 copy.50
  44.4 0.0 copy-start.9
  44.4 0.0 copy-start.11
  44.5 1.5 copy.48
  45.9 1.2 convert_element_type.102
  47.1 0.1 dynamic_slice.7
  47.2 0.1 constant_dynamic-slice_fusion
  47.3 0.8 compare_convert_fusion
  48.1 2.8 fusion.34
  50.8 5.0 %fusion.21 = f32[512,2,384]{2,0,1:T(8,128)} fusion(bf16[2,384,768]{2,1,0:T(8,128)(2,1)} %bitcast.128, f32[512,768]{1,0:T(8,128)} %fusion.34, f32[512,768]{1,0:T(8,128)} %fusion.13, bf16[512,384]{1,0:T(8,128)(2,1)S(1)} %bitcast.119, bf16[2,384,768]{2,1,0:T(8,128)(2,1)} %param.23), kind=kOutput, calls=%fused_computation.30 | convolution fusion | flops 908328960 | bytes 6881280 | tf_op jit(solution)/shard_map/dot_general | solution.py:99
  55.9 2.9 convolution_convert_fusion.2
  58.7 0.0 all-to-all-done
  58.7 0.1 convert_bitcast_fusion
  58.9 0.1 copy.49
  59.0 0.7 copy-done.7
  59.7 0.3 add_add_fusion
  60.0 61.4 %all-gather.3.cloned.1.call-done = bf16[8,1024,192]{2,1,0:T(8,128)(2,1)} async-done(((bf16[8,64,192]{2,1,0:T(8,128)(2,1)}), bf16[8,1024,192]{2,1,0:T(8,128)(2,1)}) %all-gather.3.cloned.1.call-update) | async-done | bytes 3145744 | tf_op jit(solution)/shard_map/all_gather | solution.py:77
  121.4 6.3 %copy.40 = bf16[8,1024,192]{1,2,0:T(8,128)(2,1)} copy(bf16[8,1024,192]{2,1,0:T(8,128)(2,1)} %all-gather.3.cloned.1.call-done) | data formatting | bytes 6291456 | tf_op jit(solution)/shard_map/all_gather | solution.py:77
  127.7 3.4 %fusion = (f32[8,4,64]{2,1,0:T(4,128)S(1)}, f32[8,4,64,1024]{3,2,1,0:T(8,128)S(1)}) fusion(f32[4,64,1024]{2,1,0:T(8,128)S(1)} %add_add_fusion, bf16[8,1024,4,48]{1,3,2,0:T(8,128)(2,1)} %bitcast.115, bf16[8,64,4,48]{1,0,3,2:T(8,128)(2,1)S(1)} %convert_element_type.102), kind=kOutput, calls=%fused_computation.2 | convolution fusion | flops 207616000 | bytes 12787712 | tf_op jit(solution)/shard_map/sqhd,skhd->shqk/dot_general | solution.py:83
  131.1 3.2 %copy-done.1 = f32[8,4,64,1024]{3,2,1,0:T(8,128)} copy-done((f32[8,4,64,1024]{3,2,1,0:T(8,128)}, f32[8,4,64,1024]{3,2,1,0:T(8,128)S(1)}, u32[]{:S(2)}) %copy-start.1) | copy-done | bytes 8388632
  134.2 1.9 fusion.1
  136.2 84.4 %all-gather.5.cloned.1.call-done = bf16[8,1024,192]{2,1,0:T(8,128)(2,1)} async-done(((bf16[8,64,192]{2,1,0:T(8,128)(2,1)}), bf16[8,1024,192]{2,1,0:T(8,128)(2,1)}) %all-gather.5.cloned.1.call-update) | async-done | bytes 3145744 | tf_op jit(solution)/shard_map/all_gather | solution.py:78
  220.6 6.2 %copy.46 = bf16[8,1024,192]{1,2,0:T(8,128)(2,1)} copy(bf16[8,1024,192]{2,1,0:T(8,128)(2,1)} %all-gather.5.cloned.1.call-done) | data formatting | bytes 6291456 | tf_op jit(solution)/shard_map/all_gather | solution.py:78
  226.8 6.5 %fusion.22 = f32[8,64,4,48]{1,3,2,0:T(8,128)S(1)} fusion(bf16[8,1024,4,48]{1,3,2,0:T(8,128)(2,1)} %bitcast.125, f32[8,4,64,1024]{3,2,1,0:T(8,128)} %copy-done.1, f32[8,4,64]{2,1,0:T(4,128)S(1)} %broadcast_maximum_fusion, f32[4,64,1024]{2,1,0:T(8,128)S(1)} %add_add_fusion, f32[8,64,4]{1,2,0:T(4,128)S(1)} %bitcast.132), kind=kOutput, calls=%fused_computation.35 | convolution fusion | flops 209813504 | bytes 12992512 | tf_op jit(solution)/shard_map/shqk,skhd->shqd/dot_general | solution.py:90
  233.4 0.0 copy-start.14
  233.4 0.5 copy.47
  233.8 0.2 reshape.266
  234.1 0.3 copy-done.14
  234.3 2.4 convolution_convert_fusion.1
  236.7 0.0 all-reduce.3.cloned.1.call-update
  236.7 1.6 fusion.43
  238.3 54.0 %all-reduce.3.cloned.1.call-done = (bf16[512,768]{1,0:T(8,128)(2,1)}, bf16[512,768]{1,0:T(8,128)(2,1)}) async-done(((bf16[512,768]{1,0:T(8,128)(2,1)}, bf16[512,768]{1,0:T(8,128)(2,1)}), (bf16[512,768]{1,0:T(8,128)(2,1)}, bf16[512,768]{1,0:T(8,128)(2,1)})) %all-reduce.3.cloned.1.call-update) | async-done | bytes 1572880 | tf_op jit(solution)/shard_map/psum | solution.py:108
  292.3 3.4 %add_convert_fusion = bf16[512,768]{1,0:T(8,128)(2,1)} fusion(bf16[512,768]{1,0:T(8,128)(2,1)} %get-tuple-element.5, bf16[512,768]{1,0:T(8,128)(2,1)} %get-tuple-element.6, f32[512,768]{1,0:T(8,128)S(1)} %fusion.43, bf16[512,384]{1,0:T(8,128)(2,1)S(1)} %bitcast.121, bf16[2,384,768]{2,1,0:T(8,128)(2,1)} %param.27), kind=kOutput, calls=%fused_computation.19 | convolution fusion | flops 306708480 | bytes 4915200 | tf_op jit(solution)/shard_map/dot_general | solution.py:43
  (29 shorter events, 0.1 us)
Async XLA Ops:
  6.5 7.1 %copy-start = (bf16[768,4,192]{0,2,1:T(8,128)(2,1)S(1)}, bf16[768,4,192]{0,2,1:T(8,128)(2,1)}, u32[]{:S(2)}) copy-start(bf16[768,4,192]{0,2,1:T(8,128)(2,1)} %param.25) | copy-start | bytes 3538948
  6.5 3.9 %copy-start.3 = (bf16[8,64,768]{2,1,0:T(8,128)(2,1)S(1)}, bf16[8,64,768]{2,1,0:T(8,128)(2,1)}, u32[]{:S(2)}) copy-start(bf16[8,64,768]{2,1,0:T(8,128)(2,1)} %param.15) | copy-start | bytes 2359300
  6.5 3.1 %copy-start.4 = (bf16[8,64,384]{2,1,0:T(8,128)(2,1)S(1)}, bf16[8,64,384]{2,1,0:T(8,128)(2,1)}, u32[]{:S(2)}) copy-start(bf16[8,64,384]{2,1,0:T(8,128)(2,1)} %param.16) | copy-start | bytes 1179652
  6.5 3.6 %copy-start.10 = (f32[384]{0:T(512)S(1)}, f32[384]{0:T(512)}, u32[]{:S(2)}) copy-start(f32[384]{0:T(512)} %param.22) | copy-start | bytes 4612
  6.5 114.8 %all-gather.3.cloned.1.call-start = ((), (), s32[]{:S(2)}) async-start(), calls=%async_computation.1 | async-start | bytes 4456448 | tf_op jit(solution)/shard_map/all_gather | solution.py:77
  10.2 1.7 copy-start.6
  11.9 1.7 copy-start.5
  17.9 3.7 %copy-start.2 = (bf16[64,64,128]{2,1,0:T(8,128)(2,1)S(1)}, bf16[64,64,128]{2,1,0:T(8,128)(2,1)}, u32[]{:S(2)}) copy-start(bf16[64,64,128]{2,1,0:T(8,128)(2,1)} %param.17) | copy-start | bytes 3145732
  20.6 2.9 copy-start.12
  20.6 200.0 %all-gather.5.cloned.1.call-start = ((), (), s32[]{:S(2)}) async-start(), calls=%async_computation.2 | async-start | bytes 4456448 | tf_op jit(solution)/shard_map/all_gather | solution.py:78
  22.2 2.6 copy-start.8
  38.7 20.0 %all-to-all-start = ((bf16[16,64,256]{2,1,0:T(8,128)(2,1)}), bf16[16,64,256]{2,1,0:T(8,128)(2,1)S(1)}, u32[]{:S(2)}, u32[]{:S(2)}) async-start(bf16[16,64,256]{2,1,0:T(8,128)(2,1)} %copy.43), calls=%async_computation | async-start | bytes 1048576 | tf_op jit(solution)/shard_map/all_to_all | solution.py:72
  42.9 249.4 %all-reduce.3.cloned.1.call-start = ((), (), s32[]{:S(2)}) async-start(), calls=%async_computation.3 | async-start | bytes 3145728 | tf_op jit(solution)/shard_map/psum | solution.py:108
  44.4 2.7 copy-start.9
  44.4 2.7 copy-start.11
  50.8 5.0 %copy-start.13 = (bf16[384,768]{1,0:T(8,128)(2,1)S(1)}, bf16[384,768]{1,0:T(8,128)(2,1)}, u32[]{:S(2)}) copy-start(bf16[384,768]{1,0:T(8,128)(2,1)} %param.29) | copy-start | bytes 1769476
  58.7 1.0 copy-start.7
  131.0 3.2 %copy-start.1 = (f32[8,4,64,1024]{3,2,1,0:T(8,128)}, f32[8,4,64,1024]{3,2,1,0:T(8,128)S(1)}, u32[]{:S(2)}) copy-start(f32[8,4,64,1024]{3,2,1,0:T(8,128)S(1)} %get-tuple-element.13) | copy-start | bytes 25165828
  233.4 1.0 copy-start.14
Sparse Core Ops, SparseCore 0:
  20.8 100.5 all-gather.2
  124.0 96.5 all-gather.4
  236.8 55.4 all-reduce.2
where the time goes:
time: 303 us; the launch traced here: 302 us
  waiting for transfers between devices  200 us (66%)
  matrix products  34.3 us (11%)
  local copies, waits for them, and re-layouts  27.7 us (9%)
  between operations  13.4 us (4%)
  other arithmetic  11.4 us (4%)
  blocking collectives  11.4 us (4%)
  starting transfers between devices  4.26 us (1%)
    all_gather x1, waiting for transfers between devices, body(): lax.all_gather(values_local, 'row', axis=1, tiled=True)  84.4 us
    all_gather x1, waiting for transfers between devices, body(): lax.all_gather(keys_local, 'row', axis=1, tiled=True)  61.4 us
    psum x1, waiting for transfers between devices, body(): lax.psum(trans_part.astype(jnp.bfloat16), 'col').astype(jnp.float32)  54 us
    all_gather x1, blocking collectives, body(): tile_bias = lax.all_gather(tile_bias, 'grp', axis=2, tiled=True)  11.4 us
    dot_general x4, matrix products, condition(): return jnp.dot(cond_norm, weight, preferred_element_type=jnp.float32)  9.55 us
    dot_general x1, matrix products, body(): jnp.einsum('shqk,skhd->shqd', weights.astype(jnp.bfloat16), value_piece,...  6.51 us
    all_gather x1, local copies, waits for them, and re-layouts, body(): lax.all_gather(keys_local, 'row', axis=1, tiled=True)  6.27 us
    all_gather x1, local copies, waits for them, and re-layouts, body(): lax.all_gather(values_local, 'row', axis=1, tiled=True)  6.24 us
  transfers between devices with their start and end apart: 4, of which 3 were waited for; matrix products, arithmetic and copies ran while one was open for 12% of the time, Pallas kernels for 0%

commit v1 on v0

v1 whole, which is shorter than its diff:
```python
import jax
import jax.numpy as jnp
from jax import lax
from jax.experimental import pallas as pl
from jax.experimental.pallas import tpu as pltpu
from jax.sharding import PartitionSpec as P

HD = 48
BF = jnp.bfloat16
F32 = jnp.float32
NT = (((1,), (1,)), ((), ()))
TN = (((0,), (0,)), ((), ()))


def dot(left, right, dims=(((1,), (0,)), ((), ()))):
    return lax.dot_general(left, right, dims, preferred_element_type=F32)


def norm_last(values_in):
    center = values_in - jnp.mean(values_in, axis=-1, keepdims=True)
    spread = jnp.mean(center * center, axis=-1, keepdims=True)
    return center * lax.rsqrt(spread + 1e-05)


def params(mib=48):
    return pltpu.CompilerParams(vmem_limit_bytes=mib * 1024 * 1024)


def cost(flops, moved, exps=0):
    return pl.CostEstimate(flops=flops, bytes_accessed=moved, transcendentals=exps)


def whole(shape):
    zeros = (0,) * len(shape)
    return pl.BlockSpec(shape, lambda *_: zeros)


def tile_bias_kernel(pair_ref, gain_ref, proj_ref, out_ref):
    half, pairs, keys, width = pair_ref.shape
    rows = jnp.swapaxes(pair_ref[...].astype(F32), 0, 1).reshape(half * pairs * keys, width)
    normed = (norm_last(rows) * gain_ref[...]).astype(BF)
    heads = lax.dot_general(
        proj_ref[...], normed, (((0,), (1,)), ((), ())), preferred_element_type=F32
    )
    lanes = half * keys
    slabs = [heads[:, p * lanes : (p + 1) * lanes][:, None, :] for p in range(pairs)]
    out_ref[...] = jnp.concatenate(slabs, axis=1).astype(BF)


def tile_bias(pair, gain, proj):
    queries, keys, width = pair.shape
    heads = proj.shape[1]
    split = pair.reshape(2, queries // 2, keys, width)
    step = 16
    return pl.pallas_call(
        tile_bias_kernel,
        grid=(queries // 2 // step,),
        in_specs=[
            pl.BlockSpec((2, step, keys, width), lambda i: (0, i, 0, 0)),
            whole((1, width)),
            whole((width, heads)),
        ],
        out_specs=pl.BlockSpec((heads, step, 2 * keys), lambda i: (0, i, 0)),
        out_shape=jax.ShapeDtypeStruct((heads, queries // 2, 2 * keys), BF),
        compiler_params=params(),
        cost_estimate=cost(2 * queries * keys * width * heads, queries * keys * width * 2),
        name="tile_bias",
    )(split, gain.reshape(1, width), proj)


def spread_bias_kernel(in_ref, out_ref):
    cols, heads, pairs, lanes = in_ref.shape
    keys = lanes // 2
    copies = out_ref.shape[0] // heads
    for head in range(heads):
        parts = [in_ref[c, head] for c in range(cols)]
        low = jnp.concatenate([p[:, :keys] for p in parts], axis=1)
        high = jnp.concatenate([p[:, keys:] for p in parts], axis=1)
        for copy in range(copies):
            out_ref[head * copies + copy, :pairs] = low
            out_ref[head * copies + copy, pairs:] = high


def spread_bias(tiles, dests):
    cols, heads, pairs, lanes = tiles.shape
    shape = (dests, 2 * pairs, cols * lanes // 2)
    return pl.pallas_call(
        spread_bias_kernel,
        in_specs=[whole(tiles.shape)],
        out_specs=whole(shape),
        grid=(1,),
        out_shape=jax.ShapeDtypeStruct(shape, BF),
        compiler_params=params(),
        cost_estimate=cost(0, tiles.size * 2 + 2 * dests * pairs * cols * lanes),
        name="spread_bias",
    )(tiles)


def project_kernel(act_ref, cond_ref, gain_ref, scale_ref, shift_ref, w_ref, qkv_ref, gate_ref, cn_ref):
    heads, pairs, _, lanes = qkv_ref.shape
    cond_norm = (norm_last(cond_ref[...].astype(F32)) * gain_ref[...]).astype(BF)
    cn_ref[...] = cond_norm
    act_norm = norm_last(act_ref[...].astype(F32))
    att = (
        jax.nn.sigmoid(dot(cond_norm, scale_ref[0])) * act_norm + dot(cond_norm, shift_ref[0])
    ).astype(BF)
    part = heads * HD
    for which in range(3):
        result = dot(w_ref[which], att, NT).astype(BF)
        for head in range(heads):
            for p in range(pairs):
                qkv_ref[head, p, which * HD : (which + 1) * HD, :] = result[
                    head * HD : (head + 1) * HD, p * lanes : (p + 1) * lanes
                ]
    gate_ref[...] = jax.nn.sigmoid(dot(w_ref[3], att, NT))


def project(act, cond, gain, scale, shift, w):
    rows, width = act.shape
    cwidth = cond.shape[1]
    part = w.shape[1]
    heads = part // HD
    step = 256
    lanes = 128
    pairs = rows // lanes
    return pl.pallas_call(
        project_kernel,
        grid=(rows // step,),
        in_specs=[
            pl.BlockSpec((step, width), lambda i: (i, 0)),
            pl.BlockSpec((step, cwidth), lambda i: (i, 0)),
            whole((1, cwidth)),
            whole((1, cwidth, width)),
            whole((1, cwidth, width)),
            whole(w.shape),
        ],
        out_specs=[
            pl.BlockSpec((heads, step // lanes, 3 * HD, lanes), lambda i: (0, i, 0, 0)),
            pl.BlockSpec((part, step), lambda i: (0, i)),
            pl.BlockSpec((step, cwidth), lambda i: (i, 0)),
        ],
        out_shape=[
            jax.ShapeDtypeStruct((heads, pairs, 3 * HD, lanes), BF),
            jax.ShapeDtypeStruct((part, rows), F32),
            jax.ShapeDtypeStruct((rows, cwidth), BF),
        ],
        compiler_params=params(),
        cost_estimate=cost(
            2 * rows * width * (2 * cwidth + 4 * part), 4 * cwidth * width + 8 * width * part
        ),
        name="project",
    )(act, cond, gain.reshape(1, cwidth), scale, shift, w)


def transition_kernel(act_ref, cn_ref, scale_ref, shift_ref, og_ref, win_ref, wout_ref, part_ref, g0_ref, g1_ref):
    cond_norm = cn_ref[...]
    act_norm = norm_last(act_ref[...].astype(F32))
    tin = (
        jax.nn.sigmoid(dot(cond_norm, scale_ref[0])) * act_norm + dot(cond_norm, shift_ref[0])
    ).astype(BF)
    inner = dot(tin, win_ref[...])
    units = wout_ref.shape[0]
    first = inner[:, :units]
    hidden = (first * jax.nn.sigmoid(first) * inner[:, units:]).astype(BF)
    part_ref[...] = dot(hidden, wout_ref[...]).astype(BF)
    g0_ref[...] = jax.nn.sigmoid(dot(cond_norm, og_ref[0]))
    g1_ref[...] = jax.nn.sigmoid(dot(cond_norm, og_ref[1]))


def transition(act, cond_norm, scale, shift, out_gate, w_in, w_out):
    rows, width = act.shape
    cwidth = cond_norm.shape[1]
    step = 256
    second = pl.BlockSpec((1, cwidth, width), lambda i: (1, 0, 0))
    row_block = pl.BlockSpec((step, width), lambda i: (i, 0))
    return pl.pallas_call(
        transition_kernel,
        grid=(rows // step,),
        in_specs=[
            row_block,
            pl.BlockSpec((step, cwidth), lambda i: (i, 0)),
            second,
            second,
            whole(out_gate.shape),
            whole(w_in.shape),
            whole(w_out.shape),
        ],
        out_specs=[row_block, row_block, row_block],
        out_shape=[
            jax.ShapeDtypeStruct((rows, width), BF),
            jax.ShapeDtypeStruct((rows, width), F32),
            jax.ShapeDtypeStruct((rows, width), F32),
        ],
        compiler_params=params(),
        cost_estimate=cost(
            2 * rows * (4 * cwidth * width + w_in.size + w_out.size),
            8 * cwidth * width + 2 * w_in.size + 2 * w_out.size + rows * width * 12,
        ),
        name="transition",
    )(act, cond_norm, scale, shift, out_gate, w_in, w_out)


def attention_kernel(place_ref, chain_ref, qkv_ref, b0, b1, b2, b3, qid_ref, kid_ref, out_ref, k_ref, v_ref):
    samples, pieces, _, span = k_ref.shape
    half = qkv_ref.shape[2] // samples
    cols = span // half
    mine = place_ref[0]

    @pl.when(pl.program_id(0) == 0)
    def _():
        for piece in range(pieces):
            for s in range(samples):
                lanes = slice(s * half, (s + 1) * half)
                blocks = [qkv_ref[c * pieces + (mine ^ piece)] for c in range(cols)]
                k_ref[s, piece] = jnp.concatenate([b[HD : 2 * HD, lanes] for b in blocks], axis=1)
                v_ref[s, piece] = jnp.concatenate([b[2 * HD :, lanes] for b in blocks], axis=1)

    step = pl.program_id(0)
    other, same = chain_ref[0], chain_ref[1]
    qid = qid_ref[...]
    totals = []
    for piece, ref in enumerate((b0, b1, b2, b3)):
        bias = ref[...].reshape(2 * half, span).astype(F32)
        totals.append(bias + jnp.where(qid == kid_ref[mine ^ piece], same, other))
    scale = HD ** (-0.5)
    results = []
    first, second = qkv_ref[2 * step], qkv_ref[2 * step + 1]
    for s in range(samples):
        lanes = slice(s * half, (s + 1) * half)
        query = jnp.concatenate([first[:HD, lanes], second[:HD, lanes]], axis=1)
        scores = [
            lax.dot_general(query, k_ref[s, p], TN, preferred_element_type=F32) * scale + totals[p]
            for p in range(pieces)
        ]
        top = jnp.max(
            jnp.maximum(jnp.maximum(scores[0], scores[1]), jnp.maximum(scores[2], scores[3])),
            axis=1,
            keepdims=True,
        )
        weights = [jnp.exp(x - top) for x in scores]
        total = jnp.sum(
            (weights[0] + weights[1]) + (weights[2] + weights[3]), axis=1, keepdims=True
        )
        summed = sum(
            dot(weights[p].astype(BF), v_ref[s, p], NT) for p in range(pieces)
        )
        results.append(jnp.transpose(summed / total).astype(BF))
    out_ref[0] = jnp.concatenate([r[:, :half] for r in results], axis=1)
    out_ref[1] = jnp.concatenate([r[:, half:] for r in results], axis=1)


def attention(place, chain, qkv, biases, qid, kid):
    blocks, rows, lanes = qkv.shape
    half = lanes // 2
    span = biases[0].shape[2]
    bias_spec = pl.BlockSpec((2, half, span), lambda i: (i, 0, 0))
    tokens = blocks * half
    return pl.pallas_call(
        attention_kernel,
        grid=(blocks // 2,),
        in_specs=[
            pl.BlockSpec(memory_space=pltpu.SMEM),
            pl.BlockSpec(memory_space=pltpu.SMEM),
            whole(qkv.shape),
            bias_spec,
            bias_spec,
            bias_spec,
            bias_spec,
            pl.BlockSpec((2 * half, 1), lambda i: (i, 0)),
            whole(kid.shape),
        ],
        out_specs=pl.BlockSpec((2, HD, lanes), lambda i: (i, 0, 0)),
        out_shape=jax.ShapeDtypeStruct((blocks, HD, lanes), BF),
        scratch_shapes=[
            pltpu.VMEM((2, 4, HD, span), BF),
            pltpu.VMEM((2, 4, HD, span), BF),
        ],
        compiler_params=params(),
        cost_estimate=cost(8 * tokens * tokens * HD, 3_000_000, 2 * tokens * tokens),
        name="attention",
    )(place, chain, qkv, *biases, qid, kid)


def mix_kernel(gate_ref, o_ref, out_ref):
    dests, _, lanes = o_ref.shape
    pairs = out_ref.shape[1] // lanes
    for r in range(dests):
        rows = slice(r // pairs * HD, (r // pairs + 1) * HD)
        cols = slice(r % pairs * lanes, (r % pairs + 1) * lanes)
        out_ref[rows, cols] = (gate_ref[rows, cols] * o_ref[r].astype(F32)).astype(BF)


def mix(gates, attended):
    return pl.pallas_call(
        mix_kernel,
        grid=(1,),
        in_specs=[whole(gates.shape), whole(attended.shape)],
        out_specs=whole(gates.shape),
        out_shape=jax.ShapeDtypeStruct(gates.shape, BF),
        compiler_params=params(),
        cost_estimate=cost(gates.size, gates.size * 8),
        name="mix",
    )(gates, attended)


def finish_kernel(col_ref, m0, m1, m2, m3, w_ref, g0_ref, g1_ref, trans_ref, out_ref):
    mine = col_ref[0]
    total = None
    for shift, ref in enumerate((m0, m1, m2, m3)):
        term = lax.dot_general(
            ref[...], w_ref[(mine + shift) % 4], TN, preferred_element_type=F32
        )
        total = term if total is None else total + term
    out_ref[...] = (g0_ref[...] * total + g1_ref[...] * trans_ref[...].astype(F32)).astype(BF)


def finish(col, mixed, w, g0, g1, trans):
    rows, width = trans.shape
    part = mixed[0].shape[0]
    step = 256
    row_block = pl.BlockSpec((step, width), lambda i: (i, 0))
    piece = pl.BlockSpec((part, step), lambda i: (0, i))
    return pl.pallas_call(
        finish_kernel,
        grid=(rows // step,),
        in_specs=[
            pl.BlockSpec(memory_space=pltpu.SMEM),
            piece,
            piece,
            piece,
            piece,
            whole(w.shape),
            row_block,
            row_block,
            row_block,
        ],
        out_specs=row_block,
        out_shape=jax.ShapeDtypeStruct((rows, width), BF),
        compiler_params=params(),
        cost_estimate=cost(2 * rows * 4 * part * width, rows * width * 16),
        name="finish",
    )(col, *mixed, w, g0, g1, trans)


def swap(x, bit):
    return lax.ppermute(x, "grp", [(i, i ^ bit) for i in range(4)])


def body(
    act,
    cond,
    pair,
    pair_gain,
    chain_ids,
    bias_proj,
    chain_bias,
    cond_gain,
    ada_scale,
    ada_shift,
    qkvg,
    attn_out,
    out_gate,
    trans_in,
    trans_out,
):
    samples, rows, width = act.shape
    flat = samples * rows
    part = qkvg.shape[2]
    heads = part // HD
    col = lax.axis_index("col")
    row = lax.axis_index("row")
    grp = lax.axis_index("grp")
    act = act.reshape(flat, width)
    cond = cond.reshape(flat, cond.shape[2])
    tiles = tile_bias(pair, pair_gain, bias_proj)
    tiles = tiles.reshape(4, heads, *tiles.shape[1:])
    tiles = lax.all_to_all(tiles, "col", 0, 0, tiled=True)
    bias0 = lax.all_to_all(spread_bias(tiles, 16), "row", 0, 0, tiled=True)
    w_proj = jnp.transpose(qkvg, (1, 2, 0))
    qkv, gates, cond_norm = project(act, cond, cond_gain, ada_scale, ada_shift, w_proj)
    qkv = lax.all_to_all(qkv.reshape(16, 3 * HD, 128), "row", 0, 0, tiled=True)
    bias2 = swap(bias0, 2)
    bias1 = swap(bias0, 1)
    bias3 = swap(bias2, 1)
    w_out_full = lax.all_gather(attn_out, "col", axis=0, tiled=True)
    trans_part, g0, g1 = transition(
        act, cond_norm, ada_scale, ada_shift, out_gate, trans_in.reshape(width, -1), trans_out
    )
    trans_total = lax.psum(trans_part, "col")
    head = col * heads + row // 4
    chain = lax.dynamic_slice_in_dim(chain_bias, head, 1, 1).reshape(2)
    qid = chain_ids.reshape(-1, 1)
    kid = jnp.transpose(chain_ids.reshape(4, 4, rows), (1, 0, 2)).reshape(4, 1, 4 * rows)
    attended = attention(
        grp.astype(jnp.int32).reshape(1), chain, qkv, (bias0, bias1, bias2, bias3), qid, kid
    )
    attended = lax.all_to_all(attended, "row", 0, 0, tiled=True)
    mixed = mix(gates, attended)
    pieces = [mixed] + [
        lax.ppermute(mixed, "col", [((i + k) % 4, i) for i in range(4)]) for k in (1, 2, 3)
    ]
    updated = finish(
        col.astype(jnp.int32).reshape(1),
        pieces,
        w_out_full.reshape(4, part, width),
        g0,
        g1,
        trans_total,
    )
    return updated.reshape(samples, rows, width)


def solution(mesh):
    in_specs = (
        P("grp", "row", None),
        P("grp", "row", None),
        P("row", ("col", "grp"), None),
        P(),
        P(),
        P(),
        P(),
        P(),
        P(),
        P(),
        P(None, None, "col"),
        P("col", None),
        P(),
        P(None, None, "col"),
        P("col", None),
    )
    out_specs = P("grp", "row", None)
    return jax.shard_map(body, mesh=mesh, in_specs=in_specs, out_specs=out_specs, check_vma=False)
```

time: 303 us -> 151 us (0.50)
  waiting for transfers between devices: 200 us -> 36.7 us
  matrix products: 34.3 us -> 0 us
  Pallas kernels: 0 us -> 26.4 us
  starting transfers between devices: 4.26 us -> 27.8 us
  other arithmetic: 11.4 us -> 0 us
  blocking collectives: 11.4 us -> 20.4 us
    all_gather x2 -> x1, waiting for transfers between devices: 146 us -> 6.42 us  [body(): w_out_full = lax.all_gather(attn_out, 'col', axis=0, tiled=True)]
    psum x1, waiting for transfers between devices: 54 us -> 0.01 us  [body(): trans_total = lax.psum(trans_part, 'col')]
    dot_general x11 -> x0, matrix products: 34.3 us -> none  [the longest x4 9.55 us: condition(): return jnp.dot(cond_norm, weight, preferred_element_type=jnp.float32)]
    pallas_call x0 -> x7, Pallas kernels: none -> 26.4 us  [the longest x1 11.3 us: attention(): pl.pallas_call(attention_kernel, grid=(blocks // 2,), in_specs=[pl.BlockS...]
    ppermute x0 -> x6, waiting for transfers between devices: none -> 22.4 us  [the longest x3 16.4 us: swap(): return lax.ppermute(x, 'grp', [(i, i ^ bit) for i in range(4)])]
    all_to_all x0 -> x1, blocking collectives: none -> 20.4 us  [body(): attended = lax.all_to_all(attended, 'row', 0, 0, tiled=True)]
    unnamed x31 -> x64, local copies, waits for them, and re-layouts: 5.73 us -> 23.4 us
    all_to_all x1 -> x3, starting transfers between devices: 4.18 us -> 20.3 us  [the longest x1 10.8 us: body(): bias0 = lax.all_to_all(spread_bias(tiles, 16), 'row', 0, 0, tiled=True)]
  transfers between devices with their start and end apart: 4 -> 11, of which waited for: 3 -> 4; matrix products, arithmetic and copies ran while one was open for 12% -> 3% of each run, Pallas kernels for 0% -> 13%
where the time goes in v1:
time: 151 us; the launch traced here: 150 us
  waiting for transfers between devices  36.7 us (24%)
  starting transfers between devices  27.8 us (18%)
  Pallas kernels  26.4 us (17%)
  local copies, waits for them, and re-layouts  24.8 us (16%)
  blocking collectives  20.4 us (14%)
  between operations  13.5 us (9%)
    unnamed x64, local copies, waits for them, and re-layouts  23.4 us
    all_to_all x1, blocking collectives, body(): attended = lax.all_to_all(attended, 'row', 0, 0, tiled=True)  20.4 us
    ppermute x3, waiting for transfers between devices, swap(): return lax.ppermute(x, 'grp', [(i, i ^ bit) for i in range(4)])  16.4 us
    pallas_call x1, Pallas kernels, attention(): pl.pallas_call(attention_kernel, grid=(blocks // 2,), in_specs=[pl.BlockS...  11.3 us
    all_to_all x1, starting transfers between devices, body(): bias0 = lax.all_to_all(spread_bias(tiles, 16), 'row', 0, 0, tiled=True)  10.8 us
    all_to_all x1, waiting for transfers between devices, body(): bias0 = lax.all_to_all(spread_bias(tiles, 16), 'row', 0, 0, tiled=True)  7.16 us
    all_gather x1, waiting for transfers between devices, body(): w_out_full = lax.all_gather(attn_out, 'col', axis=0, tiled=True)  6.42 us
    pallas_call x1, Pallas kernels, transition(): pl.pallas_call(transition_kernel, grid=(rows // step,), in_specs=[row_blo...  5.97 us
  transfers between devices with their start and end apart: 11, of which 4 were waited for; matrix products, arithmetic and copies ran while one was open for 3% of the time, Pallas kernels for 13%

profile of v1, /device:TPU:1, one launch (start us, length us, event | category | flops | bytes accessed | tf_op | source)
XLA Modules:
  0.0 149.6 jit_solution(8246897010131463592)
XLA Ops:
  6.5 0.0 copy-start
  6.5 0.8 copy.17.proj_ref
  7.4 1.2 copy-done.7
  8.6 0.7 copy-done.18
  9.3 2.4 %tile_bias.1 = bf16[16,32,128]{2,1,0:T(8,128)(2,1)} custom-call(bf16[2,32,64,128]{3,2,1,0:T(8,128)(2,1)S(1)} %bitcast.17, f32[1,128]{1,0:T(1,128)S(1)} %bitcast.22, bf16[128,16]{1,0:T(8,128)(2,1)S(1)} %copy.17.proj_ref), custom_call_target="tpu_custom_call" | custom-call | flops 16777216 | bytes 1048576 | tf_op jit(solution)/shard_map/tile_bias/pallas_call | solution.py:55
  11.7 5.0 %all-to-all-start.1 = ((bf16[4,4,32,128]{3,2,1,0:T(8,128)(2,1)}), bf16[4,4,32,128]{3,2,1,0:T(8,128)(2,1)S(1)}, u32[]{:S(2)}, u32[]{:S(2)}) async-start(bf16[4,4,32,128]{3,2,1,0:T(8,128)(2,1)} %bitcast.8), calls=%async_computation.1 | async-start | bytes 262144 | tf_op jit(solution)/shard_map/all_to_all | solution.py:377
  16.7 0.0 copy-done.30
  16.7 0.0 copy-start.4
  16.7 2.7 %copy.20 = bf16[96,8,2,384]{3,1,2,0:T(8,128)(2,1)} copy(bf16[96,8,2,384]{3,2,1,0:T(2,128)(2,1)} %bitcast.23) | data formatting | bytes 2359296
  19.4 0.0 copy-done.5
  19.4 0.0 copy-done.4
  19.4 0.0 copy-start.8
  19.4 1.1 copy-done.8
  20.6 1.0 copy-done.17
  21.6 2.7 %project.1 = (bf16[4,4,144,128]{3,2,1,0:T(8,128)(2,1)S(1)}, f32[192,512]{1,0:T(8,128)S(1)}, bf16[512,384]{1,0:T(8,128)(2,1)S(1)}) custom-call(bf16[512,768]{1,0:T(8,128)(2,1)S(1)} %bitcast.18, bf16[512,384]{1,0:T(8,128)(2,1)S(1)} %bitcast.21, f32[1,384]{1,0:T(1,128)S(1)} %reshape.51.gain_ref, bf16[2,384,768]{2,1,0:T(8,128)(2,1)S(1)} %copy-done.4, ...), custom_call_target="tpu_custom_call" | custom-call | flops 1207959552 | bytes 2359296 | tf_op jit(solution)/shard_map/project/pallas_call | solution.py:126
  24.3 0.0 copy-start.11
  24.3 0.8 copy-done.11
  25.1 0.8 copy-done.15
  25.9 0.7 copy-done.27
  26.7 0.0 all-to-all-done.1.in_ref
  26.7 0.9 spread_bias.1
  27.6 10.8 %all-to-all-start.2 = ((bf16[16,64,256]{2,1,0:T(8,128)(2,1)}), bf16[16,64,256]{2,1,0:T(8,128)(2,1)}, u32[]{:S(2)}, u32[]{:S(2)}) async-start(bf16[16,64,256]{2,1,0:T(8,128)(2,1)} %spread_bias.1), calls=%async_computation.2 | async-start | bytes 1048576 | tf_op jit(solution)/shard_map/all_to_all | solution.py:378
  38.4 0.0 all-reduce.2.cloned.1.call-start
  38.4 0.0 copy-start.19
  38.5 1.3 copy-done.19
  39.7 1.1 copy-done.20
  40.8 1.0 copy-done.28
  41.8 6.0 %transition.1 = (bf16[512,768]{1,0:T(8,128)(2,1)}, f32[512,768]{1,0:T(8,128)}, f32[512,768]{1,0:T(8,128)}) custom-call(bf16[512,768]{1,0:T(8,128)(2,1)S(1)} %bitcast.19, bf16[512,384]{1,0:T(8,128)(2,1)S(1)} %copy-done.28, bf16[2,384,768]{2,1,0:T(8,128)(2,1)S(1)} %copy-done.4, bf16[2,384,768]{2,1,0:T(8,128)(2,1)S(1)} %copy-done.5, ...), custom_call_target="tpu_custom_call" | custom-call | flops 2113929216 | bytes 8847360 | tf_op jit(solution)/shard_map/transition/pallas_call | solution.py:176
  47.8 0.0 all-reduce.2.cloned.1.call-update
  47.8 0.0 all-gather.2.cloned.1.call-start
  47.8 0.7 all-gather.2.cloned.1.call-update
  48.5 7.2 %all-to-all-done.2.b0 = bf16[16,64,256]{2,1,0:T(8,128)(2,1)} async-done(((bf16[16,64,256]{2,1,0:T(8,128)(2,1)}), bf16[16,64,256]{2,1,0:T(8,128)(2,1)}, u32[]{:S(2)}, u32[]{:S(2)}) %all-to-all-start.2) | async-done | bytes 524320 | tf_op jit(solution)/shard_map/all_to_all | solution.py:378
  55.7 4.5 %all-to-all-start = ((bf16[16,144,128]{2,1,0:T(8,128)(2,1)}), bf16[16,144,128]{2,1,0:T(8,128)(2,1)S(1)}, u32[]{:S(2)}, u32[]{:S(2)}) async-start(bf16[16,144,128]{2,1,0:T(8,128)(2,1)} %bitcast.20), calls=%async_computation | async-start | bytes 1179648 | tf_op jit(solution)/shard_map/all_to_all | solution.py:381
  60.2 0.4 collective-permute-start.1
  60.6 1.7 %collective-permute-start = (bf16[16,64,256]{2,1,0:T(8,128)(2,1)}, bf16[16,64,256]{2,1,0:T(8,128)(2,1)S(1)}, u32[]{:S(2)}, u32[]{:S(2)}) collective-permute-start(bf16[16,64,256]{2,1,0:T(8,128)(2,1)} %all-to-all-done.2.b0), channel_id=1, source_target_pairs={{0,1},{1,0},{2,3},{3,2},{4,5},{5,4},{6,7},{7,6},{8,9},{9,8},{10,11... | collective-permute-start | bytes 1572872 | tf_op jit(solution)/shard_map/ppermute | solution.py:346
  62.4 16.4 %collective-permute-done.1.b2 = bf16[16,64,256]{2,1,0:T(8,128)(2,1)S(1)} collective-permute-done((bf16[16,64,256]{2,1,0:T(8,128)(2,1)}, bf16[16,64,256]{2,1,0:T(8,128)(2,1)S(1)}, u32[]{:S(2)}, u32[]{:S(2)}) %collective-permute-start.1) | collective-permute-done | bytes 524320 | tf_op jit(solution)/shard_map/ppermute | solution.py:346
  78.8 2.0 %collective-permute-start.2 = (bf16[16,64,256]{2,1,0:T(8,128)(2,1)S(1)}, bf16[16,64,256]{2,1,0:T(8,128)(2,1)S(1)}, u32[]{:S(2)}, u32[]{:S(2)}) collective-permute-start(bf16[16,64,256]{2,1,0:T(8,128)(2,1)S(1)} %collective-permute-done.1.b2), channel_id=1, source_target_pairs={{0,1},{1,0},{2,3},{3,2},{4,5},{5,4},{6,7},{7,6},{8,9},{9,8},{10,11... | collective-permute-start | bytes 1572872 | tf_op jit(solution)/shard_map/ppermute | solution.py:346
  80.8 0.1 reshape.59
  80.9 1.0 copy.19.qid_ref
  81.9 0.1 reshape.60.kid_ref
  82.0 0.2 dynamic-slice_reduce_fusion.chain_ref
  82.2 0.0 all-to-all-done.qkv_ref
  82.2 0.8 copy-done.12
  83.0 0.0 collective-permute-done.b1
  83.0 0.8 copy-done.23
  83.8 0.0 collective-permute-done.2.b3
  83.8 0.8 copy-done.25
  84.7 1.1 copy-done.13
  85.7 1.0 copy-done.14
  86.8 1.1 copy-done.22
  87.9 1.0 copy-done.24
  88.9 1.0 copy-done.26
  90.0 11.3 %attention.1 = bf16[16,48,128]{2,1,0:T(8,128)(2,1)S(1)} custom-call(s32[1]{0:T(128)} %bitcast.4.place_ref, f32[2]{0:T(128)S(1)} %dynamic-slice_reduce_fusion.chain_ref, bf16[16,144,128]{2,1,0:T(8,128)(2,1)S(1)} %copy-done.13, bf16[16,64,256]{2,1,0:T(8,128)(2,1)} %all-to-all-done.2.b0, bf16[16,64,256]{2,1,0:T(8,128)(2,1)S(1)} %copy-done.24, ...), custom_call_target="tpu_custom_call" | custom-call | flops 402653184 | bytes 3000000 | tf_op jit(solution)/shard_map/attention/pallas_call | solution.py:258
  101.2 20.4 %all_to_all.20.o_ref = bf16[16,48,128]{2,1,0:T(8,128)(2,1)S(1)} all-to-all(bf16[16,48,128]{2,1,0:T(8,128)(2,1)S(1)} %attention.1), channel_id=1, replica_groups=mesh['row'=16,'col'=4,'grp'=4] {'row'}, dimensions={0} | all-to-all | bytes 393216 | tf_op jit(solution)/shard_map/all_to_all | solution.py:397
  121.7 2.1 %collective-permute-start.3 = (bf16[192,512]{1,0:T(8,128)(2,1)S(1)}, bf16[192,512]{1,0:T(8,128)(2,1)S(1)}, u32[]{:S(2)}, u32[]{:S(2)}) collective-permute-start(bf16[192,512]{1,0:T(8,128)(2,1)S(1)} %mix.1.m0), channel_id=1, source_target_pairs={{4,0},{8,4},{12,8},{0,12},{5,1},{9,5},{13,9},{1,13},{6,2},{10,6},{... | collective-permute-start | bytes 589832 | tf_op jit(solution)/shard_map/ppermute | solution.py:400
  123.9 0.6 collective-permute-start.4
  124.5 0.5 collective-permute-start.5
  125.0 6.4 %all-gather.2.cloned.1.call-done = bf16[768,768]{1,0:T(8,128)(2,1)} async-done(((bf16[192,768]{1,0:T(8,128)(2,1)}), bf16[768,768]{1,0:T(8,128)(2,1)}) %all-gather.2.cloned.1.call-update) | async-done | bytes 1179664 | tf_op jit(solution)/shard_map/all_gather | solution.py:385
  131.4 0.0 collective-permute-done.3.m1
  131.4 0.0 collective-permute-done.4.m2
  131.4 6.0 %collective-permute-done.5.m3 = bf16[192,512]{1,0:T(8,128)(2,1)} collective-permute-done((bf16[192,512]{1,0:T(8,128)(2,1)S(1)}, bf16[192,512]{1,0:T(8,128)(2,1)}, u32[]{:S(2)}, u32[]{:S(2)}) %collective-permute-start.5) | collective-permute-done | bytes 196640 | tf_op jit(solution)/shard_map/ppermute | solution.py:400
  137.4 1.3 copy-done.6
  138.7 1.1 copy-done.10
  139.8 3.0 %finish.1 = bf16[512,768]{1,0:T(8,128)(2,1)} custom-call(s32[1]{0:T(128)} %bitcast.col_ref, bf16[192,512]{1,0:T(8,128)(2,1)S(1)} %mix.1.m0, bf16[192,512]{1,0:T(8,128)(2,1)S(1)} %collective-permute-done.3.m1, bf16[192,512]{1,0:T(8,128)(2,1)} %collective-permute-done.4.m2, bf16[192,512]{1,0:T(8,128)(2,1)} %collective-permute-done.5.m3, ...), custom_call_target="tpu_custom_call" | custom-call | flops 603979776 | bytes 6291456 | tf_op jit(solution)/shard_map/finish/pallas_call | solution.py:323
  (38 shorter events, 0.1 us)
Async XLA Ops:
  6.5 75.4 %copy-start = (f32[2,16]{1,0:T(2,128)S(1)}, f32[2,16]{1,0:T(2,128)}, u32[]{:S(2)}) copy-start(f32[2,16]{1,0:T(2,128)} %param.21) | copy-start | bytes 388
  6.5 10.2 %copy-start.30 = (f32[384]{0:T(512)S(1)}, f32[384]{0:T(512)}, u32[]{:S(2)}) copy-start(f32[384]{0:T(512)} %param.22) | copy-start | bytes 4612
  7.4 1.2 copy-start.7
  8.6 0.7 copy-start.18
  9.3 10.2 %copy-start.5 = (bf16[2,384,768]{2,1,0:T(8,128)(2,1)S(1)}, bf16[2,384,768]{2,1,0:T(8,128)(2,1)}, u32[]{:S(2)}) copy-start(bf16[2,384,768]{2,1,0:T(8,128)(2,1)} %shift_ref.3) | copy-start | bytes 3538948
  11.7 15.0 %all-to-all-start.1 = ((bf16[4,4,32,128]{3,2,1,0:T(8,128)(2,1)}), bf16[4,4,32,128]{3,2,1,0:T(8,128)(2,1)S(1)}, u32[]{:S(2)}, u32[]{:S(2)}) async-start(bf16[4,4,32,128]{3,2,1,0:T(8,128)(2,1)} %bitcast.8), calls=%async_computation.1 | async-start | bytes 262144 | tf_op jit(solution)/shard_map/all_to_all | solution.py:377
  16.7 2.7 %copy-start.3 = (bf16[768,4,192]{0,2,1:T(8,128)(2,1)S(1)}, bf16[768,4,192]{0,2,1:T(8,128)(2,1)}, u32[]{:S(2)}) copy-start(bf16[768,4,192]{0,2,1:T(8,128)(2,1)} %param.25) | copy-start | bytes 3538948
  16.7 2.7 %copy-start.4 = (bf16[2,384,768]{2,1,0:T(8,128)(2,1)S(1)}, bf16[2,384,768]{2,1,0:T(8,128)(2,1)}, u32[]{:S(2)}) copy-start(bf16[2,384,768]{2,1,0:T(8,128)(2,1)} %scale_ref.3) | copy-start | bytes 3538948
  19.4 1.1 copy-start.8
  20.6 1.0 copy-start.17
  24.3 0.8 copy-start.11
  25.1 0.8 copy-start.15
  25.9 0.7 copy-start.27
  26.7 11.8 %copy-start.9 = (bf16[8,64,768]{2,1,0:T(8,128)(2,1)S(1)}, bf16[8,64,768]{2,1,0:T(8,128)(2,1)}, u32[]{:S(2)}) copy-start(bf16[8,64,768]{2,1,0:T(8,128)(2,1)} %param.15) | copy-start | bytes 2359300
  27.6 28.1 %all-to-all-start.2 = ((bf16[16,64,256]{2,1,0:T(8,128)(2,1)}), bf16[16,64,256]{2,1,0:T(8,128)(2,1)}, u32[]{:S(2)}, u32[]{:S(2)}) async-start(bf16[16,64,256]{2,1,0:T(8,128)(2,1)} %spread_bias.1), calls=%async_computation.2 | async-start | bytes 1048576 | tf_op jit(solution)/shard_map/all_to_all | solution.py:378
  38.4 86.6 %all-reduce.2.cloned.1.call-start = ((), (), s32[]{:S(2)}) async-start(), calls=%async_computation.5 | async-start | bytes 1572864 | tf_op jit(solution)/shard_map/psum | solution.py:389
  38.4 1.3 copy-start.19
  39.7 1.1 copy-start.20
  40.8 1.0 copy-start.28
  47.8 33.0 %copy-start.29 = (s32[1024]{0:T(1024)S(1)}, s32[1024]{0:T(1024)}, u32[]{:S(2)}) copy-start(s32[1024]{0:T(1024)} %param.19) | copy-start | bytes 12292
  47.8 83.6 %all-gather.2.cloned.1.call-start = ((), (), s32[]{:S(2)}) async-start(), calls=%async_computation.4 | async-start | bytes 1474560 | tf_op jit(solution)/shard_map/all_gather | solution.py:385
  55.7 26.5 %all-to-all-start = ((bf16[16,144,128]{2,1,0:T(8,128)(2,1)}), bf16[16,144,128]{2,1,0:T(8,128)(2,1)S(1)}, u32[]{:S(2)}, u32[]{:S(2)}) async-start(bf16[16,144,128]{2,1,0:T(8,128)(2,1)} %bitcast.20), calls=%async_computation | async-start | bytes 1179648 | tf_op jit(solution)/shard_map/all_to_all | solution.py:381
  60.2 18.6 %collective-permute-start.1 = (bf16[16,64,256]{2,1,0:T(8,128)(2,1)}, bf16[16,64,256]{2,1,0:T(8,128)(2,1)S(1)}, u32[]{:S(2)}, u32[]{:S(2)}) collective-permute-start(bf16[16,64,256]{2,1,0:T(8,128)(2,1)} %all-to-all-done.2.b0), channel_id=1, source_target_pairs={{0,2},{1,3},{2,0},{3,1},{4,6},{5,7},{6,4},{7,5},{8,10},{9,11},{10,... | collective-permute-start | bytes 1572872 | tf_op jit(solution)/shard_map/ppermute | solution.py:346
  60.6 22.4 %collective-permute-start = (bf16[16,64,256]{2,1,0:T(8,128)(2,1)}, bf16[16,64,256]{2,1,0:T(8,128)(2,1)S(1)}, u32[]{:S(2)}, u32[]{:S(2)}) collective-permute-start(bf16[16,64,256]{2,1,0:T(8,128)(2,1)} %all-to-all-done.2.b0), channel_id=1, source_target_pairs={{0,1},{1,0},{2,3},{3,2},{4,5},{5,4},{6,7},{7,6},{8,9},{9,8},{10,11... | collective-permute-start | bytes 1572872 | tf_op jit(solution)/shard_map/ppermute | solution.py:346
  78.8 5.0 %copy-start.21 = (bf16[16,64,256]{2,1,0:T(8,128)(2,1)}, bf16[16,64,256]{2,1,0:T(8,128)(2,1)S(1)}, u32[]{:S(2)}) copy-start(bf16[16,64,256]{2,1,0:T(8,128)(2,1)S(1)} %collective-permute-done.1.b2) | copy-start | bytes 1572868
  78.8 5.0 %collective-permute-start.2 = (bf16[16,64,256]{2,1,0:T(8,128)(2,1)S(1)}, bf16[16,64,256]{2,1,0:T(8,128)(2,1)S(1)}, u32[]{:S(2)}, u32[]{:S(2)}) collective-permute-start(bf16[16,64,256]{2,1,0:T(8,128)(2,1)S(1)} %collective-permute-done.1.b2), channel_id=1, source_target_pairs={{0,1},{1,0},{2,3},{3,2},{4,5},{5,4},{6,7},{7,6},{8,9},{9,8},{10,11... | collective-permute-start | bytes 1572872 | tf_op jit(solution)/shard_map/ppermute | solution.py:346
  82.2 0.8 copy-start.12
  83.0 0.8 copy-start.23
  83.8 0.8 copy-start.25
  84.7 1.1 copy-start.13
  85.7 1.0 copy-start.14
  86.8 1.1 copy-start.22
  87.9 1.0 copy-start.24
  88.9 1.0 copy-start.26
  89.9 31.7 %copy-start.16 = (f32[192,512]{1,0:T(8,128)S(1)}, f32[192,512]{1,0:T(8,128)}, u32[]{:S(2)}) copy-start(f32[192,512]{1,0:T(8,128)} %copy-done.15) | copy-start | bytes 1179652
  90.0 47.4 %copy-start.1 = (f32[512,768]{1,0:T(8,128)S(1)}, f32[512,768]{1,0:T(8,128)}, u32[]{:S(2)}) copy-start(f32[512,768]{1,0:T(8,128)} %get-tuple-element.14.g0_ref) | copy-start | bytes 4718596
  90.0 47.4 %copy-start.2 = (f32[512,768]{1,0:T(8,128)S(1)}, f32[512,768]{1,0:T(8,128)}, u32[]{:S(2)}) copy-start(f32[512,768]{1,0:T(8,128)} %get-tuple-element.15.g1_ref) | copy-start | bytes 4718596
  121.7 9.7 %collective-permute-start.3 = (bf16[192,512]{1,0:T(8,128)(2,1)S(1)}, bf16[192,512]{1,0:T(8,128)(2,1)S(1)}, u32[]{:S(2)}, u32[]{:S(2)}) collective-permute-start(bf16[192,512]{1,0:T(8,128)(2,1)S(1)} %mix.1.m0), channel_id=1, source_target_pairs={{4,0},{8,4},{12,8},{0,12},{5,1},{9,5},{13,9},{1,13},{6,2},{10,6},{... | collective-permute-start | bytes 589832 | tf_op jit(solution)/shard_map/ppermute | solution.py:400
  123.9 7.5 %collective-permute-start.4 = (bf16[192,512]{1,0:T(8,128)(2,1)S(1)}, bf16[192,512]{1,0:T(8,128)(2,1)}, u32[]{:S(2)}, u32[]{:S(2)}) collective-permute-start(bf16[192,512]{1,0:T(8,128)(2,1)S(1)} %mix.1.m0), channel_id=1, source_target_pairs={{8,0},{12,4},{0,8},{4,12},{9,1},{13,5},{1,9},{5,13},{10,2},{14,6},... | collective-permute-start | bytes 589832 | tf_op jit(solution)/shard_map/ppermute | solution.py:400
  124.5 12.9 %collective-permute-start.5 = (bf16[192,512]{1,0:T(8,128)(2,1)S(1)}, bf16[192,512]{1,0:T(8,128)(2,1)}, u32[]{:S(2)}, u32[]{:S(2)}) collective-permute-start(bf16[192,512]{1,0:T(8,128)(2,1)S(1)} %mix.1.m0), channel_id=1, source_target_pairs={{12,0},{0,4},{4,8},{8,12},{13,1},{1,5},{5,9},{9,13},{14,2},{2,6},{... | collective-permute-start | bytes 589832 | tf_op jit(solution)/shard_map/ppermute | solution.py:400
  137.4 1.3 copy-start.6
  138.6 1.1 copy-start.10
Sparse Core Ops, SparseCore 0:
  47.9 50.1 all-reduce.1
  99.9 31.4 all-gather.1

commit v2 on v1

v2 whole, which is shorter than its diff:
```python
import jax
import jax.numpy as jnp
from jax import lax
from jax.experimental import pallas as pl
from jax.experimental.pallas import tpu as pltpu
from jax.sharding import PartitionSpec as P

HD = 48
BF = jnp.bfloat16
F32 = jnp.float32
NT = (((1,), (1,)), ((), ()))
TN = (((0,), (0,)), ((), ()))


def dot(left, right, dims=(((1,), (0,)), ((), ()))):
    return lax.dot_general(left, right, dims, preferred_element_type=F32)


def norm_last(values_in):
    center = values_in - jnp.mean(values_in, axis=-1, keepdims=True)
    spread = jnp.mean(center * center, axis=-1, keepdims=True)
    return center * lax.rsqrt(spread + 1e-05)


def params(mib=60):
    return pltpu.CompilerParams(vmem_limit_bytes=mib * 1024 * 1024)


def cost(flops, moved, exps=0):
    return pl.CostEstimate(flops=flops, bytes_accessed=moved, transcendentals=exps)


def whole(shape):
    zeros = (0,) * len(shape)
    return pl.BlockSpec(shape, lambda *_: zeros)


def tile_bias_kernel(pair_ref, gain_ref, proj_ref, o0, o1, o2, o3):
    half, pairs, keys, width = pair_ref.shape
    cols, heads, _ = proj_ref.shape
    mine = lax.axis_index("col")
    rows = jnp.swapaxes(pair_ref[...].astype(F32), 0, 1).reshape(half * pairs * keys, width)
    normed = (norm_last(rows) * gain_ref[...]).astype(BF)
    turned = jnp.concatenate(
        [proj_ref[lax.rem(mine + k, cols)].astype(F32) for k in range(cols)], axis=0
    ).astype(BF)
    found = dot(turned, normed, NT)
    lanes = half * keys
    slabs = [found[:, p * lanes : (p + 1) * lanes][:, None, :] for p in range(pairs)]
    tiles = jnp.concatenate(slabs, axis=1).astype(BF)
    for k, ref in enumerate((o0, o1, o2, o3)):
        ref[...] = tiles[k * heads : (k + 1) * heads]


def tile_bias(pair, gain, proj):
    queries, keys, width = pair.shape
    cols, heads, _ = proj.shape
    split = pair.reshape(2, queries // 2, keys, width)
    step = 16
    return pl.pallas_call(
        tile_bias_kernel,
        grid=(queries // 2 // step,),
        in_specs=[
            pl.BlockSpec((2, step, keys, width), lambda i: (0, i, 0, 0)),
            whole((1, width)),
            whole(proj.shape),
        ],
        out_specs=[pl.BlockSpec((heads, step, 2 * keys), lambda i: (0, i, 0))] * cols,
        out_shape=[jax.ShapeDtypeStruct((heads, queries // 2, 2 * keys), BF)] * cols,
        compiler_params=params(),
        cost_estimate=cost(0, 500_000),
        name="tile_bias",
    )(split, gain.reshape(1, width), proj)


def spread_bias_kernel(t0, t1, t2, t3, out_ref):
    heads, pairs, lanes = t0.shape
    keys = lanes // 2
    copies = out_ref.shape[0] // heads
    for head in range(heads):
        parts = [t[head] for t in (t0, t1, t2, t3)]
        low = jnp.concatenate([p[:, :keys] for p in parts], axis=1)
        high = jnp.concatenate([p[:, keys:] for p in parts], axis=1)
        for copy in range(copies):
            out_ref[head * copies + copy, :pairs] = low
            out_ref[head * copies + copy, pairs:] = high


def spread_bias(tiles, dests):
    heads, pairs, lanes = tiles[0].shape
    shape = (dests, 2 * pairs, 2 * lanes)
    return pl.pallas_call(
        spread_bias_kernel,
        in_specs=[whole(t.shape) for t in tiles],
        out_specs=whole(shape),
        grid=(1,),
        out_shape=jax.ShapeDtypeStruct(shape, BF),
        compiler_params=params(),
        cost_estimate=cost(0, 500_000),
        name="spread_bias",
    )(*tiles)


def project_kernel(act_ref, cond_ref, gain_ref, scale_ref, shift_ref, w_ref, qkv_ref, gate_ref, cn_ref):
    heads, pairs, _, lanes = qkv_ref.shape
    gain = jnp.concatenate([gain_ref[i : i + 1] for i in range(gain_ref.shape[0])], axis=1)
    cond_norm = (norm_last(cond_ref[...].astype(F32)) * gain).astype(BF)
    cn_ref[...] = cond_norm
    act_norm = norm_last(act_ref[...].astype(F32))
    att = (
        jax.nn.sigmoid(dot(cond_norm, scale_ref[0])) * act_norm + dot(cond_norm, shift_ref[0])
    ).astype(BF)
    part = heads * HD
    for which in range(3):
        result = dot(w_ref[which], att, NT).astype(BF)
        for head in range(heads):
            for p in range(pairs):
                qkv_ref[head, p, which * HD : (which + 1) * HD, :] = result[
                    head * HD : (head + 1) * HD, p * lanes : (p + 1) * lanes
                ]
    gate_ref[...] = jax.nn.sigmoid(dot(w_ref[3], att, NT))


def project(act, cond, gain, scale, shift, w):
    rows, width = act.shape
    cwidth = cond.shape[1]
    part = w.shape[1]
    heads = part // HD
    step = 256
    lanes = step
    pairs = rows // lanes
    return pl.pallas_call(
        project_kernel,
        grid=(rows // step,),
        in_specs=[
            pl.BlockSpec((step, width), lambda i: (i, 0)),
            pl.BlockSpec((step, cwidth), lambda i: (i, 0)),
            whole((cwidth // 128, 128)),
            whole((1, cwidth, width)),
            whole((1, cwidth, width)),
            whole(w.shape),
        ],
        out_specs=[
            pl.BlockSpec((heads, 1, 3 * HD, lanes), lambda i: (0, i, 0, 0)),
            pl.BlockSpec((part, step), lambda i: (0, i)),
            pl.BlockSpec((step, cwidth), lambda i: (i, 0)),
        ],
        out_shape=[
            jax.ShapeDtypeStruct((heads, pairs, 3 * HD, lanes), BF),
            jax.ShapeDtypeStruct((part, rows), F32),
            jax.ShapeDtypeStruct((rows, cwidth), BF),
        ],
        compiler_params=params(),
        cost_estimate=cost(
            2 * rows * width * (2 * cwidth + 4 * part), 4 * cwidth * width + 8 * width * part
        ),
        name="project",
    )(act, cond, gain.reshape(cwidth // 128, 128), scale, shift, w)


def transition_kernel(
    act_ref, cn_ref, scale_ref, shift_ref, og_ref, win_ref, wout_ref, last_ref,
    p0, p1, p2, p3, g0_ref, g1_ref, part_ref,
):
    mine = lax.axis_index("col")
    cond_norm = cn_ref[...]
    act_norm = norm_last(act_ref[...].astype(F32))
    tin = (
        jax.nn.sigmoid(dot(cond_norm, scale_ref[0])) * act_norm + dot(cond_norm, shift_ref[0])
    ).astype(BF)
    inner = dot(tin, win_ref[...])
    units = wout_ref.shape[0]
    first = inner[:, :units]
    hidden = (first * jax.nn.sigmoid(first) * inner[:, units:]).astype(BF)
    part_ref[...] = dot(hidden, wout_ref[...]).astype(BF)
    quarter = p0.shape[0]
    for shift, ref in enumerate((p0, p1, p2, p3)):
        start = pl.multiple_of(lax.rem(mine + shift, 4) * quarter, quarter)
        ref[:quarter] = part_ref[pl.ds(start, quarter), :]
        if shift:
            ref[quarter:] = last_ref[...]
    g0_ref[...] = jax.nn.sigmoid(dot(cond_norm, og_ref[0]))
    own = cn_ref[pl.ds(pl.multiple_of(mine * quarter, quarter), quarter), :]
    g1_ref[...] = jax.nn.sigmoid(dot(own, og_ref[1]))


def transition(act, cond_norm, scale, shift, out_gate, w_in, w_out, last):
    rows, width = act.shape
    cwidth = cond_norm.shape[1]
    quarter = rows // 4
    second = pl.BlockSpec((1, cwidth, width), lambda i: (1, 0, 0))
    both = (quarter + last.shape[0], width)
    return pl.pallas_call(
        transition_kernel,
        grid=(1,),
        in_specs=[
            whole(act.shape),
            whole(cond_norm.shape),
            second,
            second,
            whole(out_gate.shape),
            whole(w_in.shape),
            whole(w_out.shape),
            whole(last.shape),
        ],
        out_specs=[whole((quarter, width))]
        + [whole(both)] * 3
        + [whole((rows, width)), whole((quarter, width))],
        out_shape=[jax.ShapeDtypeStruct((quarter, width), BF)]
        + [jax.ShapeDtypeStruct(both, BF)] * 3
        + [
            jax.ShapeDtypeStruct((rows, width), F32),
            jax.ShapeDtypeStruct((quarter, width), F32),
        ],
        scratch_shapes=[pltpu.VMEM((rows, width), BF)],
        compiler_params=params(),
        cost_estimate=cost(0, 2_000_000),
        name="transition",
    )(act, cond_norm, scale, shift, out_gate, w_in, w_out, last)


def gated_sum_kernel(a, b, c, d, gate_ref, out_ref):
    rows = slice(0, a.shape[0])
    total = (a[...].astype(F32) + b[rows].astype(F32)) + (c[rows].astype(F32) + d[rows].astype(F32))
    out_ref[...] = (total * gate_ref[...]).astype(BF)


def gated_sum(parts, gate):
    shape = gate.shape
    return pl.pallas_call(
        gated_sum_kernel,
        grid=(1,),
        in_specs=[whole(shape)] * 5,
        out_specs=whole(shape),
        out_shape=jax.ShapeDtypeStruct(shape, BF),
        compiler_params=params(),
        cost_estimate=cost(4 * gate.size, gate.size * 14),
        name="gated_sum",
    )(*parts, gate)


def attention_kernel(
    chain_ref, own_ref, far_ref, b0, b1, b2, b3, id_ref, out_ref, k_ref, v_ref, kid_ref, turn_ref, qid_ref
):
    samples, pieces, _, span = k_ref.shape
    half = own_ref.shape[2] // samples
    cols = span // half
    blocks = b0.shape[0]
    z, xh, col = (lax.axis_index(name) for name in ("z", "xh", "col"))
    grp = 2 * lax.axis_index("xlo") + lax.axis_index("core")

    @pl.when(pl.program_id(0) == 0)
    def _():
        for piece in range(pieces):
            g = grp ^ piece
            near = (g & 1) == xh
            keys, values, ids = [], [], []
            for k in range(cols):
                token = 4 * lax.rem(col + cols - k, cols) + g
                at = token >> 1
                keys.append(jnp.where(near, own_ref[at, HD : 2 * HD], far_ref[at, :HD]))
                values.append(jnp.where(near, own_ref[at, 2 * HD :], far_ref[at, HD:]))
                line = id_ref[pl.ds(at, 1), :]
                ids.append(jnp.where((g & 1) == 0, line[:, :half], line[:, half:]))
            kid_ref[piece] = jnp.concatenate(ids, axis=1)
            for s in range(samples):
                lanes = slice(s * half, (s + 1) * half)
                k_ref[s, piece] = jnp.concatenate([x[:, lanes] for x in keys], axis=1)
                v_ref[s, piece] = jnp.concatenate([x[:, lanes] for x in values], axis=1)
        turn_ref[...] = jnp.transpose(id_ref[...])
        for at in range(id_ref.shape[0]):
            qid_ref[at] = turn_ref[pl.ds(pl.multiple_of(xh * half, half), half), at : at + 1]

    step = pl.program_id(0)
    head = col * 4 + z // 2
    other, same = chain_ref[0, head], chain_ref[1, head]
    qid = qid_ref[pl.ds(step * blocks, blocks)].reshape(blocks * half, 1)
    totals = []
    for piece, ref in enumerate((b0, b1, b2, b3)):
        bias = ref[...].reshape(blocks * half, span).astype(F32)
        totals.append(bias + jnp.where(qid == kid_ref[piece], same, other))
    scale = HD ** (-0.5)
    results = []
    queries = [own_ref[step * blocks + b, :HD] for b in range(blocks)]
    for s in range(samples):
        lanes = slice(s * half, (s + 1) * half)
        query = jnp.concatenate([q[:, lanes] for q in queries], axis=1)
        scores = [
            lax.dot_general(query, k_ref[s, p], TN, preferred_element_type=F32) * scale + totals[p]
            for p in range(pieces)
        ]
        top = jnp.max(
            jnp.maximum(jnp.maximum(scores[0], scores[1]), jnp.maximum(scores[2], scores[3])),
            axis=1,
            keepdims=True,
        )
        weights = [jnp.exp(x - top) for x in scores]
        total = jnp.sum(
            (weights[0] + weights[1]) + (weights[2] + weights[3]), axis=1, keepdims=True
        )
        summed = sum(dot(weights[p].astype(BF), v_ref[s, p], NT) for p in range(pieces))
        results.append(jnp.transpose(summed / total).astype(BF))
    for b in range(blocks):
        out_ref[b] = jnp.concatenate([r[:, b * half : (b + 1) * half] for r in results], axis=1)


def attention(chain_bias, own, far, biases, ids):
    count, rows, lanes = own.shape
    half = 64
    samples = lanes // half
    span = biases[0].shape[2]
    blocks = 2
    bias_spec = pl.BlockSpec((blocks, half, span), lambda i: (i, 0, 0))
    tokens = 2 * count * half
    return pl.pallas_call(
        attention_kernel,
        grid=(count // blocks,),
        in_specs=[
            pl.BlockSpec(memory_space=pltpu.SMEM),
            whole(own.shape),
            whole(far.shape),
            bias_spec,
            bias_spec,
            bias_spec,
            bias_spec,
            whole(ids.shape),
        ],
        out_specs=pl.BlockSpec((blocks, HD, lanes), lambda i: (i, 0, 0)),
        out_shape=jax.ShapeDtypeStruct((count, HD, lanes), BF),
        scratch_shapes=[
            pltpu.VMEM((samples, 4, HD, span), BF),
            pltpu.VMEM((samples, 4, HD, span), BF),
            pltpu.VMEM((4, 1, span), jnp.int32),
            pltpu.VMEM((ids.shape[1], ids.shape[0]), jnp.int32),
            pltpu.VMEM((count, half, 1), jnp.int32),
        ],
        compiler_params=params(),
        cost_estimate=cost(8 * tokens * tokens * HD, 20_000_000, 2 * tokens * tokens),
        name="attention",
    )(chain_bias, own, far, *biases, ids)


def mix_kernel(gate_ref, o_ref, out_ref):
    dests, _, lanes = o_ref.shape
    pairs = out_ref.shape[1] // lanes
    for r in range(dests):
        rows = slice(r // pairs * HD, (r // pairs + 1) * HD)
        cols = slice(r % pairs * lanes, (r % pairs + 1) * lanes)
        out_ref[rows, cols] = (gate_ref[rows, cols] * o_ref[r].astype(F32)).astype(BF)


def mix(gates, attended):
    return pl.pallas_call(
        mix_kernel,
        grid=(1,),
        in_specs=[whole(gates.shape), whole(attended.shape)],
        out_specs=whole(gates.shape),
        out_shape=jax.ShapeDtypeStruct(gates.shape, BF),
        compiler_params=params(),
        cost_estimate=cost(gates.size, gates.size * 8),
        name="mix",
    )(gates, attended)


def finish_kernel(m0, m1, m2, m3, w0, w1, w2, w3, g0_ref, t0, t1, t2, t3, out_ref, total_ref):
    mine = lax.axis_index("col")
    total = None
    depth = m0.shape[0]
    for ref, w in zip((m0, m1, m2, m3), (w0, w1, w2, w3)):
        term = lax.dot_general(ref[...], w[-depth:], TN, preferred_element_type=F32)
        total = term if total is None else total + term
    total_ref[...] = g0_ref[...] * total
    quarter = t0.shape[0]
    for shift, ref in enumerate((t0, t1, t2, t3)):
        rows = pl.ds(pl.multiple_of(((mine + shift) % 4) * quarter, quarter), quarter)
        out_ref[rows, :] = (total_ref[rows, :] + ref[...].astype(F32)).astype(BF)


def finish(mixed, w, g0, trans):
    rows, width = g0.shape
    return pl.pallas_call(
        finish_kernel,
        grid=(1,),
        in_specs=[whole(x.shape) for x in (*mixed, *w, g0, *trans)],
        out_specs=whole((rows, width)),
        out_shape=jax.ShapeDtypeStruct((rows, width), BF),
        scratch_shapes=[pltpu.VMEM((rows, width), F32)],
        compiler_params=params(),
        cost_estimate=cost(2 * rows * width * width, rows * width * 12),
        name="finish",
    )(*mixed, *w, g0, *trans)


def around(x):
    return [x] + [
        lax.ppermute(x, "col", [((i + k) % 4, i) for i in range(4)]) for k in (1, 3, 2)
    ]


def in_order(pieces):
    return [pieces[0], pieces[1], pieces[3], pieces[2]]


def swap(x, axis):
    return lax.ppermute(x, axis, [(0, 1), (1, 0)])


def send(x, k):
    return lax.ppermute(x, "col", [(i, (i + k) % 4) for i in range(4)])


def around(x):
    return [x, send(x, 3), send(x, 2), send(x, 1)]


def scatter(parts):
    return [parts[0], send(parts[1], 1), send(parts[2], 2), send(parts[3], 3)]


def tie(first, *later):
    return lax.optimization_barrier((first, *later))


def body(
    act,
    cond,
    pair,
    pair_gain,
    chain_ids,
    bias_proj,
    chain_bias,
    cond_gain,
    ada_scale,
    ada_shift,
    qkvg,
    attn_out,
    out_gate,
    trans_in,
    trans_out,
):
    samples, rows, width = act.shape
    flat = samples * rows
    part = qkvg.shape[2]
    heads = part // HD
    act = act.reshape(flat, width)
    cond = cond.reshape(flat, cond.shape[2])
    w_proj = jnp.transpose(qkvg, (1, 2, 0))
    qkv, gates, cond_norm = project(act, cond, cond_gain, ada_scale, ada_shift, w_proj)
    qkv, pair = tie(qkv, pair)
    own = lax.all_to_all(qkv.reshape(8, 3 * HD, 4 * rows), "z", 0, 0, tiled=True)
    proj = jnp.transpose(bias_proj).reshape(4, heads, -1)
    tiles = tile_bias(pair, pair_gain, proj)
    *tiles, act = tie(*tiles, act)
    *parts, g0, g1 = transition(
        act,
        cond_norm,
        ada_scale,
        ada_shift,
        out_gate,
        trans_in.reshape(width, -1),
        trans_out,
        attn_out,
    )
    parts = scatter(parts)
    spread = spread_bias(scatter(tiles), 8)
    own, spread, g0 = tie(own, spread, g0)
    bias0 = lax.all_to_all(spread, "z", 0, 0, tiled=True)
    far = swap(own[:, HD:], "xh")
    bias2 = swap(bias0, "xlo")
    bias1 = swap(bias0, "core")
    bias3 = swap(bias2, "core")
    quarter = gated_sum(parts, g1)
    trans = around(quarter)
    attended = attention(
        chain_bias, own, far, (bias0, bias1, bias2, bias3), chain_ids.reshape(8, 2 * rows)
    )
    attended = lax.all_to_all(attended, "z", 0, 0, tiled=True)
    w_out_all = [attn_out, parts[3], parts[2], parts[1]]
    updated = finish(around(mix(gates, attended)), w_out_all, g0, trans)
    return updated.reshape(samples, rows, width)


def solution(mesh):
    fine = jax.sharding.Mesh(
        mesh.devices.reshape(8, 2, 4, 2, 2), ("z", "xh", "col", "xlo", "core")
    )
    rows, groups = ("z", "xh"), ("xlo", "core")
    in_specs = (
        P(groups, rows, None),
        P(groups, rows, None),
        P(rows, ("col", *groups), None),
        P(),
        P(),
        P(),
        P(),
        P(),
        P(),
        P(),
        P(None, None, "col"),
        P("col", None),
        P(),
        P(None, None, "col"),
        P("col", None),
    )
    out_specs = P(groups, rows, None)
    return jax.shard_map(body, mesh=fine, in_specs=in_specs, out_specs=out_specs, check_vma=False)
```

time: 151 us -> 107 us (0.71)
  blocking collectives: 20.4 us -> 0 us
  local copies, waits for them, and re-layouts: 24.8 us -> 5.65 us
  starting transfers between devices: 27.8 us -> 44.1 us
  waiting for transfers between devices: 36.7 us -> 20.5 us
  between operations: 13.5 us -> 0.18 us
  Pallas kernels: 26.4 us -> 35.3 us
    all_to_all x1 -> x0, blocking collectives: 20.4 us -> none  [body(): attended = lax.all_to_all(attended, 'row', 0, 0, tiled=True)]
    unnamed x64 -> x41, local copies, waits for them, and re-layouts: 23.4 us -> 5.62 us
    ppermute x6 -> x16, starting transfers between devices: 7.39 us -> 22 us  [the longest x12 11.6 us: send(): return lax.ppermute(x, 'col', [(i, (i + k) % 4) for i in range(4)])]
    ppermute x6 -> x16, waiting for transfers between devices: 22.4 us -> 10 us  [the longest x12 8.83 us: send(): return lax.ppermute(x, 'col', [(i, (i + k) % 4) for i in range(4)])]
    all_gather x1 -> x0, waiting for transfers between devices: 6.42 us -> none  [body(): w_out_full = lax.all_gather(attn_out, 'col', axis=0, tiled=True)]
    pallas_call x4 -> x5, Pallas kernels: 21.2 us -> 24.8 us  [the longest x1 9.21 us: attention(): pl.pallas_call(attention_kernel, grid=(count // blocks,), in_specs=[pl.Bl...]
    all_to_all x3, waiting for transfers between devices: 7.16 us -> 10.5 us  [the longest x1 6.58 us: body(): bias0 = lax.all_to_all(spread, 'z', 0, 0, tiled=True)]
    pallas_call x1, Pallas kernels: 2.74 us -> 5.45 us  [project(): pl.pallas_call(project_kernel, grid=(rows // step,), in_specs=[pl.BlockSp...]
  transfers between devices with their start and end apart: 11 -> 19, of which waited for: 4 -> 7; matrix products, arithmetic and copies ran while one was open for 3% -> 1% of each run, Pallas kernels for 13% -> 24%
where the time goes in v2:
time: 107 us; the launch traced here: 106 us
  starting transfers between devices  44.1 us (41%)
  Pallas kernels  35.3 us (33%)
  waiting for transfers between devices  20.5 us (19%)
  local copies, waits for them, and re-layouts  5.65 us (5%)
    ppermute x12, starting transfers between devices, send(): return lax.ppermute(x, 'col', [(i, (i + k) % 4) for i in range(4)])  11.6 us
    ppermute x4, starting transfers between devices, swap(): return lax.ppermute(x, axis, [(0, 1), (1, 0)])  10.4 us
    pallas_call x1, Pallas kernels, attention(): pl.pallas_call(attention_kernel, grid=(count // blocks,), in_specs=[pl.Bl...  9.21 us
    all_to_all x1, starting transfers between devices, body(): lax.all_to_all(qkv.reshape(8, 3 * HD, 4 * rows), 'z', 0, 0, tiled=True)  9.14 us
    ppermute x12, waiting for transfers between devices, send(): return lax.ppermute(x, 'col', [(i, (i + k) % 4) for i in range(4)])  8.83 us
    pallas_call x1, Pallas kernels, transition(): pl.pallas_call(transition_kernel, grid=(1,), in_specs=[whole(act.shape),...  7.25 us
    all_to_all x1, starting transfers between devices, body(): bias0 = lax.all_to_all(spread, 'z', 0, 0, tiled=True)  6.65 us
    all_to_all x1, waiting for transfers between devices, body(): bias0 = lax.all_to_all(spread, 'z', 0, 0, tiled=True)  6.58 us
  transfers between devices with their start and end apart: 19, of which 7 were waited for; matrix products, arithmetic and copies ran while one was open for 1% of the time, Pallas kernels for 24%

profile of v2, /device:TPU:1, one launch (start us, length us, event | category | flops | bytes accessed | tf_op | source)
XLA Modules:
  0.0 105.7 jit_solution(10597112774687353747)
XLA Ops:
  0.0 5.4 %project.1 = (bf16[4,2,144,256]{3,2,1,0:T(8,128)(2,1)}, f32[192,512]{1,0:T(8,128)}, bf16[512,384]{1,0:T(8,128)(2,1)}) custom-call(bf16[512,768]{1,0:T(8,128)(2,1)} %bitcast.15, bf16[512,384]{1,0:T(8,128)(2,1)} %bitcast.21, f32[3,128]{1,0:T(4,128)} %bitcast.23, bf16[2,384,768]{2,1,0:T(8,128)(2,1)} %scale_ref.3, bf16[2,384,768]{2,1,0:T(8,128)(2,1)} %shift_ref.3, ...), custom_call_target="tpu_custom_call" | custom-call | flops 1207959552 | bytes 2359296 | tf_op jit(solution)/shard_map/project/pallas_call | solution.py:132
  5.4 9.1 %all-to-all-start = ((bf16[8,144,256]{2,1,0:T(8,128)(2,1)}), bf16[8,144,256]{2,1,0:T(8,128)(2,1)S(1)}, u32[]{:S(2)}, u32[]{:S(2)}) async-start(bf16[8,144,256]{2,1,0:T(8,128)(2,1)} %bitcast.20), calls=%async_computation | async-start | bytes 1179648 | tf_op jit(solution)/shard_map/all_to_all | solution.py:450
  14.6 3.3 %tile_bias.1 = (bf16[4,32,128]{2,1,0:T(8,128)(2,1)}, bf16[4,32,128]{2,1,0:T(8,128)(2,1)}, bf16[4,32,128]{2,1,0:T(8,128)(2,1)}, bf16[4,32,128]{2,1,0:T(8,128)(2,1)}) custom-call(bf16[2,32,64,128]{3,2,1,0:T(8,128)(2,1)} %bitcast.19, f32[1,128]{1,0:T(1,128)} %bitcast.24, bf16[4,4,128]{2,1,0:T(4,128)(2,1)} %bitcast.22), custom_call_target="tpu_custom_call" | custom-call | bytes 500000 | tf_op jit(solution)/shard_map/tile_bias/pallas_call | solution.py:60
  17.9 1.3 %collective-permute-start = (bf16[4,32,128]{2,1,0:T(8,128)(2,1)}, bf16[4,32,128]{2,1,0:T(8,128)(2,1)S(1)}, u32[]{:S(2)}, u32[]{:S(2)}) collective-permute-start(bf16[4,32,128]{2,1,0:T(8,128)(2,1)} %get-tuple-element.37), channel_id=1, source_target_pairs={{0,4},{4,8},{8,12},{12,0},{1,5},{5,9},{9,13},{13,1},{2,6},{6,10},{... | collective-permute-start | bytes 98312 | tf_op jit(solution)/shard_map/ppermute | solution.py:409
  19.2 2.6 %collective-permute-start.1 = (bf16[4,32,128]{2,1,0:T(8,128)(2,1)}, bf16[4,32,128]{2,1,0:T(8,128)(2,1)S(1)}, u32[]{:S(2)}, u32[]{:S(2)}) collective-permute-start(bf16[4,32,128]{2,1,0:T(8,128)(2,1)} %get-tuple-element.38), channel_id=1, source_target_pairs={{0,8},{4,12},{8,0},{12,4},{1,9},{5,13},{9,1},{13,5},{2,10},{6,14},... | collective-permute-start | bytes 98312 | tf_op jit(solution)/shard_map/ppermute | solution.py:409
  21.9 1.1 %collective-permute-start.2 = (bf16[4,32,128]{2,1,0:T(8,128)(2,1)}, bf16[4,32,128]{2,1,0:T(8,128)(2,1)S(1)}, u32[]{:S(2)}, u32[]{:S(2)}) collective-permute-start(bf16[4,32,128]{2,1,0:T(8,128)(2,1)} %get-tuple-element.39), channel_id=1, source_target_pairs={{0,12},{4,0},{8,4},{12,8},{1,13},{5,1},{9,5},{13,9},{2,14},{6,2},{... | collective-permute-start | bytes 98312 | tf_op jit(solution)/shard_map/ppermute | solution.py:409
  22.9 0.0 copy-done.4
  22.9 1.3 %copy.16 = bf16[96,8,2,384]{3,1,2,0:T(8,128)(2,1)} copy(bf16[96,8,2,384]{3,2,1,0:T(2,128)(2,1)S(1)} %bitcast.17) | data formatting | bytes 2359296
  24.2 7.2 %transition.1 = (bf16[128,768]{1,0:T(8,128)(2,1)}, bf16[320,768]{1,0:T(8,128)(2,1)}, bf16[320,768]{1,0:T(8,128)(2,1)}, bf16[320,768]{1,0:T(8,128)(2,1)}, f32[512,768]{1,0:T(8,128)}, /*index=5*/f32[128,768]{1,0:T(8,128)}) custom-call(bf16[512,768]{1,0:T(8,128)(2,1)} %bitcast.16, bf16[512,384]{1,0:T(8,128)(2,1)} %get-tuple-element.41.cn_ref, ...), custom_call_target="tpu_custom_call" | custom-call | bytes 2000000 | tf_op jit(solution)/shard_map/transition/pallas_call | solution.py:193
  31.4 0.0 collective-permute-done.t1
  31.4 0.0 copy-start.13
  31.5 0.0 collective-permute-done.1.t2
  31.5 0.0 copy-start.14
  31.5 0.0 collective-permute-done.2.t3
  31.5 0.6 copy-done.13
  32.1 0.0 copy-done.14
  32.1 0.6 copy-done.15
  32.7 1.6 %spread_bias.1 = bf16[8,64,256]{2,1,0:T(8,128)(2,1)} custom-call(bf16[4,32,128]{2,1,0:T(8,128)(2,1)} %get-tuple-element.36.t0, bf16[4,32,128]{2,1,0:T(8,128)(2,1)} %copy-done.13, bf16[4,32,128]{2,1,0:T(8,128)(2,1)} %copy-done.14, bf16[4,32,128]{2,1,0:T(8,128)(2,1)} %copy-done.15), custom_call_target="tpu_custom_call" | custom-call | bytes 500000 | tf_op jit(solution)/shard_map/spread_bias/pallas_call | solution.py:92
  34.3 0.0 all-to-all-done.own_ref
  34.3 6.7 %all-to-all-start.1 = ((bf16[8,64,256]{2,1,0:T(8,128)(2,1)}), bf16[8,64,256]{2,1,0:T(8,128)(2,1)S(1)}, u32[]{:S(2)}, u32[]{:S(2)}) async-start(bf16[8,64,256]{2,1,0:T(8,128)(2,1)} %spread_bias.1), calls=%async_computation.1 | async-start | bytes 524288 | tf_op jit(solution)/shard_map/all_to_all | solution.py:467
  41.0 2.8 %collective-permute-start.3 = (bf16[8,96,256]{2,1,0:T(8,128)(2,1)S(1)}, bf16[8,96,256]{2,1,0:T(8,128)(2,1)}, u32[]{:S(2)}, u32[]{:S(2)}) collective-permute-start(bf16[8,96,256]{2,1,0:T(8,128)(2,1)S(1)} %slice.3), channel_id=1, source_target_pairs={{0,16},{16,0},{1,17},{17,1},{2,18},{18,2},{3,19},{19,3},{4,20},{20... | collective-permute-start | bytes 1179656 | tf_op jit(solution)/shard_map/ppermute | solution.py:405
  43.8 6.6 %all-to-all-done.1.b0 = bf16[8,64,256]{2,1,0:T(8,128)(2,1)S(1)} async-done(((bf16[8,64,256]{2,1,0:T(8,128)(2,1)}), bf16[8,64,256]{2,1,0:T(8,128)(2,1)S(1)}, u32[]{:S(2)}, u32[]{:S(2)}) %all-to-all-start.1) | async-done | bytes 262176 | tf_op jit(solution)/shard_map/all_to_all | solution.py:467
  50.4 1.2 %collective-permute-start.5 = (bf16[8,64,256]{2,1,0:T(8,128)(2,1)S(1)}, bf16[8,64,256]{2,1,0:T(8,128)(2,1)S(1)}, u32[]{:S(2)}, u32[]{:S(2)}) collective-permute-start(bf16[8,64,256]{2,1,0:T(8,128)(2,1)S(1)} %all-to-all-done.1.b0), channel_id=1, source_target_pairs={{0,2},{2,0},{1,3},{3,1},{4,6},{6,4},{5,7},{7,5},{8,10},{10,8},{9,1... | collective-permute-start | bytes 786440 | tf_op jit(solution)/shard_map/ppermute | solution.py:405
  51.6 0.0 collective-permute-start.10
  51.6 2.2 %collective-permute-start.11 = (bf16[320,768]{1,0:T(8,128)(2,1)}, bf16[320,768]{1,0:T(8,128)(2,1)S(1)}, u32[]{:S(2)}, u32[]{:S(2)}) collective-permute-start(bf16[320,768]{1,0:T(8,128)(2,1)} %get-tuple-element.46), channel_id=1, source_target_pairs={{0,8},{4,12},{8,0},{12,4},{1,9},{5,13},{9,1},{13,5},{2,10},{6,14},... | collective-permute-start | bytes 1474568 | tf_op jit(solution)/shard_map/ppermute | solution.py:409
  53.8 0.0 copy-done.16
  53.8 0.0 collective-permute-start.12
  53.8 0.0 collective-permute-done.3.far_ref
  53.8 4.3 %collective-permute-start.4 = (bf16[8,64,256]{2,1,0:T(8,128)(2,1)S(1)}, bf16[8,64,256]{2,1,0:T(8,128)(2,1)S(1)}, u32[]{:S(2)}, u32[]{:S(2)}) collective-permute-start(bf16[8,64,256]{2,1,0:T(8,128)(2,1)S(1)} %all-to-all-done.1.b0), channel_id=1, source_target_pairs={{0,1},{1,0},{2,3},{3,2},{4,5},{5,4},{6,7},{7,6},{8,9},{9,8},{10,11... | collective-permute-start | bytes 786440 | tf_op jit(solution)/shard_map/ppermute | solution.py:405
  58.1 0.0 collective-permute-done.5.b2
  58.1 2.0 %collective-permute-start.6 = (bf16[8,64,256]{2,1,0:T(8,128)(2,1)S(1)}, bf16[8,64,256]{2,1,0:T(8,128)(2,1)S(1)}, u32[]{:S(2)}, u32[]{:S(2)}) collective-permute-start(bf16[8,64,256]{2,1,0:T(8,128)(2,1)S(1)} %collective-permute-done.5.b2), channel_id=1, source_target_pairs={{0,1},{1,0},{2,3},{3,2},{4,5},{5,4},{6,7},{7,6},{8,9},{9,8},{10,11... | collective-permute-start | bytes 786440 | tf_op jit(solution)/shard_map/ppermute | solution.py:405
  60.2 0.0 collective-permute-done.4.b1
  60.2 1.2 %collective-permute-done.6.b3 = bf16[8,64,256]{2,1,0:T(8,128)(2,1)S(1)} collective-permute-done((bf16[8,64,256]{2,1,0:T(8,128)(2,1)S(1)}, bf16[8,64,256]{2,1,0:T(8,128)(2,1)S(1)}, u32[]{:S(2)}, u32[]{:S(2)}) %collective-permute-start.6) | collective-permute-done | bytes 262176 | tf_op jit(solution)/shard_map/ppermute | solution.py:405
  61.3 0.0 copy-done.3
  61.4 0.7 copy-done.19
  62.0 9.2 %attention.1 = bf16[8,48,256]{2,1,0:T(8,128)(2,1)} custom-call(f32[2,16]{1,0:T(2,128)} %chain_ref.1, bf16[8,144,256]{2,1,0:T(8,128)(2,1)} %copy-done.3, bf16[8,96,256]{2,1,0:T(8,128)(2,1)} %collective-permute-done.3.far_ref, bf16[8,64,256]{2,1,0:T(8,128)(2,1)} %copy-done.6, bf16[8,64,256]{2,1,0:T(8,128)(2,1)} %copy-done.18, bf16[8,64,256]{2,1,0:T(8,128)(2,1)} %copy-done.17, ...), custom_call_target="tpu_custom_call" | custom-call | flops 402653184 | bytes 20000000 | tf_op jit(solution)/shard_map/attention/pallas_call | solution.py:315
  71.2 6.3 %all-to-all-start.2 = ((bf16[8,48,256]{2,1,0:T(8,128)(2,1)}), bf16[8,48,256]{2,1,0:T(8,128)(2,1)S(1)}, u32[]{:S(2)}, u32[]{:S(2)}) async-start(bf16[8,48,256]{2,1,0:T(8,128)(2,1)} %attention.1), calls=%async_computation.2 | async-start | bytes 393216 | tf_op jit(solution)/shard_map/all_to_all | solution.py:477
  77.5 0.0 collective-permute-done.10.d.w1
  77.6 0.0 collective-permute-done.11.c.w2
  77.6 0.0 copy-start.1
  77.6 0.0 collective-permute-done.12.b.w3
  77.6 0.7 copy-done
  78.3 0.2 copy-done.1
  78.5 0.2 copy-done.2
  78.7 2.1 %gated_sum.1.t0 = bf16[128,768]{1,0:T(8,128)(2,1)} custom-call(bf16[128,768]{1,0:T(8,128)(2,1)} %get-tuple-element.49.a, bf16[320,768]{1,0:T(8,128)(2,1)} %copy-done.2, bf16[320,768]{1,0:T(8,128)(2,1)} %copy-done.1, bf16[320,768]{1,0:T(8,128)(2,1)} %copy-done, f32[128,768]{1,0:T(8,128)} %get-tuple-element.50.gate_ref), custom_call_target="tpu_custom_call" | custom-call | flops 393216 | bytes 1376256 | tf_op jit(solution)/shard_map/gated_sum/pallas_call | solution.py:230
  80.8 0.0 collective-permute-start.13
  80.8 2.2 %collective-permute-start.14 = (bf16[128,768]{1,0:T(8,128)(2,1)}, bf16[128,768]{1,0:T(8,128)(2,1)S(1)}, u32[]{:S(2)}, u32[]{:S(2)}) collective-permute-start(bf16[128,768]{1,0:T(8,128)(2,1)} %gated_sum.1.t0), channel_id=1, source_target_pairs={{0,8},{4,12},{8,0},{12,4},{1,9},{5,13},{9,1},{13,5},{2,10},{6,14},... | collective-permute-start | bytes 589832 | tf_op jit(solution)/shard_map/ppermute | solution.py:409
  83.0 0.0 collective-permute-start.15
  83.0 4.0 %all-to-all-done.2.o_ref = bf16[8,48,256]{2,1,0:T(8,128)(2,1)S(1)} async-done(((bf16[8,48,256]{2,1,0:T(8,128)(2,1)}), bf16[8,48,256]{2,1,0:T(8,128)(2,1)S(1)}, u32[]{:S(2)}, u32[]{:S(2)}) %all-to-all-start.2) | async-done | bytes 196640 | tf_op jit(solution)/shard_map/all_to_all | solution.py:477
  87.0 0.7 copy-done.5
  87.7 1.8 %mix.1.m0 = bf16[192,512]{1,0:T(8,128)(2,1)} custom-call(f32[192,512]{1,0:T(8,128)} %get-tuple-element.28.gate_ref, bf16[8,48,256]{2,1,0:T(8,128)(2,1)} %copy-done.5), custom_call_target="tpu_custom_call" | custom-call | flops 98304 | bytes 786432 | tf_op jit(solution)/shard_map/mix/pallas_call | solution.py:353
  89.4 0.0 collective-permute-start.7
  89.4 2.2 %collective-permute-start.8 = (bf16[192,512]{1,0:T(8,128)(2,1)}, bf16[192,512]{1,0:T(8,128)(2,1)S(1)}, u32[]{:S(2)}, u32[]{:S(2)}) collective-permute-start(bf16[192,512]{1,0:T(8,128)(2,1)} %mix.1.m0), channel_id=1, source_target_pairs={{0,8},{4,12},{8,0},{12,4},{1,9},{5,13},{9,1},{13,5},{2,10},{6,14},... | collective-permute-start | bytes 589832 | tf_op jit(solution)/shard_map/ppermute | solution.py:409
  91.6 0.0 collective-permute-done.13.t1
  91.6 0.0 collective-permute-start.9
  91.6 0.0 collective-permute-done.14.t2
  91.6 0.0 copy-start.8
  91.6 1.6 %collective-permute-done.15.t3 = bf16[128,768]{1,0:T(8,128)(2,1)S(1)} collective-permute-done((bf16[128,768]{1,0:T(8,128)(2,1)}, bf16[128,768]{1,0:T(8,128)(2,1)S(1)}, u32[]{:S(2)}, u32[]{:S(2)}) %collective-permute-start.15) | collective-permute-done | bytes 196640 | tf_op jit(solution)/shard_map/ppermute | solution.py:409
  93.2 0.9 collective-permute-done.7.m1
  94.1 1.5 %collective-permute-done.8.m2 = bf16[192,512]{1,0:T(8,128)(2,1)S(1)} collective-permute-done((bf16[192,512]{1,0:T(8,128)(2,1)}, bf16[192,512]{1,0:T(8,128)(2,1)S(1)}, u32[]{:S(2)}, u32[]{:S(2)}) %collective-permute-start.8) | collective-permute-done | bytes 196640 | tf_op jit(solution)/shard_map/ppermute | solution.py:409
  95.7 4.8 %collective-permute-done.9.m3 = bf16[192,512]{1,0:T(8,128)(2,1)S(1)} collective-permute-done((bf16[192,512]{1,0:T(8,128)(2,1)}, bf16[192,512]{1,0:T(8,128)(2,1)S(1)}, u32[]{:S(2)}, u32[]{:S(2)}) %collective-permute-start.9) | collective-permute-done | bytes 196640 | tf_op jit(solution)/shard_map/ppermute | solution.py:409
  100.5 0.0 copy-done.7
  100.5 0.7 copy-done.12
  101.2 4.5 %finish.1 = bf16[512,768]{1,0:T(8,128)(2,1)} custom-call(bf16[192,512]{1,0:T(8,128)(2,1)} %mix.1.m0, bf16[192,512]{1,0:T(8,128)(2,1)} %copy-done.10, bf16[192,512]{1,0:T(8,128)(2,1)} %copy-done.11, bf16[192,512]{1,0:T(8,128)(2,1)} %copy-done.12, bf16[192,768]{1,0:T(8,128)(2,1)} %w0.1, bf16[320,768]{1,0:T(8,128)(2,1)} %copy-done, bf16[320,768]{1,0:T(8,128)(2,1)} %copy-done.1, ...), custom_call_target="tpu_custom_call" | custom-call | flops 603979776 | bytes 4718592 | tf_op jit(solution)/shard_map/finish/pallas_call | solution.py:381
  (24 shorter events, 0.1 us)
Async XLA Ops:
  5.4 17.5 %copy-start.4 = (bf16[768,2,384]{2,1,0:T(2,128)(2,1)S(1)}, bf16[768,2,384]{2,1,0:T(2,128)(2,1)}, u32[]{:S(2)}) copy-start(bf16[768,2,384]{2,1,0:T(2,128)(2,1)} %param.28) | copy-start | bytes 3538948
  5.4 28.8 %all-to-all-start = ((bf16[8,144,256]{2,1,0:T(8,128)(2,1)}), bf16[8,144,256]{2,1,0:T(8,128)(2,1)S(1)}, u32[]{:S(2)}, u32[]{:S(2)}) async-start(bf16[8,144,256]{2,1,0:T(8,128)(2,1)} %bitcast.20), calls=%async_computation | async-start | bytes 1179648 | tf_op jit(solution)/shard_map/all_to_all | solution.py:450
  17.9 13.5 %collective-permute-start = (bf16[4,32,128]{2,1,0:T(8,128)(2,1)}, bf16[4,32,128]{2,1,0:T(8,128)(2,1)S(1)}, u32[]{:S(2)}, u32[]{:S(2)}) collective-permute-start(bf16[4,32,128]{2,1,0:T(8,128)(2,1)} %get-tuple-element.37), channel_id=1, source_target_pairs={{0,4},{4,8},{8,12},{12,0},{1,5},{5,9},{9,13},{13,1},{2,6},{6,10},{... | collective-permute-start | bytes 98312 | tf_op jit(solution)/shard_map/ppermute | solution.py:409
  19.2 12.2 %collective-permute-start.1 = (bf16[4,32,128]{2,1,0:T(8,128)(2,1)}, bf16[4,32,128]{2,1,0:T(8,128)(2,1)S(1)}, u32[]{:S(2)}, u32[]{:S(2)}) collective-permute-start(bf16[4,32,128]{2,1,0:T(8,128)(2,1)} %get-tuple-element.38), channel_id=1, source_target_pairs={{0,8},{4,12},{8,0},{12,4},{1,9},{5,13},{9,1},{13,5},{2,10},{6,14},... | collective-permute-start | bytes 98312 | tf_op jit(solution)/shard_map/ppermute | solution.py:409
  21.9 9.6 %collective-permute-start.2 = (bf16[4,32,128]{2,1,0:T(8,128)(2,1)}, bf16[4,32,128]{2,1,0:T(8,128)(2,1)S(1)}, u32[]{:S(2)}, u32[]{:S(2)}) collective-permute-start(bf16[4,32,128]{2,1,0:T(8,128)(2,1)} %get-tuple-element.39), channel_id=1, source_target_pairs={{0,12},{4,0},{8,4},{12,8},{1,13},{5,1},{9,5},{13,9},{2,14},{6,2},{... | collective-permute-start | bytes 98312 | tf_op jit(solution)/shard_map/ppermute | solution.py:409
  31.4 22.3 %copy-start.16 = (bf16[320,768]{1,0:T(8,128)(2,1)S(1)}, bf16[320,768]{1,0:T(8,128)(2,1)}, u32[]{:S(2)}) copy-start(bf16[320,768]{1,0:T(8,128)(2,1)} %get-tuple-element.47) | copy-start | bytes 1474564
  31.4 0.6 copy-start.13
  31.5 0.6 copy-start.14
  32.1 0.6 copy-start.15
  34.3 27.0 %copy-start.3 = (bf16[8,144,256]{2,1,0:T(8,128)(2,1)}, bf16[8,144,256]{2,1,0:T(8,128)(2,1)S(1)}, u32[]{:S(2)}) copy-start(bf16[8,144,256]{2,1,0:T(8,128)(2,1)S(1)} %all-to-all-done.own_ref) | copy-start | bytes 1769476
  34.3 16.1 %all-to-all-start.1 = ((bf16[8,64,256]{2,1,0:T(8,128)(2,1)}), bf16[8,64,256]{2,1,0:T(8,128)(2,1)S(1)}, u32[]{:S(2)}, u32[]{:S(2)}) async-start(bf16[8,64,256]{2,1,0:T(8,128)(2,1)} %spread_bias.1), calls=%async_computation.1 | async-start | bytes 524288 | tf_op jit(solution)/shard_map/all_to_all | solution.py:467
  41.0 12.8 %collective-permute-start.3 = (bf16[8,96,256]{2,1,0:T(8,128)(2,1)S(1)}, bf16[8,96,256]{2,1,0:T(8,128)(2,1)}, u32[]{:S(2)}, u32[]{:S(2)}) collective-permute-start(bf16[8,96,256]{2,1,0:T(8,128)(2,1)S(1)} %slice.3), channel_id=1, source_target_pairs={{0,16},{16,0},{1,17},{17,1},{2,18},{18,2},{3,19},{19,3},{4,20},{20... | collective-permute-start | bytes 1179656 | tf_op jit(solution)/shard_map/ppermute | solution.py:405
  50.4 11.0 %copy-start.6 = (bf16[8,64,256]{2,1,0:T(8,128)(2,1)}, bf16[8,64,256]{2,1,0:T(8,128)(2,1)S(1)}, u32[]{:S(2)}) copy-start(bf16[8,64,256]{2,1,0:T(8,128)(2,1)S(1)} %all-to-all-done.1.b0) | copy-start | bytes 786436
  50.4 7.7 %collective-permute-start.5 = (bf16[8,64,256]{2,1,0:T(8,128)(2,1)S(1)}, bf16[8,64,256]{2,1,0:T(8,128)(2,1)S(1)}, u32[]{:S(2)}, u32[]{:S(2)}) collective-permute-start(bf16[8,64,256]{2,1,0:T(8,128)(2,1)S(1)} %all-to-all-done.1.b0), channel_id=1, source_target_pairs={{0,2},{2,0},{1,3},{3,1},{4,6},{6,4},{5,7},{7,5},{8,10},{10,8},{9,1... | collective-permute-start | bytes 786440 | tf_op jit(solution)/shard_map/ppermute | solution.py:405
  51.6 26.0 %collective-permute-start.10 = (bf16[320,768]{1,0:T(8,128)(2,1)}, bf16[320,768]{1,0:T(8,128)(2,1)S(1)}, u32[]{:S(2)}, u32[]{:S(2)}) collective-permute-start(bf16[320,768]{1,0:T(8,128)(2,1)} %get-tuple-element.45), channel_id=1, source_target_pairs={{0,12},{4,0},{8,4},{12,8},{1,13},{5,1},{9,5},{13,9},{2,14},{6,2},{... | collective-permute-start | bytes 1474568 | tf_op jit(solution)/shard_map/ppermute | solution.py:409
  51.6 26.0 %collective-permute-start.11 = (bf16[320,768]{1,0:T(8,128)(2,1)}, bf16[320,768]{1,0:T(8,128)(2,1)S(1)}, u32[]{:S(2)}, u32[]{:S(2)}) collective-permute-start(bf16[320,768]{1,0:T(8,128)(2,1)} %get-tuple-element.46), channel_id=1, source_target_pairs={{0,8},{4,12},{8,0},{12,4},{1,9},{5,13},{9,1},{13,5},{2,10},{6,14},... | collective-permute-start | bytes 1474568 | tf_op jit(solution)/shard_map/ppermute | solution.py:409
  53.8 23.8 %collective-permute-start.12 = (bf16[320,768]{1,0:T(8,128)(2,1)S(1)}, bf16[320,768]{1,0:T(8,128)(2,1)S(1)}, u32[]{:S(2)}, u32[]{:S(2)}) collective-permute-start(bf16[320,768]{1,0:T(8,128)(2,1)S(1)} %copy-done.16), channel_id=1, source_target_pairs={{0,4},{4,8},{8,12},{12,0},{1,5},{5,9},{9,13},{13,1},{2,6},{6,10},{... | collective-permute-start | bytes 1474568 | tf_op jit(solution)/shard_map/ppermute | solution.py:409
  53.8 6.4 %collective-permute-start.4 = (bf16[8,64,256]{2,1,0:T(8,128)(2,1)S(1)}, bf16[8,64,256]{2,1,0:T(8,128)(2,1)S(1)}, u32[]{:S(2)}, u32[]{:S(2)}) collective-permute-start(bf16[8,64,256]{2,1,0:T(8,128)(2,1)S(1)} %all-to-all-done.1.b0), channel_id=1, source_target_pairs={{0,1},{1,0},{2,3},{3,2},{4,5},{5,4},{6,7},{7,6},{8,9},{9,8},{10,11... | collective-permute-start | bytes 786440 | tf_op jit(solution)/shard_map/ppermute | solution.py:405
  58.1 3.2 %copy-start.17 = (bf16[8,64,256]{2,1,0:T(8,128)(2,1)}, bf16[8,64,256]{2,1,0:T(8,128)(2,1)S(1)}, u32[]{:S(2)}) copy-start(bf16[8,64,256]{2,1,0:T(8,128)(2,1)S(1)} %collective-permute-done.5.b2) | copy-start | bytes 786436
  58.1 3.2 %collective-permute-start.6 = (bf16[8,64,256]{2,1,0:T(8,128)(2,1)S(1)}, bf16[8,64,256]{2,1,0:T(8,128)(2,1)S(1)}, u32[]{:S(2)}, u32[]{:S(2)}) collective-permute-start(bf16[8,64,256]{2,1,0:T(8,128)(2,1)S(1)} %collective-permute-done.5.b2), channel_id=1, source_target_pairs={{0,1},{1,0},{2,3},{3,2},{4,5},{5,4},{6,7},{7,6},{8,9},{9,8},{10,11... | collective-permute-start | bytes 786440 | tf_op jit(solution)/shard_map/ppermute | solution.py:405
  60.2 1.2 %copy-start.18 = (bf16[8,64,256]{2,1,0:T(8,128)(2,1)}, bf16[8,64,256]{2,1,0:T(8,128)(2,1)S(1)}, u32[]{:S(2)}) copy-start(bf16[8,64,256]{2,1,0:T(8,128)(2,1)S(1)} %collective-permute-done.4.b1) | copy-start | bytes 786436
  61.3 0.7 copy-start.19
  71.2 15.7 %all-to-all-start.2 = ((bf16[8,48,256]{2,1,0:T(8,128)(2,1)}), bf16[8,48,256]{2,1,0:T(8,128)(2,1)S(1)}, u32[]{:S(2)}, u32[]{:S(2)}) async-start(bf16[8,48,256]{2,1,0:T(8,128)(2,1)} %attention.1), calls=%async_computation.2 | async-start | bytes 393216 | tf_op jit(solution)/shard_map/all_to_all | solution.py:477
  77.5 0.8 copy-start
  77.6 0.9 copy-start.1
  77.6 1.1 %copy-start.2 = (bf16[320,768]{1,0:T(8,128)(2,1)}, bf16[320,768]{1,0:T(8,128)(2,1)S(1)}, u32[]{:S(2)}) copy-start(bf16[320,768]{1,0:T(8,128)(2,1)S(1)} %collective-permute-done.12.b.w3) | copy-start | bytes 1474564
  80.8 10.8 %collective-permute-start.13 = (bf16[128,768]{1,0:T(8,128)(2,1)}, bf16[128,768]{1,0:T(8,128)(2,1)S(1)}, u32[]{:S(2)}, u32[]{:S(2)}) collective-permute-start(bf16[128,768]{1,0:T(8,128)(2,1)} %gated_sum.1.t0), channel_id=1, source_target_pairs={{0,12},{4,0},{8,4},{12,8},{1,13},{5,1},{9,5},{13,9},{2,14},{6,2},{... | collective-permute-start | bytes 589832 | tf_op jit(solution)/shard_map/ppermute | solution.py:409
  80.8 10.8 %collective-permute-start.14 = (bf16[128,768]{1,0:T(8,128)(2,1)}, bf16[128,768]{1,0:T(8,128)(2,1)S(1)}, u32[]{:S(2)}, u32[]{:S(2)}) collective-permute-start(bf16[128,768]{1,0:T(8,128)(2,1)} %gated_sum.1.t0), channel_id=1, source_target_pairs={{0,8},{4,12},{8,0},{12,4},{1,9},{5,13},{9,1},{13,5},{2,10},{6,14},... | collective-permute-start | bytes 589832 | tf_op jit(solution)/shard_map/ppermute | solution.py:409
  83.0 10.2 %collective-permute-start.15 = (bf16[128,768]{1,0:T(8,128)(2,1)}, bf16[128,768]{1,0:T(8,128)(2,1)S(1)}, u32[]{:S(2)}, u32[]{:S(2)}) collective-permute-start(bf16[128,768]{1,0:T(8,128)(2,1)} %gated_sum.1.t0), channel_id=1, source_target_pairs={{0,4},{4,8},{8,12},{12,0},{1,5},{5,9},{9,13},{13,1},{2,6},{6,10},{... | collective-permute-start | bytes 589832 | tf_op jit(solution)/shard_map/ppermute | solution.py:409
  87.0 0.7 copy-start.5
  89.4 4.7 %collective-permute-start.7 = (bf16[192,512]{1,0:T(8,128)(2,1)}, bf16[192,512]{1,0:T(8,128)(2,1)S(1)}, u32[]{:S(2)}, u32[]{:S(2)}) collective-permute-start(bf16[192,512]{1,0:T(8,128)(2,1)} %mix.1.m0), channel_id=1, source_target_pairs={{0,12},{4,0},{8,4},{12,8},{1,13},{5,1},{9,5},{13,9},{2,14},{6,2},{... | collective-permute-start | bytes 589832 | tf_op jit(solution)/shard_map/ppermute | solution.py:409
  89.4 6.3 %collective-permute-start.8 = (bf16[192,512]{1,0:T(8,128)(2,1)}, bf16[192,512]{1,0:T(8,128)(2,1)S(1)}, u32[]{:S(2)}, u32[]{:S(2)}) collective-permute-start(bf16[192,512]{1,0:T(8,128)(2,1)} %mix.1.m0), channel_id=1, source_target_pairs={{0,8},{4,12},{8,0},{12,4},{1,9},{5,13},{9,1},{13,5},{2,10},{6,14},... | collective-permute-start | bytes 589832 | tf_op jit(solution)/shard_map/ppermute | solution.py:409
  91.6 8.9 %copy-start.7 = (bf16[128,768]{1,0:T(8,128)(2,1)}, bf16[128,768]{1,0:T(8,128)(2,1)S(1)}, u32[]{:S(2)}) copy-start(bf16[128,768]{1,0:T(8,128)(2,1)S(1)} %collective-permute-done.13.t1) | copy-start | bytes 589828
  91.6 8.8 %collective-permute-start.9 = (bf16[192,512]{1,0:T(8,128)(2,1)}, bf16[192,512]{1,0:T(8,128)(2,1)S(1)}, u32[]{:S(2)}, u32[]{:S(2)}) collective-permute-start(bf16[192,512]{1,0:T(8,128)(2,1)} %mix.1.m0), channel_id=1, source_target_pairs={{0,4},{4,8},{8,12},{12,0},{1,5},{5,9},{9,13},{13,1},{2,6},{6,10},{... | collective-permute-start | bytes 589832 | tf_op jit(solution)/shard_map/ppermute | solution.py:409
  91.6 8.8 %copy-start.8 = (bf16[128,768]{1,0:T(8,128)(2,1)}, bf16[128,768]{1,0:T(8,128)(2,1)S(1)}, u32[]{:S(2)}) copy-start(bf16[128,768]{1,0:T(8,128)(2,1)S(1)} %collective-permute-done.14.t2) | copy-start | bytes 589828
  93.2 7.2 %copy-start.9 = (bf16[128,768]{1,0:T(8,128)(2,1)}, bf16[128,768]{1,0:T(8,128)(2,1)S(1)}, u32[]{:S(2)}) copy-start(bf16[128,768]{1,0:T(8,128)(2,1)S(1)} %collective-permute-done.15.t3) | copy-start | bytes 589828
  94.1 6.3 %copy-start.10 = (bf16[192,512]{1,0:T(8,128)(2,1)}, bf16[192,512]{1,0:T(8,128)(2,1)S(1)}, u32[]{:S(2)}) copy-start(bf16[192,512]{1,0:T(8,128)(2,1)S(1)} %collective-permute-done.7.m1) | copy-start | bytes 589828
  95.7 4.8 %copy-start.11 = (bf16[192,512]{1,0:T(8,128)(2,1)}, bf16[192,512]{1,0:T(8,128)(2,1)S(1)}, u32[]{:S(2)}) copy-start(bf16[192,512]{1,0:T(8,128)(2,1)S(1)} %collective-permute-done.8.m2) | copy-start | bytes 589828
  100.5 0.7 copy-start.12

commit v3 on v2

--- a/solution.py
+++ b/solution.py
@@ -8,6 +8,7 @@
 HD = 48
 BF = jnp.bfloat16
 F32 = jnp.float32
+LOG2E = 1.4426950408889634
 NT = (((1,), (1,)), ((), ()))
 TN = (((0,), (0,)), ((), ()))
 
@@ -33,6 +34,23 @@
 def whole(shape):
     zeros = (0,) * len(shape)
     return pl.BlockSpec(shape, lambda *_: zeros)
+
+
+ANY = pl.BlockSpec(memory_space=pl.ANY)
+
+
+def fetch(pairs, sems):
+    copies = [
+        pltpu.make_async_copy(source, target, sems.at[i])
+        for i, (source, target) in enumerate(pairs)
+    ]
+    for copy in copies:
+        copy.start()
+    return copies
+
+
+def room(*shapes, dtype=BF):
+    return [pltpu.VMEM(shape, dtype) for shape in shapes]
 
 
 def tile_bias_kernel(pair_ref, gain_ref, proj_ref, o0, o1, o2, o3):
@@ -95,7 +113,7 @@
         out_specs=whole(shape),
         grid=(1,),
         out_shape=jax.ShapeDtypeStruct(shape, BF),
-        compiler_params=params(),
+        compiler_params=params(8),
         cost_estimate=cost(0, 500_000),
         name="spread_bias",
     )(*tiles)
@@ -156,6 +174,11 @@
         ),
         name="project",
     )(act, cond, gain.reshape(cwidth // 128, 128), scale, shift, w)
+
+
+def half_rows(rows, other=0):
+    start = (lax.axis_index("core") ^ other) * (rows // 2)
+    return pl.ds(pl.multiple_of(start, rows // 2), rows // 2)
 
 
 def transition_kernel(
@@ -178,7 +201,7 @@
         start = pl.multiple_of(lax.rem(mine + shift, 4) * quarter, quarter)
         ref[:quarter] = part_ref[pl.ds(start, quarter), :]
         if shift:
-            ref[quarter:] = last_ref[...]
+            ref[quarter:] = last_ref[half_rows(last_ref.shape[0]), :]
     g0_ref[...] = jax.nn.sigmoid(dot(cond_norm, og_ref[0]))
     own = cn_ref[pl.ds(pl.multiple_of(mine * quarter, quarter), quarter), :]
     g1_ref[...] = jax.nn.sigmoid(dot(own, og_ref[1]))
@@ -189,7 +212,7 @@
     cwidth = cond_norm.shape[1]
     quarter = rows // 4
     second = pl.BlockSpec((1, cwidth, width), lambda i: (1, 0, 0))
-    both = (quarter + last.shape[0], width)
+    both = (quarter + last.shape[0] // 2, width)
     return pl.pallas_call(
         transition_kernel,
         grid=(1,),
@@ -219,22 +242,25 @@
     )(act, cond_norm, scale, shift, out_gate, w_in, w_out, last)
 
 
-def gated_sum_kernel(a, b, c, d, gate_ref, out_ref):
+def gated_sum_kernel(a, b, c, d, gate_ref, out_ref, pack_ref):
     rows = slice(0, a.shape[0])
     total = (a[...].astype(F32) + b[rows].astype(F32)) + (c[rows].astype(F32) + d[rows].astype(F32))
     out_ref[...] = (total * gate_ref[...]).astype(BF)
+    for i, ref in enumerate((d, c, b)):
+        pack_ref[i] = ref[a.shape[0] :]
 
 
 def gated_sum(parts, gate):
     shape = gate.shape
+    pack = (3, parts[1].shape[0] - shape[0], shape[1])
     return pl.pallas_call(
         gated_sum_kernel,
         grid=(1,),
-        in_specs=[whole(shape)] * 5,
-        out_specs=whole(shape),
-        out_shape=jax.ShapeDtypeStruct(shape, BF),
-        compiler_params=params(),
-        cost_estimate=cost(4 * gate.size, gate.size * 14),
+        in_specs=[whole(x.shape) for x in (*parts, gate)],
+        out_specs=[whole(shape), whole(pack)],
+        out_shape=[jax.ShapeDtypeStruct(shape, BF), jax.ShapeDtypeStruct(pack, BF)],
+        compiler_params=params(8),
+        cost_estimate=cost(30_000_000_000, 1000),
         name="gated_sum",
     )(*parts, gate)
 
@@ -242,9 +268,9 @@
 def attention_kernel(
     chain_ref, own_ref, far_ref, b0, b1, b2, b3, id_ref, out_ref, k_ref, v_ref, kid_ref, turn_ref, qid_ref
 ):
-    samples, pieces, _, span = k_ref.shape
+    samples, cols, pieces = k_ref.shape[0], 4, 4
     half = own_ref.shape[2] // samples
-    cols = span // half
+    span = cols * half
     blocks = b0.shape[0]
     z, xh, col = (lax.axis_index(name) for name in ("z", "xh", "col"))
     grp = 2 * lax.axis_index("xlo") + lax.axis_index("core")
@@ -262,43 +288,34 @@
                 values.append(jnp.where(near, own_ref[at, 2 * HD :], far_ref[at, HD:]))
                 line = id_ref[pl.ds(at, 1), :]
                 ids.append(jnp.where((g & 1) == 0, line[:, :half], line[:, half:]))
-            kid_ref[piece] = jnp.concatenate(ids, axis=1)
+            here = slice(piece * span, (piece + 1) * span)
+            kid_ref[:, here] = jnp.concatenate(ids, axis=1)
             for s in range(samples):
                 lanes = slice(s * half, (s + 1) * half)
-                k_ref[s, piece] = jnp.concatenate([x[:, lanes] for x in keys], axis=1)
-                v_ref[s, piece] = jnp.concatenate([x[:, lanes] for x in values], axis=1)
+                k_ref[s, :, here] = jnp.concatenate([x[:, lanes] for x in keys], axis=1)
+                v_ref[s, :, here] = jnp.concatenate([x[:, lanes] for x in values], axis=1)
         turn_ref[...] = jnp.transpose(id_ref[...])
         for at in range(id_ref.shape[0]):
             qid_ref[at] = turn_ref[pl.ds(pl.multiple_of(xh * half, half), half), at : at + 1]
 
     step = pl.program_id(0)
     head = col * 4 + z // 2
-    other, same = chain_ref[0, head], chain_ref[1, head]
+    other, same = chain_ref[0, head] * LOG2E, chain_ref[1, head] * LOG2E
     qid = qid_ref[pl.ds(step * blocks, blocks)].reshape(blocks * half, 1)
-    totals = []
-    for piece, ref in enumerate((b0, b1, b2, b3)):
-        bias = ref[...].reshape(blocks * half, span).astype(F32)
-        totals.append(bias + jnp.where(qid == kid_ref[piece], same, other))
-    scale = HD ** (-0.5)
+    bias = jnp.concatenate(
+        [ref[...].reshape(blocks * half, span) for ref in (b0, b1, b2, b3)], axis=1
+    ).astype(F32)
+    bias = bias * LOG2E + jnp.where(qid == kid_ref[...], same, other)
+    scale = HD ** (-0.5) * LOG2E
     results = []
     queries = [own_ref[step * blocks + b, :HD] for b in range(blocks)]
     for s in range(samples):
         lanes = slice(s * half, (s + 1) * half)
         query = jnp.concatenate([q[:, lanes] for q in queries], axis=1)
-        scores = [
-            lax.dot_general(query, k_ref[s, p], TN, preferred_element_type=F32) * scale + totals[p]
-            for p in range(pieces)
-        ]
-        top = jnp.max(
-            jnp.maximum(jnp.maximum(scores[0], scores[1]), jnp.maximum(scores[2], scores[3])),
-            axis=1,
-            keepdims=True,
-        )
-        weights = [jnp.exp(x - top) for x in scores]
-        total = jnp.sum(
-            (weights[0] + weights[1]) + (weights[2] + weights[3]), axis=1, keepdims=True
-        )
-        summed = sum(dot(weights[p].astype(BF), v_ref[s, p], NT) for p in range(pieces))
+        scores = dot(query, k_ref[s], TN) * scale + bias
+        weights = jnp.exp2(scores - jnp.max(scores, axis=1, keepdims=True))
+        total = jnp.sum(weights, axis=1, keepdims=True)
+        summed = dot(weights.astype(BF), v_ref[s], NT)
         results.append(jnp.transpose(summed / total).astype(BF))
     for b in range(blocks):
         out_ref[b] = jnp.concatenate([r[:, b * half : (b + 1) * half] for r in results], axis=1)
@@ -309,7 +326,7 @@
     half = 64
     samples = lanes // half
     span = biases[0].shape[2]
-    blocks = 2
+    blocks = count
     bias_spec = pl.BlockSpec((blocks, half, span), lambda i: (i, 0, 0))
     tokens = 2 * count * half
     return pl.pallas_call(
@@ -328,14 +345,14 @@
         out_specs=pl.BlockSpec((blocks, HD, lanes), lambda i: (i, 0, 0)),
         out_shape=jax.ShapeDtypeStruct((count, HD, lanes), BF),
         scratch_shapes=[
-            pltpu.VMEM((samples, 4, HD, span), BF),
-            pltpu.VMEM((samples, 4, HD, span), BF),
-            pltpu.VMEM((4, 1, span), jnp.int32),
+            pltpu.VMEM((samples, HD, 4 * span), BF),
+            pltpu.VMEM((samples, HD, 4 * span), BF),
+            pltpu.VMEM((1, 4 * span), jnp.int32),
             pltpu.VMEM((ids.shape[1], ids.shape[0]), jnp.int32),
             pltpu.VMEM((count, half, 1), jnp.int32),
         ],
-        compiler_params=params(),
-        cost_estimate=cost(8 * tokens * tokens * HD, 20_000_000, 2 * tokens * tokens),
+        compiler_params=params(32),
+        cost_estimate=cost(0, 1000),
         name="attention",
     )(chain_bias, own, far, *biases, ids)
 
@@ -356,49 +373,68 @@
         in_specs=[whole(gates.shape), whole(attended.shape)],
         out_specs=whole(gates.shape),
         out_shape=jax.ShapeDtypeStruct(gates.shape, BF),
-        compiler_params=params(),
+        compiler_params=params(8),
         cost_estimate=cost(gates.size, gates.size * 8),
         name="mix",
     )(gates, attended)
 
 
-def finish_kernel(m0, m1, m2, m3, w0, w1, w2, w3, g0_ref, t0, t1, t2, t3, out_ref, total_ref):
+def finish_kernel(
+    m0, m1, m2, m3, w0, wa, wb, g0_hbm, t0, t1, t2, t3, out_hbm,
+    m_ref, w_ref, g0_ref, t_ref, total_ref, out_ref, in_sems, out_sems,
+):
     mine = lax.axis_index("col")
-    total = None
-    depth = m0.shape[0]
-    for ref, w in zip((m0, m1, m2, m3), (w0, w1, w2, w3)):
-        term = lax.dot_general(ref[...], w[-depth:], TN, preferred_element_type=F32)
-        total = term if total is None else total + term
+    depth = w_ref.shape[1]
+    copies = fetch(
+        [
+            *[(source, m_ref.at[i]) for i, source in enumerate((m0, m1, m2, m3))],
+            (w0, w_ref.at[0]),
+            *[(wa.at[i], w_ref.at[i + 1, half_rows(depth)]) for i in range(3)],
+            *[(wb.at[i], w_ref.at[i + 1, half_rows(depth, 1)]) for i in range(3)],
+            (g0_hbm, g0_ref),
+            *[(source, t_ref.at[i]) for i, source in enumerate((t0, t1, t2, t3))],
+        ],
+        in_sems,
+    )
+    for i in range(11):
+        copies[i].wait()
+    mixed = m_ref[...].reshape(-1, m_ref.shape[2])
+    total = dot(mixed, w_ref[...].reshape(-1, w_ref.shape[2]), TN)
+    copies[11].wait()
     total_ref[...] = g0_ref[...] * total
-    quarter = t0.shape[0]
-    for shift, ref in enumerate((t0, t1, t2, t3)):
-        rows = pl.ds(pl.multiple_of(((mine + shift) % 4) * quarter, quarter), quarter)
-        out_ref[rows, :] = (total_ref[rows, :] + ref[...].astype(F32)).astype(BF)
+    quarter = t_ref.shape[1]
+    outs = []
+    for shift in range(4):
+        copies[12 + shift].wait()
+        rows = pl.ds(pl.multiple_of(lax.rem(mine + shift, 4) * quarter, quarter), quarter)
+        out_ref[shift] = (total_ref[rows, :] + t_ref[shift].astype(F32)).astype(BF)
+        outs.append(pltpu.make_async_copy(out_ref.at[shift], out_hbm.at[rows], out_sems.at[shift]))
+        outs[shift].start()
+    for copy in outs:
+        copy.wait()
 
 
 def finish(mixed, w, g0, trans):
     rows, width = g0.shape
     return pl.pallas_call(
         finish_kernel,
-        grid=(1,),
-        in_specs=[whole(x.shape) for x in (*mixed, *w, g0, *trans)],
-        out_specs=whole((rows, width)),
+        in_specs=[ANY] * 12,
+        out_specs=ANY,
         out_shape=jax.ShapeDtypeStruct((rows, width), BF),
-        scratch_shapes=[pltpu.VMEM((rows, width), F32)],
+        scratch_shapes=[
+            pltpu.VMEM((4, *mixed[0].shape), BF),
+            pltpu.VMEM((4, *w[0].shape), BF),
+            pltpu.VMEM((rows, width), F32),
+            pltpu.VMEM((4, rows // 4, width), BF),
+            pltpu.VMEM((rows, width), F32),
+            pltpu.VMEM((4, rows // 4, width), BF),
+            pltpu.SemaphoreType.DMA((16,)),
+            pltpu.SemaphoreType.DMA((4,)),
+        ],
         compiler_params=params(),
         cost_estimate=cost(2 * rows * width * width, rows * width * 12),
         name="finish",
     )(*mixed, *w, g0, *trans)
-
-
-def around(x):
-    return [x] + [
-        lax.ppermute(x, "col", [((i + k) % 4, i) for i in range(4)]) for k in (1, 3, 2)
-    ]
-
-
-def in_order(pieces):
-    return [pieces[0], pieces[1], pieces[3], pieces[2]]
 
 
 def swap(x, axis):
@@ -450,32 +486,27 @@
     own = lax.all_to_all(qkv.reshape(8, 3 * HD, 4 * rows), "z", 0, 0, tiled=True)
     proj = jnp.transpose(bias_proj).reshape(4, heads, -1)
     tiles = tile_bias(pair, pair_gain, proj)
-    *tiles, act = tie(*tiles, act)
-    *parts, g0, g1 = transition(
-        act,
-        cond_norm,
-        ada_scale,
-        ada_shift,
-        out_gate,
-        trans_in.reshape(width, -1),
-        trans_out,
-        attn_out,
-    )
-    parts = scatter(parts)
     spread = spread_bias(scatter(tiles), 8)
-    own, spread, g0 = tie(own, spread, g0)
+    win = trans_in.reshape(width, -1)
+    own, spread, act, win = tie(own, spread, act, win)
     bias0 = lax.all_to_all(spread, "z", 0, 0, tiled=True)
     far = swap(own[:, HD:], "xh")
+    *parts, g0, g1 = transition(
+        act, cond_norm, ada_scale, ada_shift, out_gate, win, trans_out, attn_out
+    )
+    bias0, g0 = tie(bias0, g0)
+    far, *parts = tie(far, *parts)
+    parts = scatter(parts)
     bias2 = swap(bias0, "xlo")
     bias1 = swap(bias0, "core")
     bias3 = swap(bias2, "core")
-    quarter = gated_sum(parts, g1)
+    quarter, pack = gated_sum(parts, g1)
     trans = around(quarter)
+    w_out_all = [attn_out, pack, swap(pack, "core")]
     attended = attention(
         chain_bias, own, far, (bias0, bias1, bias2, bias3), chain_ids.reshape(8, 2 * rows)
     )
     attended = lax.all_to_all(attended, "z", 0, 0, tiled=True)
-    w_out_all = [attn_out, parts[3], parts[2], parts[1]]
     updated = finish(around(mix(gates, attended)), w_out_all, g0, trans)
     return updated.reshape(samples, rows, width)
 

time: 107 us -> 98.9 us (0.924)
  Pallas kernels: 35.3 us -> 26.5 us
  waiting for transfers between devices: 20.5 us -> 25.1 us
  local copies, waits for them, and re-layouts: 5.65 us -> 2 us
    all_to_all x1, waiting for transfers between devices: 0.01 us -> 8.01 us  [body(): lax.all_to_all(qkv.reshape(8, 3 * HD, 4 * rows), 'z', 0, 0, tiled=True)]
    ppermute x12, starting transfers between devices: 11.6 us -> 19.5 us  [send(): return lax.ppermute(x, 'col', [(i, (i + k) % 4) for i in range(4)])]
    all_to_all x1, waiting for transfers between devices: 6.58 us -> 1.95 us  [body(): bias0 = lax.all_to_all(spread, 'z', 0, 0, tiled=True)]
    unnamed x41 -> x35, local copies, waits for them, and re-layouts: 5.62 us -> 1.98 us
    pallas_call x1, Pallas kernels: 9.21 us -> 5.92 us  [attention(): pl.pallas_call(attention_kernel, grid=(count // blocks,), in_specs=[pl.Bl...]
    all_to_all x1, starting transfers between devices: 6.65 us -> 3.41 us  [body(): bias0 = lax.all_to_all(spread, 'z', 0, 0, tiled=True)]
    ppermute x4 -> x5, starting transfers between devices: 10.4 us -> 7.34 us  [swap(): return lax.ppermute(x, axis, [(0, 1), (1, 0)])]
    pallas_call x2, Pallas kernels: 6.68 us -> 3.75 us  [the longest x1 3.62 us: finish(): pl.pallas_call(finish_kernel, in_specs=[ANY] * 12, out_specs=ANY, out_sha...]
  transfers between devices with their start and end apart: 19 -> 20, of which waited for: 7 -> 9; matrix products, arithmetic and copies ran while one was open for 1% -> 1% of each run, Pallas kernels for 24% -> 18%
where the time goes in v3:
time: 98.9 us; the launch traced here: 98.5 us
  starting transfers between devices  44.5 us (45%)
  Pallas kernels  26.5 us (27%)
  waiting for transfers between devices  25.1 us (25%)
  local copies, waits for them, and re-layouts  2 us (2%)
    ppermute x12, starting transfers between devices, send(): return lax.ppermute(x, 'col', [(i, (i + k) % 4) for i in range(4)])  19.5 us
    all_to_all x1, starting transfers between devices, body(): lax.all_to_all(qkv.reshape(8, 3 * HD, 4 * rows), 'z', 0, 0, tiled=True)  9.14 us
    ppermute x12, waiting for transfers between devices, send(): return lax.ppermute(x, 'col', [(i, (i + k) % 4) for i in range(4)])  8.8 us
    all_to_all x1, waiting for transfers between devices, body(): lax.all_to_all(qkv.reshape(8, 3 * HD, 4 * rows), 'z', 0, 0, tiled=True)  8.01 us
    ppermute x5, starting transfers between devices, swap(): return lax.ppermute(x, axis, [(0, 1), (1, 0)])  7.34 us
    pallas_call x1, Pallas kernels, transition(): pl.pallas_call(transition_kernel, grid=(1,), in_specs=[whole(act.shape),...  7.2 us
    pallas_call x1, Pallas kernels, attention(): pl.pallas_call(attention_kernel, grid=(count // blocks,), in_specs=[pl.Bl...  5.92 us
    pallas_call x1, Pallas kernels, project(): pl.pallas_call(project_kernel, grid=(rows // step,), in_specs=[pl.BlockSp...  5.44 us
  transfers between devices with their start and end apart: 20, of which 9 were waited for; matrix products, arithmetic and copies ran while one was open for 1% of the time, Pallas kernels for 18%

profile of v3, /device:TPU:1, one launch (start us, length us, event | category | flops | bytes accessed | tf_op | source)
XLA Modules:
  0.0 98.5 jit_solution(7707645435286980295)
XLA Ops:
  0.0 5.4 %project.1 = (bf16[4,2,144,256]{3,2,1,0:T(8,128)(2,1)}, f32[192,512]{1,0:T(8,128)}, bf16[512,384]{1,0:T(8,128)(2,1)}) custom-call(bf16[512,768]{1,0:T(8,128)(2,1)} %bitcast.16, bf16[512,384]{1,0:T(8,128)(2,1)} %bitcast.22, f32[3,128]{1,0:T(4,128)} %bitcast.24, bf16[2,384,768]{2,1,0:T(8,128)(2,1)} %scale_ref.3, bf16[2,384,768]{2,1,0:T(8,128)(2,1)} %shift_ref.3, ...), custom_call_target="tpu_custom_call" | custom-call | flops 1207959552 | bytes 2359296 | tf_op jit(solution)/shard_map/project/pallas_call | solution.py:150
  5.4 9.1 %all-to-all-start = ((bf16[8,144,256]{2,1,0:T(8,128)(2,1)}), bf16[8,144,256]{2,1,0:T(8,128)(2,1)S(1)}, u32[]{:S(2)}, u32[]{:S(2)}) async-start(bf16[8,144,256]{2,1,0:T(8,128)(2,1)} %bitcast.21), calls=%async_computation | async-start | bytes 1179648 | tf_op jit(solution)/shard_map/all_to_all | solution.py:486
  14.6 3.3 %tile_bias.1 = (bf16[4,32,128]{2,1,0:T(8,128)(2,1)}, bf16[4,32,128]{2,1,0:T(8,128)(2,1)}, bf16[4,32,128]{2,1,0:T(8,128)(2,1)}, bf16[4,32,128]{2,1,0:T(8,128)(2,1)}) custom-call(bf16[2,32,64,128]{3,2,1,0:T(8,128)(2,1)} %bitcast.20, f32[1,128]{1,0:T(1,128)} %bitcast.25, bf16[4,4,128]{2,1,0:T(4,128)(2,1)} %bitcast.23), custom_call_target="tpu_custom_call" | custom-call | bytes 500000 | tf_op jit(solution)/shard_map/tile_bias/pallas_call | solution.py:78
  17.9 1.4 %collective-permute-start = (bf16[4,32,128]{2,1,0:T(8,128)(2,1)}, bf16[4,32,128]{2,1,0:T(8,128)(2,1)S(1)}, u32[]{:S(2)}, u32[]{:S(2)}) collective-permute-start(bf16[4,32,128]{2,1,0:T(8,128)(2,1)} %get-tuple-element.38), channel_id=1, source_target_pairs={{0,4},{4,8},{8,12},{12,0},{1,5},{5,9},{9,13},{13,1},{2,6},{6,10},{... | collective-permute-start | bytes 98312 | tf_op jit(solution)/shard_map/ppermute | solution.py:445
  19.2 2.6 %collective-permute-start.1 = (bf16[4,32,128]{2,1,0:T(8,128)(2,1)}, bf16[4,32,128]{2,1,0:T(8,128)(2,1)S(1)}, u32[]{:S(2)}, u32[]{:S(2)}) collective-permute-start(bf16[4,32,128]{2,1,0:T(8,128)(2,1)} %get-tuple-element.39), channel_id=1, source_target_pairs={{0,8},{4,12},{8,0},{12,4},{1,9},{5,13},{9,1},{13,5},{2,10},{6,14},... | collective-permute-start | bytes 98312 | tf_op jit(solution)/shard_map/ppermute | solution.py:445
  21.9 1.1 %collective-permute-start.2 = (bf16[4,32,128]{2,1,0:T(8,128)(2,1)}, bf16[4,32,128]{2,1,0:T(8,128)(2,1)S(1)}, u32[]{:S(2)}, u32[]{:S(2)}) collective-permute-start(bf16[4,32,128]{2,1,0:T(8,128)(2,1)} %get-tuple-element.40), channel_id=1, source_target_pairs={{0,12},{4,0},{8,4},{12,8},{1,13},{5,1},{9,5},{13,9},{2,14},{6,2},{... | collective-permute-start | bytes 98312 | tf_op jit(solution)/shard_map/ppermute | solution.py:445
  22.9 0.0 copy-done.9
  22.9 1.2 %copy.16 = bf16[96,8,2,384]{3,1,2,0:T(8,128)(2,1)} copy(bf16[96,8,2,384]{3,2,1,0:T(2,128)(2,1)S(1)} %bitcast.18) | data formatting | bytes 2359296
  24.2 0.0 collective-permute-done.t1
  24.2 0.0 collective-permute-done.1.t2
  24.2 0.9 collective-permute-done.2.t3
  25.1 0.0 copy-done.4
  25.1 0.8 spread_bias.1
  25.9 8.0 %all-to-all-done.own_ref = bf16[8,144,256]{2,1,0:T(8,128)(2,1)S(1)} async-done(((bf16[8,144,256]{2,1,0:T(8,128)(2,1)}), bf16[8,144,256]{2,1,0:T(8,128)(2,1)S(1)}, u32[]{:S(2)}, u32[]{:S(2)}) %all-to-all-start) | async-done | bytes 589856 | tf_op jit(solution)/shard_map/all_to_all | solution.py:486
  33.9 3.4 %all-to-all-start.1 = ((bf16[8,64,256]{2,1,0:T(8,128)(2,1)}), bf16[8,64,256]{2,1,0:T(8,128)(2,1)S(1)}, u32[]{:S(2)}, u32[]{:S(2)}) async-start(bf16[8,64,256]{2,1,0:T(8,128)(2,1)} %spread_bias.1), calls=%async_computation.1 | async-start | bytes 524288 | tf_op jit(solution)/shard_map/all_to_all | solution.py:492
  37.4 2.8 %collective-permute-start.3 = (bf16[8,96,256]{2,1,0:T(8,128)(2,1)S(1)}, bf16[8,96,256]{2,1,0:T(8,128)(2,1)S(1)}, u32[]{:S(2)}, u32[]{:S(2)}) collective-permute-start(bf16[8,96,256]{2,1,0:T(8,128)(2,1)S(1)} %slice.3), channel_id=1, source_target_pairs={{0,16},{16,0},{1,17},{17,1},{2,18},{18,2},{3,19},{19,3},{4,20},{20... | collective-permute-start | bytes 1179656 | tf_op jit(solution)/shard_map/ppermute | solution.py:441
  40.2 7.2 %transition.1 = (bf16[128,768]{1,0:T(8,128)(2,1)}, bf16[224,768]{1,0:T(8,128)(2,1)}, bf16[224,768]{1,0:T(8,128)(2,1)}, bf16[224,768]{1,0:T(8,128)(2,1)}, f32[512,768]{1,0:T(8,128)}, /*index=5*/f32[128,768]{1,0:T(8,128)}) custom-call(bf16[512,768]{1,0:T(8,128)(2,1)} %bitcast.17, bf16[512,384]{1,0:T(8,128)(2,1)} %get-tuple-element.43.cn_ref, ...), custom_call_target="tpu_custom_call" | custom-call | bytes 2000000 | tf_op jit(solution)/shard_map/transition/pallas_call | solution.py:216
  47.4 2.0 %all-to-all-done.1.b0 = bf16[8,64,256]{2,1,0:T(8,128)(2,1)S(1)} async-done(((bf16[8,64,256]{2,1,0:T(8,128)(2,1)}), bf16[8,64,256]{2,1,0:T(8,128)(2,1)S(1)}, u32[]{:S(2)}, u32[]{:S(2)}) %all-to-all-start.1) | async-done | bytes 262176 | tf_op jit(solution)/shard_map/all_to_all | solution.py:492
  49.4 1.2 %collective-permute-start.5 = (bf16[8,64,256]{2,1,0:T(8,128)(2,1)S(1)}, bf16[8,64,256]{2,1,0:T(8,128)(2,1)S(1)}, u32[]{:S(2)}, u32[]{:S(2)}) collective-permute-start(bf16[8,64,256]{2,1,0:T(8,128)(2,1)S(1)} %all-to-all-done.1.b0), channel_id=1, source_target_pairs={{0,2},{2,0},{1,3},{3,1},{4,6},{6,4},{5,7},{7,5},{8,10},{10,8},{9,1... | collective-permute-start | bytes 786440 | tf_op jit(solution)/shard_map/ppermute | solution.py:441
  50.6 0.0 collective-permute-done.3.far_ref
  50.6 1.3 %collective-permute-start.10 = (bf16[224,768]{1,0:T(8,128)(2,1)}, bf16[224,768]{1,0:T(8,128)(2,1)S(1)}, u32[]{:S(2)}, u32[]{:S(2)}) collective-permute-start(bf16[224,768]{1,0:T(8,128)(2,1)} %get-tuple-element.54), channel_id=1, source_target_pairs={{0,4},{4,8},{8,12},{12,0},{1,5},{5,9},{9,13},{13,1},{2,6},{6,10},{... | collective-permute-start | bytes 1032200 | tf_op jit(solution)/shard_map/ppermute | solution.py:445
  51.9 2.6 %collective-permute-start.11 = (bf16[224,768]{1,0:T(8,128)(2,1)}, bf16[224,768]{1,0:T(8,128)(2,1)S(1)}, u32[]{:S(2)}, u32[]{:S(2)}) collective-permute-start(bf16[224,768]{1,0:T(8,128)(2,1)} %get-tuple-element.55), channel_id=1, source_target_pairs={{0,8},{4,12},{8,0},{12,4},{1,9},{5,13},{9,1},{13,5},{2,10},{6,14},... | collective-permute-start | bytes 1032200 | tf_op jit(solution)/shard_map/ppermute | solution.py:445
  54.5 1.1 %collective-permute-start.12 = (bf16[224,768]{1,0:T(8,128)(2,1)}, bf16[224,768]{1,0:T(8,128)(2,1)S(1)}, u32[]{:S(2)}, u32[]{:S(2)}) collective-permute-start(bf16[224,768]{1,0:T(8,128)(2,1)} %get-tuple-element.56), channel_id=1, source_target_pairs={{0,12},{4,0},{8,4},{12,8},{1,13},{5,1},{9,5},{13,9},{2,14},{6,2},{... | collective-permute-start | bytes 1032200 | tf_op jit(solution)/shard_map/ppermute | solution.py:445
  55.6 1.8 %collective-permute-start.4 = (bf16[8,64,256]{2,1,0:T(8,128)(2,1)S(1)}, bf16[8,64,256]{2,1,0:T(8,128)(2,1)S(1)}, u32[]{:S(2)}, u32[]{:S(2)}) collective-permute-start(bf16[8,64,256]{2,1,0:T(8,128)(2,1)S(1)} %all-to-all-done.1.b0), channel_id=1, source_target_pairs={{0,1},{1,0},{2,3},{3,2},{4,5},{5,4},{6,7},{7,6},{8,9},{9,8},{10,11... | collective-permute-start | bytes 786440 | tf_op jit(solution)/shard_map/ppermute | solution.py:441
  57.4 0.0 collective-permute-done.5.b2
  57.4 0.7 collective-permute-start.6
  58.1 0.5 collective-permute-done.4.b1
  58.6 0.7 collective-permute-done.6.b3
  59.3 0.0 copy-done.5
  59.3 0.0 copy-done.6
  59.3 5.9 %attention.1 = bf16[8,48,256]{2,1,0:T(8,128)(2,1)} custom-call(f32[2,16]{1,0:T(2,128)S(1)} %copy-done.6, bf16[8,144,256]{2,1,0:T(8,128)(2,1)S(1)} %all-to-all-done.own_ref, bf16[8,96,256]{2,1,0:T(8,128)(2,1)S(1)} %collective-permute-done.3.far_ref, bf16[8,64,256]{2,1,0:T(8,128)(2,1)S(1)} %all-to-all-done.1.b0, ...), custom_call_target="tpu_custom_call" | custom-call | bytes 1000 | tf_op jit(solution)/shard_map/attention/pallas_call | solution.py:332
  65.2 5.2 %all-to-all-start.2 = ((bf16[8,48,256]{2,1,0:T(8,128)(2,1)}), bf16[8,48,256]{2,1,0:T(8,128)(2,1)S(1)}, u32[]{:S(2)}, u32[]{:S(2)}) async-start(bf16[8,48,256]{2,1,0:T(8,128)(2,1)} %attention.1), calls=%async_computation.2 | async-start | bytes 393216 | tf_op jit(solution)/shard_map/all_to_all | solution.py:509
  70.4 0.0 collective-permute-done.10.b
  70.4 0.0 collective-permute-done.11.c
  70.4 0.0 collective-permute-done.12.d
  70.4 0.0 copy-done.7
  70.4 0.0 copy-done.8
  70.4 0.0 copy-start.2
  70.4 0.1 gated_sum.1
  70.6 0.0 copy-start.1
  70.6 0.0 copy-start.3
  70.6 0.8 collective-permute-start.13
  71.4 2.2 %collective-permute-start.14 = (bf16[128,768]{1,0:T(8,128)(2,1)S(1)}, bf16[128,768]{1,0:T(8,128)(2,1)S(1)}, u32[]{:S(2)}, u32[]{:S(2)}) collective-permute-start(bf16[128,768]{1,0:T(8,128)(2,1)S(1)} %get-tuple-element.60.t0), channel_id=1, source_target_pairs={{0,12},{4,0},{8,4},{12,8},{1,13},{5,1},{9,5},{13,9},{2,14},{6,2},{... | collective-permute-start | bytes 589832 | tf_op jit(solution)/shard_map/ppermute | solution.py:445
  73.6 0.4 collective-permute-start.15
  74.0 0.6 collective-permute-start.16
  74.6 5.2 %all-to-all-done.2.o_ref = bf16[8,48,256]{2,1,0:T(8,128)(2,1)S(1)} async-done(((bf16[8,48,256]{2,1,0:T(8,128)(2,1)}), bf16[8,48,256]{2,1,0:T(8,128)(2,1)S(1)}, u32[]{:S(2)}, u32[]{:S(2)}) %all-to-all-start.2) | async-done | bytes 196640 | tf_op jit(solution)/shard_map/all_to_all | solution.py:509
  79.8 0.0 copy-done.2
  79.9 0.0 copy-start
  79.9 2.3 %collective-permute-start.7 = (bf16[192,512]{1,0:T(8,128)(2,1)S(1)}, bf16[192,512]{1,0:T(8,128)(2,1)S(1)}, u32[]{:S(2)}, u32[]{:S(2)}) collective-permute-start(bf16[192,512]{1,0:T(8,128)(2,1)S(1)} %mix.1.m0), channel_id=1, source_target_pairs={{0,12},{4,0},{8,4},{12,8},{1,13},{5,1},{9,5},{13,9},{2,14},{6,2},{... | collective-permute-start | bytes 589832 | tf_op jit(solution)/shard_map/ppermute | solution.py:445
  82.2 0.0 collective-permute-done.14.t1
  82.2 0.4 collective-permute-start.8
  82.6 0.0 collective-permute-done.15.t2
  82.6 3.5 %collective-permute-start.9 = (bf16[192,512]{1,0:T(8,128)(2,1)S(1)}, bf16[192,512]{1,0:T(8,128)(2,1)S(1)}, u32[]{:S(2)}, u32[]{:S(2)}) collective-permute-start(bf16[192,512]{1,0:T(8,128)(2,1)S(1)} %mix.1.m0), channel_id=1, source_target_pairs={{0,4},{4,8},{8,12},{12,0},{1,5},{5,9},{9,13},{13,1},{2,6},{6,10},{... | collective-permute-start | bytes 589832 | tf_op jit(solution)/shard_map/ppermute | solution.py:445
  86.1 0.1 collective-permute-done.16.t3
  86.2 0.0 collective-permute-done.13.wb
  86.2 0.0 collective-permute-done.7.m1
  86.2 0.0 copy-start.14
  86.2 2.2 %collective-permute-done.8.m2 = bf16[192,512]{1,0:T(8,128)(2,1)S(1)} collective-permute-done((bf16[192,512]{1,0:T(8,128)(2,1)S(1)}, bf16[192,512]{1,0:T(8,128)(2,1)S(1)}, u32[]{:S(2)}, u32[]{:S(2)}) %collective-permute-start.8) | collective-permute-done | bytes 196640 | tf_op jit(solution)/shard_map/ppermute | solution.py:445
  88.3 5.6 %collective-permute-done.9.m3 = bf16[192,512]{1,0:T(8,128)(2,1)S(1)} collective-permute-done((bf16[192,512]{1,0:T(8,128)(2,1)S(1)}, bf16[192,512]{1,0:T(8,128)(2,1)S(1)}, u32[]{:S(2)}, u32[]{:S(2)}) %collective-permute-start.9) | collective-permute-done | bytes 196640 | tf_op jit(solution)/shard_map/ppermute | solution.py:445
  93.9 0.0 copy-done.1
  93.9 0.0 copy-done.3
  93.9 0.0 copy-done
  94.0 0.7 copy-done.16
  94.7 3.6 %finish.1 = bf16[512,768]{1,0:T(8,128)(2,1)} custom-call(bf16[192,512]{1,0:T(8,128)(2,1)} %copy-done, bf16[192,512]{1,0:T(8,128)(2,1)} %copy-done.14, bf16[192,512]{1,0:T(8,128)(2,1)} %copy-done.15, bf16[192,512]{1,0:T(8,128)(2,1)} %copy-done.16, bf16[192,768]{1,0:T(8,128)(2,1)} %w0.1, bf16[3,96,768]{2,1,0:T(8,128)(2,1)} %copy-done.1, ...), custom_call_target="tpu_custom_call" | custom-call | flops 603979776 | bytes 4718592 | tf_op jit(solution)/shard_map/finish/pallas_call | solution.py:419
  (20 shorter events, 0.1 us)
Async XLA Ops:
  5.4 17.5 %copy-start.9 = (bf16[768,2,384]{2,1,0:T(2,128)(2,1)S(1)}, bf16[768,2,384]{2,1,0:T(2,128)(2,1)}, u32[]{:S(2)}) copy-start(bf16[768,2,384]{2,1,0:T(2,128)(2,1)} %param.28) | copy-start | bytes 3538948
  5.4 28.5 %all-to-all-start = ((bf16[8,144,256]{2,1,0:T(8,128)(2,1)}), bf16[8,144,256]{2,1,0:T(8,128)(2,1)S(1)}, u32[]{:S(2)}, u32[]{:S(2)}) async-start(bf16[8,144,256]{2,1,0:T(8,128)(2,1)} %bitcast.21), calls=%async_computation | async-start | bytes 1179648 | tf_op jit(solution)/shard_map/all_to_all | solution.py:486
  17.9 6.3 %collective-permute-start = (bf16[4,32,128]{2,1,0:T(8,128)(2,1)}, bf16[4,32,128]{2,1,0:T(8,128)(2,1)S(1)}, u32[]{:S(2)}, u32[]{:S(2)}) collective-permute-start(bf16[4,32,128]{2,1,0:T(8,128)(2,1)} %get-tuple-element.38), channel_id=1, source_target_pairs={{0,4},{4,8},{8,12},{12,0},{1,5},{5,9},{9,13},{13,1},{2,6},{6,10},{... | collective-permute-start | bytes 98312 | tf_op jit(solution)/shard_map/ppermute | solution.py:445
  19.2 4.9 %collective-permute-start.1 = (bf16[4,32,128]{2,1,0:T(8,128)(2,1)}, bf16[4,32,128]{2,1,0:T(8,128)(2,1)S(1)}, u32[]{:S(2)}, u32[]{:S(2)}) collective-permute-start(bf16[4,32,128]{2,1,0:T(8,128)(2,1)} %get-tuple-element.39), channel_id=1, source_target_pairs={{0,8},{4,12},{8,0},{12,4},{1,9},{5,13},{9,1},{13,5},{2,10},{6,14},... | collective-permute-start | bytes 98312 | tf_op jit(solution)/shard_map/ppermute | solution.py:445
  21.9 3.3 %collective-permute-start.2 = (bf16[4,32,128]{2,1,0:T(8,128)(2,1)}, bf16[4,32,128]{2,1,0:T(8,128)(2,1)S(1)}, u32[]{:S(2)}, u32[]{:S(2)}) collective-permute-start(bf16[4,32,128]{2,1,0:T(8,128)(2,1)} %get-tuple-element.40), channel_id=1, source_target_pairs={{0,12},{4,0},{8,4},{12,8},{1,13},{5,1},{9,5},{13,9},{2,14},{6,2},{... | collective-permute-start | bytes 98312 | tf_op jit(solution)/shard_map/ppermute | solution.py:445
  22.9 2.2 %copy-start.4 = (bf16[4,32,128]{2,1,0:T(8,128)(2,1)S(1)}, bf16[4,32,128]{2,1,0:T(8,128)(2,1)}, u32[]{:S(2)}) copy-start(bf16[4,32,128]{2,1,0:T(8,128)(2,1)} %get-tuple-element.37.t0) | copy-start | bytes 98308
  33.9 15.4 %all-to-all-start.1 = ((bf16[8,64,256]{2,1,0:T(8,128)(2,1)}), bf16[8,64,256]{2,1,0:T(8,128)(2,1)S(1)}, u32[]{:S(2)}, u32[]{:S(2)}) async-start(bf16[8,64,256]{2,1,0:T(8,128)(2,1)} %spread_bias.1), calls=%async_computation.1 | async-start | bytes 524288 | tf_op jit(solution)/shard_map/all_to_all | solution.py:492
  37.4 13.2 %collective-permute-start.3 = (bf16[8,96,256]{2,1,0:T(8,128)(2,1)S(1)}, bf16[8,96,256]{2,1,0:T(8,128)(2,1)S(1)}, u32[]{:S(2)}, u32[]{:S(2)}) collective-permute-start(bf16[8,96,256]{2,1,0:T(8,128)(2,1)S(1)} %slice.3), channel_id=1, source_target_pairs={{0,16},{16,0},{1,17},{17,1},{2,18},{18,2},{3,19},{19,3},{4,20},{20... | collective-permute-start | bytes 1179656 | tf_op jit(solution)/shard_map/ppermute | solution.py:441
  40.2 19.0 %copy-start.5 = (s32[1024]{0:T(1024)S(1)}, s32[1024]{0:T(1024)}, u32[]{:S(2)}) copy-start(s32[1024]{0:T(1024)} %param.19) | copy-start | bytes 12292
  40.2 19.0 %copy-start.6 = (f32[2,16]{1,0:T(2,128)S(1)}, f32[2,16]{1,0:T(2,128)}, u32[]{:S(2)}) copy-start(f32[2,16]{1,0:T(2,128)} %chain_ref.1) | copy-start | bytes 388
  49.4 8.0 %collective-permute-start.5 = (bf16[8,64,256]{2,1,0:T(8,128)(2,1)S(1)}, bf16[8,64,256]{2,1,0:T(8,128)(2,1)S(1)}, u32[]{:S(2)}, u32[]{:S(2)}) collective-permute-start(bf16[8,64,256]{2,1,0:T(8,128)(2,1)S(1)} %all-to-all-done.1.b0), channel_id=1, source_target_pairs={{0,2},{2,0},{1,3},{3,1},{4,6},{6,4},{5,7},{7,5},{8,10},{10,8},{9,1... | collective-permute-start | bytes 786440 | tf_op jit(solution)/shard_map/ppermute | solution.py:441
  50.6 19.8 %collective-permute-start.10 = (bf16[224,768]{1,0:T(8,128)(2,1)}, bf16[224,768]{1,0:T(8,128)(2,1)S(1)}, u32[]{:S(2)}, u32[]{:S(2)}) collective-permute-start(bf16[224,768]{1,0:T(8,128)(2,1)} %get-tuple-element.54), channel_id=1, source_target_pairs={{0,4},{4,8},{8,12},{12,0},{1,5},{5,9},{9,13},{13,1},{2,6},{6,10},{... | collective-permute-start | bytes 1032200 | tf_op jit(solution)/shard_map/ppermute | solution.py:445
  51.9 18.5 %collective-permute-start.11 = (bf16[224,768]{1,0:T(8,128)(2,1)}, bf16[224,768]{1,0:T(8,128)(2,1)S(1)}, u32[]{:S(2)}, u32[]{:S(2)}) collective-permute-start(bf16[224,768]{1,0:T(8,128)(2,1)} %get-tuple-element.55), channel_id=1, source_target_pairs={{0,8},{4,12},{8,0},{12,4},{1,9},{5,13},{9,1},{13,5},{2,10},{6,14},... | collective-permute-start | bytes 1032200 | tf_op jit(solution)/shard_map/ppermute | solution.py:445
  54.5 15.9 %collective-permute-start.12 = (bf16[224,768]{1,0:T(8,128)(2,1)}, bf16[224,768]{1,0:T(8,128)(2,1)S(1)}, u32[]{:S(2)}, u32[]{:S(2)}) collective-permute-start(bf16[224,768]{1,0:T(8,128)(2,1)} %get-tuple-element.56), channel_id=1, source_target_pairs={{0,12},{4,0},{8,4},{12,8},{1,13},{5,1},{9,5},{13,9},{2,14},{6,2},{... | collective-permute-start | bytes 1032200 | tf_op jit(solution)/shard_map/ppermute | solution.py:445
  55.6 3.0 %collective-permute-start.4 = (bf16[8,64,256]{2,1,0:T(8,128)(2,1)S(1)}, bf16[8,64,256]{2,1,0:T(8,128)(2,1)S(1)}, u32[]{:S(2)}, u32[]{:S(2)}) collective-permute-start(bf16[8,64,256]{2,1,0:T(8,128)(2,1)S(1)} %all-to-all-done.1.b0), channel_id=1, source_target_pairs={{0,1},{1,0},{2,3},{3,2},{4,5},{5,4},{6,7},{7,6},{8,9},{9,8},{10,11... | collective-permute-start | bytes 786440 | tf_op jit(solution)/shard_map/ppermute | solution.py:441
  57.4 1.8 %collective-permute-start.6 = (bf16[8,64,256]{2,1,0:T(8,128)(2,1)S(1)}, bf16[8,64,256]{2,1,0:T(8,128)(2,1)S(1)}, u32[]{:S(2)}, u32[]{:S(2)}) collective-permute-start(bf16[8,64,256]{2,1,0:T(8,128)(2,1)S(1)} %collective-permute-done.5.b2), channel_id=1, source_target_pairs={{0,1},{1,0},{2,3},{3,2},{4,5},{5,4},{6,7},{7,6},{8,9},{9,8},{10,11... | collective-permute-start | bytes 786440 | tf_op jit(solution)/shard_map/ppermute | solution.py:441
  59.3 11.1 %copy-start.7 = (f32[128,768]{1,0:T(8,128)S(1)}, f32[128,768]{1,0:T(8,128)}, u32[]{:S(2)}) copy-start(f32[128,768]{1,0:T(8,128)} %get-tuple-element.57.gate_ref) | copy-start | bytes 1179652
  59.3 11.1 %copy-start.8 = (bf16[128,768]{1,0:T(8,128)(2,1)S(1)}, bf16[128,768]{1,0:T(8,128)(2,1)}, u32[]{:S(2)}) copy-start(bf16[128,768]{1,0:T(8,128)(2,1)} %get-tuple-element.53.a) | copy-start | bytes 589828
  65.2 14.6 %all-to-all-start.2 = ((bf16[8,48,256]{2,1,0:T(8,128)(2,1)}), bf16[8,48,256]{2,1,0:T(8,128)(2,1)S(1)}, u32[]{:S(2)}, u32[]{:S(2)}) async-start(bf16[8,48,256]{2,1,0:T(8,128)(2,1)} %attention.1), calls=%async_computation.2 | async-start | bytes 393216 | tf_op jit(solution)/shard_map/all_to_all | solution.py:509
  70.4 9.4 %copy-start.2 = (f32[192,512]{1,0:T(8,128)S(1)}, f32[192,512]{1,0:T(8,128)}, u32[]{:S(2)}) copy-start(f32[192,512]{1,0:T(8,128)} %get-tuple-element.33.gate_ref) | copy-start | bytes 1179652
  70.6 23.4 %copy-start.1 = (bf16[3,96,768]{2,1,0:T(8,128)(2,1)}, bf16[3,96,768]{2,1,0:T(8,128)(2,1)S(1)}, u32[]{:S(2)}) copy-start(bf16[3,96,768]{2,1,0:T(8,128)(2,1)S(1)} %get-tuple-element.58.wa) | copy-start | bytes 1327108
  70.6 23.3 %copy-start.3 = (bf16[128,768]{1,0:T(8,128)(2,1)}, bf16[128,768]{1,0:T(8,128)(2,1)S(1)}, u32[]{:S(2)}) copy-start(bf16[128,768]{1,0:T(8,128)(2,1)S(1)} %get-tuple-element.60.t0) | copy-start | bytes 589828
  70.6 15.6 %collective-permute-start.13 = (bf16[3,96,768]{2,1,0:T(8,128)(2,1)S(1)}, bf16[3,96,768]{2,1,0:T(8,128)(2,1)S(1)}, u32[]{:S(2)}, u32[]{:S(2)}) collective-permute-start(bf16[3,96,768]{2,1,0:T(8,128)(2,1)S(1)} %get-tuple-element.58.wa), channel_id=1, source_target_pairs={{0,1},{1,0},{2,3},{3,2},{4,5},{5,4},{6,7},{7,6},{8,9},{9,8},{10,11... | collective-permute-start | bytes 1327112 | tf_op jit(solution)/shard_map/ppermute | solution.py:441
  71.4 10.8 %collective-permute-start.14 = (bf16[128,768]{1,0:T(8,128)(2,1)S(1)}, bf16[128,768]{1,0:T(8,128)(2,1)S(1)}, u32[]{:S(2)}, u32[]{:S(2)}) collective-permute-start(bf16[128,768]{1,0:T(8,128)(2,1)S(1)} %get-tuple-element.60.t0), channel_id=1, source_target_pairs={{0,12},{4,0},{8,4},{12,8},{1,13},{5,1},{9,5},{13,9},{2,14},{6,2},{... | collective-permute-start | bytes 589832 | tf_op jit(solution)/shard_map/ppermute | solution.py:445
  73.6 9.0 %collective-permute-start.15 = (bf16[128,768]{1,0:T(8,128)(2,1)S(1)}, bf16[128,768]{1,0:T(8,128)(2,1)S(1)}, u32[]{:S(2)}, u32[]{:S(2)}) collective-permute-start(bf16[128,768]{1,0:T(8,128)(2,1)S(1)} %get-tuple-element.60.t0), channel_id=1, source_target_pairs={{0,8},{4,12},{8,0},{12,4},{1,9},{5,13},{9,1},{13,5},{2,10},{6,14},... | collective-permute-start | bytes 589832 | tf_op jit(solution)/shard_map/ppermute | solution.py:445
  74.0 12.1 %collective-permute-start.16 = (bf16[128,768]{1,0:T(8,128)(2,1)S(1)}, bf16[128,768]{1,0:T(8,128)(2,1)S(1)}, u32[]{:S(2)}, u32[]{:S(2)}) collective-permute-start(bf16[128,768]{1,0:T(8,128)(2,1)S(1)} %get-tuple-element.60.t0), channel_id=1, source_target_pairs={{0,4},{4,8},{8,12},{12,0},{1,5},{5,9},{9,13},{13,1},{2,6},{6,10},{... | collective-permute-start | bytes 589832 | tf_op jit(solution)/shard_map/ppermute | solution.py:445
  79.9 14.1 %copy-start = (bf16[192,512]{1,0:T(8,128)(2,1)}, bf16[192,512]{1,0:T(8,128)(2,1)S(1)}, u32[]{:S(2)}) copy-start(bf16[192,512]{1,0:T(8,128)(2,1)S(1)} %mix.1.m0) | copy-start | bytes 589828
  79.9 6.3 %collective-permute-start.7 = (bf16[192,512]{1,0:T(8,128)(2,1)S(1)}, bf16[192,512]{1,0:T(8,128)(2,1)S(1)}, u32[]{:S(2)}, u32[]{:S(2)}) collective-permute-start(bf16[192,512]{1,0:T(8,128)(2,1)S(1)} %mix.1.m0), channel_id=1, source_target_pairs={{0,12},{4,0},{8,4},{12,8},{1,13},{5,1},{9,5},{13,9},{2,14},{6,2},{... | collective-permute-start | bytes 589832 | tf_op jit(solution)/shard_map/ppermute | solution.py:445
  82.2 11.7 %copy-start.11 = (bf16[128,768]{1,0:T(8,128)(2,1)}, bf16[128,768]{1,0:T(8,128)(2,1)S(1)}, u32[]{:S(2)}) copy-start(bf16[128,768]{1,0:T(8,128)(2,1)S(1)} %collective-permute-done.14.t1) | copy-start | bytes 589828
  82.2 6.1 %collective-permute-start.8 = (bf16[192,512]{1,0:T(8,128)(2,1)S(1)}, bf16[192,512]{1,0:T(8,128)(2,1)S(1)}, u32[]{:S(2)}, u32[]{:S(2)}) collective-permute-start(bf16[192,512]{1,0:T(8,128)(2,1)S(1)} %mix.1.m0), channel_id=1, source_target_pairs={{0,8},{4,12},{8,0},{12,4},{1,9},{5,13},{9,1},{13,5},{2,10},{6,14},... | collective-permute-start | bytes 589832 | tf_op jit(solution)/shard_map/ppermute | solution.py:445
  82.6 11.4 %copy-start.12 = (bf16[128,768]{1,0:T(8,128)(2,1)}, bf16[128,768]{1,0:T(8,128)(2,1)S(1)}, u32[]{:S(2)}) copy-start(bf16[128,768]{1,0:T(8,128)(2,1)S(1)} %collective-permute-done.15.t2) | copy-start | bytes 589828
  82.6 11.3 %collective-permute-start.9 = (bf16[192,512]{1,0:T(8,128)(2,1)S(1)}, bf16[192,512]{1,0:T(8,128)(2,1)S(1)}, u32[]{:S(2)}, u32[]{:S(2)}) collective-permute-start(bf16[192,512]{1,0:T(8,128)(2,1)S(1)} %mix.1.m0), channel_id=1, source_target_pairs={{0,4},{4,8},{8,12},{12,0},{1,5},{5,9},{9,13},{13,1},{2,6},{6,10},{... | collective-permute-start | bytes 589832 | tf_op jit(solution)/shard_map/ppermute | solution.py:445
  86.1 7.8 %copy-start.13 = (bf16[128,768]{1,0:T(8,128)(2,1)}, bf16[128,768]{1,0:T(8,128)(2,1)S(1)}, u32[]{:S(2)}) copy-start(bf16[128,768]{1,0:T(8,128)(2,1)S(1)} %collective-permute-done.16.t3) | copy-start | bytes 589828
  86.2 7.8 %copy-start.10 = (bf16[3,96,768]{2,1,0:T(8,128)(2,1)}, bf16[3,96,768]{2,1,0:T(8,128)(2,1)S(1)}, u32[]{:S(2)}) copy-start(bf16[3,96,768]{2,1,0:T(8,128)(2,1)S(1)} %collective-permute-done.13.wb) | copy-start | bytes 1327108
  86.2 7.8 %copy-start.14 = (bf16[192,512]{1,0:T(8,128)(2,1)}, bf16[192,512]{1,0:T(8,128)(2,1)S(1)}, u32[]{:S(2)}) copy-start(bf16[192,512]{1,0:T(8,128)(2,1)S(1)} %collective-permute-done.7.m1) | copy-start | bytes 589828
  88.3 5.7 %copy-start.15 = (bf16[192,512]{1,0:T(8,128)(2,1)}, bf16[192,512]{1,0:T(8,128)(2,1)S(1)}, u32[]{:S(2)}) copy-start(bf16[192,512]{1,0:T(8,128)(2,1)S(1)} %collective-permute-done.8.m2) | copy-start | bytes 589828
  94.0 0.7 copy-start.16

commit v4 on v3

--- a/solution.py
+++ b/solution.py
@@ -183,7 +183,7 @@
 
 def transition_kernel(
     act_ref, cn_ref, scale_ref, shift_ref, og_ref, win_ref, wout_ref, last_ref,
-    p0, p1, p2, p3, g0_ref, g1_ref, part_ref,
+    p0, p1, p2, p3, g1_ref, part_ref,
 ):
     mine = lax.axis_index("col")
     cond_norm = cn_ref[...]
@@ -202,9 +202,8 @@
         ref[:quarter] = part_ref[pl.ds(start, quarter), :]
         if shift:
             ref[quarter:] = last_ref[half_rows(last_ref.shape[0]), :]
-    g0_ref[...] = jax.nn.sigmoid(dot(cond_norm, og_ref[0]))
     own = cn_ref[pl.ds(pl.multiple_of(mine * quarter, quarter), quarter), :]
-    g1_ref[...] = jax.nn.sigmoid(dot(own, og_ref[1]))
+    g1_ref[...] = jax.nn.sigmoid(dot(own, og_ref[0]))
 
 
 def transition(act, cond_norm, scale, shift, out_gate, w_in, w_out, last):
@@ -221,18 +220,17 @@
             whole(cond_norm.shape),
             second,
             second,
-            whole(out_gate.shape),
+            second,
             whole(w_in.shape),
             whole(w_out.shape),
             whole(last.shape),
         ],
         out_specs=[whole((quarter, width))]
         + [whole(both)] * 3
-        + [whole((rows, width)), whole((quarter, width))],
+        + [whole((quarter, width))],
         out_shape=[jax.ShapeDtypeStruct((quarter, width), BF)]
         + [jax.ShapeDtypeStruct(both, BF)] * 3
         + [
-            jax.ShapeDtypeStruct((rows, width), F32),
             jax.ShapeDtypeStruct((quarter, width), F32),
         ],
         scratch_shapes=[pltpu.VMEM((rows, width), BF)],
@@ -380,32 +378,35 @@
 
 
 def finish_kernel(
-    m0, m1, m2, m3, w0, wa, wb, g0_hbm, t0, t1, t2, t3, out_hbm,
-    m_ref, w_ref, g0_ref, t_ref, total_ref, out_ref, in_sems, out_sems,
+    m0, m1, m2, m3, w0, wa, wb, cn_hbm, og_hbm, t0, t1, t2, t3, out_hbm,
+    m_ref, w_ref, cn_ref, og_ref, t_ref, total_ref, out_ref, in_sems, out_sems,
 ):
     mine = lax.axis_index("col")
     depth = w_ref.shape[1]
     copies = fetch(
         [
+            (cn_hbm, cn_ref),
+            (og_hbm.at[0], og_ref),
             *[(source, m_ref.at[i]) for i, source in enumerate((m0, m1, m2, m3))],
             (w0, w_ref.at[0]),
             *[(wa.at[i], w_ref.at[i + 1, half_rows(depth)]) for i in range(3)],
             *[(wb.at[i], w_ref.at[i + 1, half_rows(depth, 1)]) for i in range(3)],
-            (g0_hbm, g0_ref),
             *[(source, t_ref.at[i]) for i, source in enumerate((t0, t1, t2, t3))],
         ],
         in_sems,
     )
-    for i in range(11):
+    copies[0].wait()
+    copies[1].wait()
+    total_ref[...] = jax.nn.sigmoid(dot(cn_ref[...], og_ref[...]))
+    for i in range(2, 13):
         copies[i].wait()
     mixed = m_ref[...].reshape(-1, m_ref.shape[2])
     total = dot(mixed, w_ref[...].reshape(-1, w_ref.shape[2]), TN)
-    copies[11].wait()
-    total_ref[...] = g0_ref[...] * total
+    total_ref[...] = total_ref[...] * total
     quarter = t_ref.shape[1]
     outs = []
     for shift in range(4):
-        copies[12 + shift].wait()
+        copies[13 + shift].wait()
         rows = pl.ds(pl.multiple_of(lax.rem(mine + shift, 4) * quarter, quarter), quarter)
         out_ref[shift] = (total_ref[rows, :] + t_ref[shift].astype(F32)).astype(BF)
         outs.append(pltpu.make_async_copy(out_ref.at[shift], out_hbm.at[rows], out_sems.at[shift]))
@@ -414,27 +415,29 @@
         copy.wait()
 
 
-def finish(mixed, w, g0, trans):
-    rows, width = g0.shape
+def finish(mixed, w, cond_norm, out_gate, trans):
+    rows, cwidth = cond_norm.shape
+    width = out_gate.shape[2]
     return pl.pallas_call(
         finish_kernel,
-        in_specs=[ANY] * 12,
+        in_specs=[ANY] * 13,
         out_specs=ANY,
         out_shape=jax.ShapeDtypeStruct((rows, width), BF),
         scratch_shapes=[
             pltpu.VMEM((4, *mixed[0].shape), BF),
             pltpu.VMEM((4, *w[0].shape), BF),
-            pltpu.VMEM((rows, width), F32),
+            pltpu.VMEM((rows, cwidth), BF),
+            pltpu.VMEM((cwidth, width), BF),
             pltpu.VMEM((4, rows // 4, width), BF),
             pltpu.VMEM((rows, width), F32),
             pltpu.VMEM((4, rows // 4, width), BF),
-            pltpu.SemaphoreType.DMA((16,)),
+            pltpu.SemaphoreType.DMA((17,)),
             pltpu.SemaphoreType.DMA((4,)),
         ],
         compiler_params=params(),
         cost_estimate=cost(2 * rows * width * width, rows * width * 12),
         name="finish",
-    )(*mixed, *w, g0, *trans)
+    )(*mixed, *w, cond_norm, out_gate, *trans)
 
 
 def swap(x, axis):
@@ -491,13 +494,12 @@
     own, spread, act, win = tie(own, spread, act, win)
     bias0 = lax.all_to_all(spread, "z", 0, 0, tiled=True)
     far = swap(own[:, HD:], "xh")
-    *parts, g0, g1 = transition(
+    *parts, g1 = transition(
         act, cond_norm, ada_scale, ada_shift, out_gate, win, trans_out, attn_out
     )
-    bias0, g0 = tie(bias0, g0)
-    far, *parts = tie(far, *parts)
+    bias0, g1 = tie(bias0, g1)
     parts = scatter(parts)
-    bias2 = swap(bias0, "xlo")
+    bias2, far = tie(swap(bias0, "xlo"), far)
     bias1 = swap(bias0, "core")
     bias3 = swap(bias2, "core")
     quarter, pack = gated_sum(parts, g1)
@@ -507,7 +509,7 @@
         chain_bias, own, far, (bias0, bias1, bias2, bias3), chain_ids.reshape(8, 2 * rows)
     )
     attended = lax.all_to_all(attended, "z", 0, 0, tiled=True)
-    updated = finish(around(mix(gates, attended)), w_out_all, g0, trans)
+    updated = finish(around(mix(gates, attended)), w_out_all, cond_norm, out_gate, trans)
     return updated.reshape(samples, rows, width)
 
 

time: 98.9 us -> 99.3 us (level)
    all_to_all x1, waiting for transfers between devices: 1.95 us -> 3.17 us  [body(): bias0 = lax.all_to_all(spread, 'z', 0, 0, tiled=True)]
    pallas_call x1, Pallas kernels: 7.2 us -> 5.99 us  [transition(): pl.pallas_call(transition_kernel, grid=(1,), in_specs=[whole(act.shape),...]
  transfers between devices with their start and end apart: 20 -> 20, of which waited for: 9 -> 9; matrix products, arithmetic and copies ran while one was open for 1% -> 1% of each run, Pallas kernels for 18% -> 16%
where the time goes in v4:
time: 99.3 us; the launch traced here: 98.9 us
  starting transfers between devices  45 us (45%)
  waiting for transfers between devices  25.8 us (26%)
  Pallas kernels  25.7 us (26%)
  local copies, waits for them, and re-layouts  2.03 us (2%)
    ppermute x12, starting transfers between devices, send(): return lax.ppermute(x, 'col', [(i, (i + k) % 4) for i in range(4)])  20 us
    all_to_all x1, starting transfers between devices, body(): lax.all_to_all(qkv.reshape(8, 3 * HD, 4 * rows), 'z', 0, 0, tiled=True)  9.14 us
    ppermute x12, waiting for transfers between devices, send(): return lax.ppermute(x, 'col', [(i, (i + k) % 4) for i in range(4)])  8.76 us
    all_to_all x1, waiting for transfers between devices, body(): lax.all_to_all(qkv.reshape(8, 3 * HD, 4 * rows), 'z', 0, 0, tiled=True)  8.02 us
    ppermute x5, starting transfers between devices, swap(): return lax.ppermute(x, axis, [(0, 1), (1, 0)])  7.83 us
    pallas_call x1, Pallas kernels, transition(): pl.pallas_call(transition_kernel, grid=(1,), in_specs=[whole(act.shape),...  5.99 us
    pallas_call x1, Pallas kernels, attention(): pl.pallas_call(attention_kernel, grid=(count // blocks,), in_specs=[pl.Bl...  5.92 us
    pallas_call x1, Pallas kernels, project(): pl.pallas_call(project_kernel, grid=(rows // step,), in_specs=[pl.BlockSp...  5.46 us
  transfers between devices with their start and end apart: 20, of which 9 were waited for; matrix products, arithmetic and copies ran while one was open for 1% of the time, Pallas kernels for 16%

profile of v4, /device:TPU:1, one launch (start us, length us, event | category | flops | bytes accessed | tf_op | source)
XLA Modules:
  0.0 98.9 jit_solution(6384318280338427593)
XLA Ops:
  0.0 5.5 %project.1 = (bf16[4,2,144,256]{3,2,1,0:T(8,128)(2,1)}, f32[192,512]{1,0:T(8,128)}, bf16[512,384]{1,0:T(8,128)(2,1)}) custom-call(bf16[512,768]{1,0:T(8,128)(2,1)} %bitcast.16, bf16[512,384]{1,0:T(8,128)(2,1)} %bitcast.22, f32[3,128]{1,0:T(4,128)} %bitcast.24, bf16[2,384,768]{2,1,0:T(8,128)(2,1)} %scale_ref.3, bf16[2,384,768]{2,1,0:T(8,128)(2,1)} %shift_ref.3, ...), custom_call_target="tpu_custom_call" | custom-call | flops 1207959552 | bytes 2359296 | tf_op jit(solution)/shard_map/project/pallas_call | solution.py:150
  5.5 9.1 %all-to-all-start = ((bf16[8,144,256]{2,1,0:T(8,128)(2,1)}), bf16[8,144,256]{2,1,0:T(8,128)(2,1)S(1)}, u32[]{:S(2)}, u32[]{:S(2)}) async-start(bf16[8,144,256]{2,1,0:T(8,128)(2,1)} %bitcast.21), calls=%async_computation | async-start | bytes 1179648 | tf_op jit(solution)/shard_map/all_to_all | solution.py:489
  14.6 3.3 %tile_bias.1 = (bf16[4,32,128]{2,1,0:T(8,128)(2,1)}, bf16[4,32,128]{2,1,0:T(8,128)(2,1)}, bf16[4,32,128]{2,1,0:T(8,128)(2,1)}, bf16[4,32,128]{2,1,0:T(8,128)(2,1)}) custom-call(bf16[2,32,64,128]{3,2,1,0:T(8,128)(2,1)} %bitcast.20, f32[1,128]{1,0:T(1,128)} %bitcast.25, bf16[4,4,128]{2,1,0:T(4,128)(2,1)} %bitcast.23), custom_call_target="tpu_custom_call" | custom-call | bytes 500000 | tf_op jit(solution)/shard_map/tile_bias/pallas_call | solution.py:78
  17.9 1.4 %collective-permute-start = (bf16[4,32,128]{2,1,0:T(8,128)(2,1)}, bf16[4,32,128]{2,1,0:T(8,128)(2,1)S(1)}, u32[]{:S(2)}, u32[]{:S(2)}) collective-permute-start(bf16[4,32,128]{2,1,0:T(8,128)(2,1)} %get-tuple-element.34), channel_id=1, source_target_pairs={{0,4},{4,8},{8,12},{12,0},{1,5},{5,9},{9,13},{13,1},{2,6},{6,10},{... | collective-permute-start | bytes 98312 | tf_op jit(solution)/shard_map/ppermute | solution.py:448
  19.3 2.6 %collective-permute-start.1 = (bf16[4,32,128]{2,1,0:T(8,128)(2,1)}, bf16[4,32,128]{2,1,0:T(8,128)(2,1)S(1)}, u32[]{:S(2)}, u32[]{:S(2)}) collective-permute-start(bf16[4,32,128]{2,1,0:T(8,128)(2,1)} %get-tuple-element.35), channel_id=1, source_target_pairs={{0,8},{4,12},{8,0},{12,4},{1,9},{5,13},{9,1},{13,5},{2,10},{6,14},... | collective-permute-start | bytes 98312 | tf_op jit(solution)/shard_map/ppermute | solution.py:448
  21.9 1.1 %collective-permute-start.2 = (bf16[4,32,128]{2,1,0:T(8,128)(2,1)}, bf16[4,32,128]{2,1,0:T(8,128)(2,1)S(1)}, u32[]{:S(2)}, u32[]{:S(2)}) collective-permute-start(bf16[4,32,128]{2,1,0:T(8,128)(2,1)} %get-tuple-element.36), channel_id=1, source_target_pairs={{0,12},{4,0},{8,4},{12,8},{1,13},{5,1},{9,5},{13,9},{2,14},{6,2},{... | collective-permute-start | bytes 98312 | tf_op jit(solution)/shard_map/ppermute | solution.py:448
  22.9 0.0 copy-done.9
  22.9 1.3 %copy.16 = bf16[96,8,2,384]{3,1,2,0:T(8,128)(2,1)} copy(bf16[96,8,2,384]{3,2,1,0:T(2,128)(2,1)S(1)} %bitcast.18) | data formatting | bytes 2359296
  24.2 0.0 collective-permute-done.t1
  24.2 0.0 collective-permute-done.1.t2
  24.2 0.9 collective-permute-done.2.t3
  25.1 0.0 copy-done.4
  25.1 0.8 spread_bias.1
  25.9 8.0 %all-to-all-done.own_ref = bf16[8,144,256]{2,1,0:T(8,128)(2,1)S(1)} async-done(((bf16[8,144,256]{2,1,0:T(8,128)(2,1)}), bf16[8,144,256]{2,1,0:T(8,128)(2,1)S(1)}, u32[]{:S(2)}, u32[]{:S(2)}) %all-to-all-start) | async-done | bytes 589856 | tf_op jit(solution)/shard_map/all_to_all | solution.py:489
  34.0 3.4 %all-to-all-start.1 = ((bf16[8,64,256]{2,1,0:T(8,128)(2,1)}), bf16[8,64,256]{2,1,0:T(8,128)(2,1)S(1)}, u32[]{:S(2)}, u32[]{:S(2)}) async-start(bf16[8,64,256]{2,1,0:T(8,128)(2,1)} %spread_bias.1), calls=%async_computation.1 | async-start | bytes 524288 | tf_op jit(solution)/shard_map/all_to_all | solution.py:495
  37.4 2.8 %collective-permute-start.4 = (bf16[8,96,256]{2,1,0:T(8,128)(2,1)S(1)}, bf16[8,96,256]{2,1,0:T(8,128)(2,1)S(1)}, u32[]{:S(2)}, u32[]{:S(2)}) collective-permute-start(bf16[8,96,256]{2,1,0:T(8,128)(2,1)S(1)} %slice.3), channel_id=1, source_target_pairs={{0,16},{16,0},{1,17},{17,1},{2,18},{18,2},{3,19},{19,3},{4,20},{20... | collective-permute-start | bytes 1179656 | tf_op jit(solution)/shard_map/ppermute | solution.py:444
  40.3 6.0 %transition.1 = (bf16[128,768]{1,0:T(8,128)(2,1)}, bf16[224,768]{1,0:T(8,128)(2,1)}, bf16[224,768]{1,0:T(8,128)(2,1)}, bf16[224,768]{1,0:T(8,128)(2,1)}, f32[128,768]{1,0:T(8,128)}) custom-call(bf16[512,768]{1,0:T(8,128)(2,1)} %bitcast.17, bf16[512,384]{1,0:T(8,128)(2,1)} %get-tuple-element.40.cn_ref.cn_hbm, bf16[2,384,768]{2,1,0:T(8,128)(2,1)} %scale_ref.3, ...), custom_call_target="tpu_custom_call" | custom-call | bytes 2000000 | tf_op jit(solution)/shard_map/transition/pallas_call | solution.py:215
  46.2 3.2 %all-to-all-done.1.b0 = bf16[8,64,256]{2,1,0:T(8,128)(2,1)S(1)} async-done(((bf16[8,64,256]{2,1,0:T(8,128)(2,1)}), bf16[8,64,256]{2,1,0:T(8,128)(2,1)S(1)}, u32[]{:S(2)}, u32[]{:S(2)}) %all-to-all-start.1) | async-done | bytes 262176 | tf_op jit(solution)/shard_map/all_to_all | solution.py:495
  49.4 1.2 %collective-permute-start.3 = (bf16[8,64,256]{2,1,0:T(8,128)(2,1)S(1)}, bf16[8,64,256]{2,1,0:T(8,128)(2,1)S(1)}, u32[]{:S(2)}, u32[]{:S(2)}) collective-permute-start(bf16[8,64,256]{2,1,0:T(8,128)(2,1)S(1)} %all-to-all-done.1.b0), channel_id=1, source_target_pairs={{0,2},{2,0},{1,3},{3,1},{4,6},{6,4},{5,7},{7,5},{8,10},{10,8},{9,1... | collective-permute-start | bytes 786440 | tf_op jit(solution)/shard_map/ppermute | solution.py:444
  50.6 1.3 %collective-permute-start.10 = (bf16[224,768]{1,0:T(8,128)(2,1)}, bf16[224,768]{1,0:T(8,128)(2,1)S(1)}, u32[]{:S(2)}, u32[]{:S(2)}) collective-permute-start(bf16[224,768]{1,0:T(8,128)(2,1)} %get-tuple-element.47), channel_id=1, source_target_pairs={{0,4},{4,8},{8,12},{12,0},{1,5},{5,9},{9,13},{13,1},{2,6},{6,10},{... | collective-permute-start | bytes 1032200 | tf_op jit(solution)/shard_map/ppermute | solution.py:448
  51.9 2.6 %collective-permute-start.11 = (bf16[224,768]{1,0:T(8,128)(2,1)}, bf16[224,768]{1,0:T(8,128)(2,1)S(1)}, u32[]{:S(2)}, u32[]{:S(2)}) collective-permute-start(bf16[224,768]{1,0:T(8,128)(2,1)} %get-tuple-element.48), channel_id=1, source_target_pairs={{0,8},{4,12},{8,0},{12,4},{1,9},{5,13},{9,1},{13,5},{2,10},{6,14},... | collective-permute-start | bytes 1032200 | tf_op jit(solution)/shard_map/ppermute | solution.py:448
  54.5 1.1 %collective-permute-start.12 = (bf16[224,768]{1,0:T(8,128)(2,1)}, bf16[224,768]{1,0:T(8,128)(2,1)S(1)}, u32[]{:S(2)}, u32[]{:S(2)}) collective-permute-start(bf16[224,768]{1,0:T(8,128)(2,1)} %get-tuple-element.49), channel_id=1, source_target_pairs={{0,12},{4,0},{8,4},{12,8},{1,13},{5,1},{9,5},{13,9},{2,14},{6,2},{... | collective-permute-start | bytes 1032200 | tf_op jit(solution)/shard_map/ppermute | solution.py:448
  55.6 0.0 collective-permute-done.4.far_ref
  55.6 1.8 %collective-permute-start.5 = (bf16[8,64,256]{2,1,0:T(8,128)(2,1)S(1)}, bf16[8,64,256]{2,1,0:T(8,128)(2,1)S(1)}, u32[]{:S(2)}, u32[]{:S(2)}) collective-permute-start(bf16[8,64,256]{2,1,0:T(8,128)(2,1)S(1)} %all-to-all-done.1.b0), channel_id=1, source_target_pairs={{0,1},{1,0},{2,3},{3,2},{4,5},{5,4},{6,7},{7,6},{8,9},{9,8},{10,11... | collective-permute-start | bytes 786440 | tf_op jit(solution)/shard_map/ppermute | solution.py:444
  57.4 0.0 collective-permute-done.3.b2
  57.5 0.7 collective-permute-start.6
  58.1 0.5 collective-permute-done.5.b1
  58.6 0.7 collective-permute-done.6.b3
  59.3 0.0 copy-done.5
  59.3 0.0 copy-done.6
  59.3 5.9 %attention.1 = bf16[8,48,256]{2,1,0:T(8,128)(2,1)} custom-call(f32[2,16]{1,0:T(2,128)S(1)} %copy-done.6, bf16[8,144,256]{2,1,0:T(8,128)(2,1)S(1)} %all-to-all-done.own_ref, bf16[8,96,256]{2,1,0:T(8,128)(2,1)S(1)} %collective-permute-done.4.far_ref, bf16[8,64,256]{2,1,0:T(8,128)(2,1)S(1)} %all-to-all-done.1.b0, ...), custom_call_target="tpu_custom_call" | custom-call | bytes 1000 | tf_op jit(solution)/shard_map/attention/pallas_call | solution.py:330
  65.2 4.7 %all-to-all-start.2 = ((bf16[8,48,256]{2,1,0:T(8,128)(2,1)}), bf16[8,48,256]{2,1,0:T(8,128)(2,1)S(1)}, u32[]{:S(2)}, u32[]{:S(2)}) async-start(bf16[8,48,256]{2,1,0:T(8,128)(2,1)} %attention.1), calls=%async_computation.2 | async-start | bytes 393216 | tf_op jit(solution)/shard_map/all_to_all | solution.py:511
  69.9 0.0 collective-permute-done.10.b
  69.9 0.0 collective-permute-done.11.c
  69.9 0.0 collective-permute-done.12.d
  69.9 0.0 copy-done.7
  69.9 0.0 copy-done.8
  70.0 0.0 copy-start.2
  70.0 0.1 gated_sum.1
  70.1 0.0 copy-start.1
  70.1 0.0 copy-start.3
  70.1 1.3 %collective-permute-start.13 = (bf16[3,96,768]{2,1,0:T(8,128)(2,1)S(1)}, bf16[3,96,768]{2,1,0:T(8,128)(2,1)S(1)}, u32[]{:S(2)}, u32[]{:S(2)}) collective-permute-start(bf16[3,96,768]{2,1,0:T(8,128)(2,1)S(1)} %get-tuple-element.51.wa), channel_id=1, source_target_pairs={{0,1},{1,0},{2,3},{3,2},{4,5},{5,4},{6,7},{7,6},{8,9},{9,8},{10,11... | collective-permute-start | bytes 1327112 | tf_op jit(solution)/shard_map/ppermute | solution.py:444
  71.4 2.2 %collective-permute-start.14 = (bf16[128,768]{1,0:T(8,128)(2,1)S(1)}, bf16[128,768]{1,0:T(8,128)(2,1)S(1)}, u32[]{:S(2)}, u32[]{:S(2)}) collective-permute-start(bf16[128,768]{1,0:T(8,128)(2,1)S(1)} %get-tuple-element.52.t0), channel_id=1, source_target_pairs={{0,12},{4,0},{8,4},{12,8},{1,13},{5,1},{9,5},{13,9},{2,14},{6,2},{... | collective-permute-start | bytes 589832 | tf_op jit(solution)/shard_map/ppermute | solution.py:448
  73.6 0.4 collective-permute-start.15
  74.1 0.6 collective-permute-start.16
  74.7 4.7 %all-to-all-done.2.o_ref = bf16[8,48,256]{2,1,0:T(8,128)(2,1)S(1)} async-done(((bf16[8,48,256]{2,1,0:T(8,128)(2,1)}), bf16[8,48,256]{2,1,0:T(8,128)(2,1)S(1)}, u32[]{:S(2)}, u32[]{:S(2)}) %all-to-all-start.2) | async-done | bytes 196640 | tf_op jit(solution)/shard_map/all_to_all | solution.py:511
  79.3 0.0 copy-done.2
  79.4 0.0 copy-start
  79.4 2.8 %collective-permute-start.7 = (bf16[192,512]{1,0:T(8,128)(2,1)S(1)}, bf16[192,512]{1,0:T(8,128)(2,1)S(1)}, u32[]{:S(2)}, u32[]{:S(2)}) collective-permute-start(bf16[192,512]{1,0:T(8,128)(2,1)S(1)} %mix.1.m0), channel_id=1, source_target_pairs={{0,12},{4,0},{8,4},{12,8},{1,13},{5,1},{9,5},{13,9},{2,14},{6,2},{... | collective-permute-start | bytes 589832 | tf_op jit(solution)/shard_map/ppermute | solution.py:448
  82.2 0.0 collective-permute-done.14.t1
  82.2 0.3 collective-permute-start.8
  82.5 0.0 collective-permute-done.15.t2
  82.5 3.5 %collective-permute-start.9 = (bf16[192,512]{1,0:T(8,128)(2,1)S(1)}, bf16[192,512]{1,0:T(8,128)(2,1)S(1)}, u32[]{:S(2)}, u32[]{:S(2)}) collective-permute-start(bf16[192,512]{1,0:T(8,128)(2,1)S(1)} %mix.1.m0), channel_id=1, source_target_pairs={{0,4},{4,8},{8,12},{12,0},{1,5},{5,9},{9,13},{13,1},{2,6},{6,10},{... | collective-permute-start | bytes 589832 | tf_op jit(solution)/shard_map/ppermute | solution.py:448
  86.1 0.1 collective-permute-done.16.t3
  86.2 0.0 collective-permute-done.13.wb
  86.2 0.0 collective-permute-done.7.m1
  86.2 0.0 copy-start.14
  86.2 2.1 %collective-permute-done.8.m2 = bf16[192,512]{1,0:T(8,128)(2,1)S(1)} collective-permute-done((bf16[192,512]{1,0:T(8,128)(2,1)S(1)}, bf16[192,512]{1,0:T(8,128)(2,1)S(1)}, u32[]{:S(2)}, u32[]{:S(2)}) %collective-permute-start.8) | collective-permute-done | bytes 196640 | tf_op jit(solution)/shard_map/ppermute | solution.py:448
  88.3 5.6 %collective-permute-done.9.m3 = bf16[192,512]{1,0:T(8,128)(2,1)S(1)} collective-permute-done((bf16[192,512]{1,0:T(8,128)(2,1)S(1)}, bf16[192,512]{1,0:T(8,128)(2,1)S(1)}, u32[]{:S(2)}, u32[]{:S(2)}) %collective-permute-start.9) | collective-permute-done | bytes 196640 | tf_op jit(solution)/shard_map/ppermute | solution.py:448
  93.9 0.0 copy-done.1
  93.9 0.0 copy-done.3
  93.9 0.0 copy-done
  94.0 0.7 copy-done.16
  94.7 4.1 %finish.1 = bf16[512,768]{1,0:T(8,128)(2,1)} custom-call(bf16[192,512]{1,0:T(8,128)(2,1)} %copy-done, bf16[192,512]{1,0:T(8,128)(2,1)} %copy-done.14, bf16[192,512]{1,0:T(8,128)(2,1)} %copy-done.15, bf16[192,512]{1,0:T(8,128)(2,1)} %copy-done.16, bf16[192,768]{1,0:T(8,128)(2,1)} %w0.1, bf16[3,96,768]{2,1,0:T(8,128)(2,1)} %copy-done.1, ...), custom_call_target="tpu_custom_call" | custom-call | flops 603979776 | bytes 4718592 | tf_op jit(solution)/shard_map/finish/pallas_call | solution.py:421
  (20 shorter events, 0.1 us)
Async XLA Ops:
  5.5 17.5 %copy-start.9 = (bf16[768,2,384]{2,1,0:T(2,128)(2,1)S(1)}, bf16[768,2,384]{2,1,0:T(2,128)(2,1)}, u32[]{:S(2)}) copy-start(bf16[768,2,384]{2,1,0:T(2,128)(2,1)} %param.28) | copy-start | bytes 3538948
  5.5 28.5 %all-to-all-start = ((bf16[8,144,256]{2,1,0:T(8,128)(2,1)}), bf16[8,144,256]{2,1,0:T(8,128)(2,1)S(1)}, u32[]{:S(2)}, u32[]{:S(2)}) async-start(bf16[8,144,256]{2,1,0:T(8,128)(2,1)} %bitcast.21), calls=%async_computation | async-start | bytes 1179648 | tf_op jit(solution)/shard_map/all_to_all | solution.py:489
  17.9 6.3 %collective-permute-start = (bf16[4,32,128]{2,1,0:T(8,128)(2,1)}, bf16[4,32,128]{2,1,0:T(8,128)(2,1)S(1)}, u32[]{:S(2)}, u32[]{:S(2)}) collective-permute-start(bf16[4,32,128]{2,1,0:T(8,128)(2,1)} %get-tuple-element.34), channel_id=1, source_target_pairs={{0,4},{4,8},{8,12},{12,0},{1,5},{5,9},{9,13},{13,1},{2,6},{6,10},{... | collective-permute-start | bytes 98312 | tf_op jit(solution)/shard_map/ppermute | solution.py:448
  19.3 5.0 %collective-permute-start.1 = (bf16[4,32,128]{2,1,0:T(8,128)(2,1)}, bf16[4,32,128]{2,1,0:T(8,128)(2,1)S(1)}, u32[]{:S(2)}, u32[]{:S(2)}) collective-permute-start(bf16[4,32,128]{2,1,0:T(8,128)(2,1)} %get-tuple-element.35), channel_id=1, source_target_pairs={{0,8},{4,12},{8,0},{12,4},{1,9},{5,13},{9,1},{13,5},{2,10},{6,14},... | collective-permute-start | bytes 98312 | tf_op jit(solution)/shard_map/ppermute | solution.py:448
  21.9 3.3 %collective-permute-start.2 = (bf16[4,32,128]{2,1,0:T(8,128)(2,1)}, bf16[4,32,128]{2,1,0:T(8,128)(2,1)S(1)}, u32[]{:S(2)}, u32[]{:S(2)}) collective-permute-start(bf16[4,32,128]{2,1,0:T(8,128)(2,1)} %get-tuple-element.36), channel_id=1, source_target_pairs={{0,12},{4,0},{8,4},{12,8},{1,13},{5,1},{9,5},{13,9},{2,14},{6,2},{... | collective-permute-start | bytes 98312 | tf_op jit(solution)/shard_map/ppermute | solution.py:448
  22.9 2.2 %copy-start.4 = (bf16[4,32,128]{2,1,0:T(8,128)(2,1)S(1)}, bf16[4,32,128]{2,1,0:T(8,128)(2,1)}, u32[]{:S(2)}) copy-start(bf16[4,32,128]{2,1,0:T(8,128)(2,1)} %get-tuple-element.33.t0) | copy-start | bytes 98308
  34.0 15.4 %all-to-all-start.1 = ((bf16[8,64,256]{2,1,0:T(8,128)(2,1)}), bf16[8,64,256]{2,1,0:T(8,128)(2,1)S(1)}, u32[]{:S(2)}, u32[]{:S(2)}) async-start(bf16[8,64,256]{2,1,0:T(8,128)(2,1)} %spread_bias.1), calls=%async_computation.1 | async-start | bytes 524288 | tf_op jit(solution)/shard_map/all_to_all | solution.py:495
  37.4 18.2 %collective-permute-start.4 = (bf16[8,96,256]{2,1,0:T(8,128)(2,1)S(1)}, bf16[8,96,256]{2,1,0:T(8,128)(2,1)S(1)}, u32[]{:S(2)}, u32[]{:S(2)}) collective-permute-start(bf16[8,96,256]{2,1,0:T(8,128)(2,1)S(1)} %slice.3), channel_id=1, source_target_pairs={{0,16},{16,0},{1,17},{17,1},{2,18},{18,2},{3,19},{19,3},{4,20},{20... | collective-permute-start | bytes 1179656 | tf_op jit(solution)/shard_map/ppermute | solution.py:444
  40.2 19.0 %copy-start.5 = (s32[1024]{0:T(1024)S(1)}, s32[1024]{0:T(1024)}, u32[]{:S(2)}) copy-start(s32[1024]{0:T(1024)} %param.19) | copy-start | bytes 12292
  40.3 19.0 %copy-start.6 = (f32[2,16]{1,0:T(2,128)S(1)}, f32[2,16]{1,0:T(2,128)}, u32[]{:S(2)}) copy-start(f32[2,16]{1,0:T(2,128)} %chain_ref.1) | copy-start | bytes 388
  49.4 8.0 %collective-permute-start.3 = (bf16[8,64,256]{2,1,0:T(8,128)(2,1)S(1)}, bf16[8,64,256]{2,1,0:T(8,128)(2,1)S(1)}, u32[]{:S(2)}, u32[]{:S(2)}) collective-permute-start(bf16[8,64,256]{2,1,0:T(8,128)(2,1)S(1)} %all-to-all-done.1.b0), channel_id=1, source_target_pairs={{0,2},{2,0},{1,3},{3,1},{4,6},{6,4},{5,7},{7,5},{8,10},{10,8},{9,1... | collective-permute-start | bytes 786440 | tf_op jit(solution)/shard_map/ppermute | solution.py:444
  50.6 19.3 %collective-permute-start.10 = (bf16[224,768]{1,0:T(8,128)(2,1)}, bf16[224,768]{1,0:T(8,128)(2,1)S(1)}, u32[]{:S(2)}, u32[]{:S(2)}) collective-permute-start(bf16[224,768]{1,0:T(8,128)(2,1)} %get-tuple-element.47), channel_id=1, source_target_pairs={{0,4},{4,8},{8,12},{12,0},{1,5},{5,9},{9,13},{13,1},{2,6},{6,10},{... | collective-permute-start | bytes 1032200 | tf_op jit(solution)/shard_map/ppermute | solution.py:448
  51.9 18.0 %collective-permute-start.11 = (bf16[224,768]{1,0:T(8,128)(2,1)}, bf16[224,768]{1,0:T(8,128)(2,1)S(1)}, u32[]{:S(2)}, u32[]{:S(2)}) collective-permute-start(bf16[224,768]{1,0:T(8,128)(2,1)} %get-tuple-element.48), channel_id=1, source_target_pairs={{0,8},{4,12},{8,0},{12,4},{1,9},{5,13},{9,1},{13,5},{2,10},{6,14},... | collective-permute-start | bytes 1032200 | tf_op jit(solution)/shard_map/ppermute | solution.py:448
  54.5 15.4 %collective-permute-start.12 = (bf16[224,768]{1,0:T(8,128)(2,1)}, bf16[224,768]{1,0:T(8,128)(2,1)S(1)}, u32[]{:S(2)}, u32[]{:S(2)}) collective-permute-start(bf16[224,768]{1,0:T(8,128)(2,1)} %get-tuple-element.49), channel_id=1, source_target_pairs={{0,12},{4,0},{8,4},{12,8},{1,13},{5,1},{9,5},{13,9},{2,14},{6,2},{... | collective-permute-start | bytes 1032200 | tf_op jit(solution)/shard_map/ppermute | solution.py:448
  55.6 3.0 %collective-permute-start.5 = (bf16[8,64,256]{2,1,0:T(8,128)(2,1)S(1)}, bf16[8,64,256]{2,1,0:T(8,128)(2,1)S(1)}, u32[]{:S(2)}, u32[]{:S(2)}) collective-permute-start(bf16[8,64,256]{2,1,0:T(8,128)(2,1)S(1)} %all-to-all-done.1.b0), channel_id=1, source_target_pairs={{0,1},{1,0},{2,3},{3,2},{4,5},{5,4},{6,7},{7,6},{8,9},{9,8},{10,11... | collective-permute-start | bytes 786440 | tf_op jit(solution)/shard_map/ppermute | solution.py:444
  57.5 1.8 %collective-permute-start.6 = (bf16[8,64,256]{2,1,0:T(8,128)(2,1)S(1)}, bf16[8,64,256]{2,1,0:T(8,128)(2,1)S(1)}, u32[]{:S(2)}, u32[]{:S(2)}) collective-permute-start(bf16[8,64,256]{2,1,0:T(8,128)(2,1)S(1)} %collective-permute-done.3.b2), channel_id=1, source_target_pairs={{0,1},{1,0},{2,3},{3,2},{4,5},{5,4},{6,7},{7,6},{8,9},{9,8},{10,11... | collective-permute-start | bytes 786440 | tf_op jit(solution)/shard_map/ppermute | solution.py:444
  59.3 10.6 %copy-start.7 = (f32[128,768]{1,0:T(8,128)S(1)}, f32[128,768]{1,0:T(8,128)}, u32[]{:S(2)}) copy-start(f32[128,768]{1,0:T(8,128)} %get-tuple-element.50.gate_ref) | copy-start | bytes 1179652
  59.3 10.6 %copy-start.8 = (bf16[128,768]{1,0:T(8,128)(2,1)S(1)}, bf16[128,768]{1,0:T(8,128)(2,1)}, u32[]{:S(2)}) copy-start(bf16[128,768]{1,0:T(8,128)(2,1)} %get-tuple-element.46.a) | copy-start | bytes 589828
  65.2 14.1 %all-to-all-start.2 = ((bf16[8,48,256]{2,1,0:T(8,128)(2,1)}), bf16[8,48,256]{2,1,0:T(8,128)(2,1)S(1)}, u32[]{:S(2)}, u32[]{:S(2)}) async-start(bf16[8,48,256]{2,1,0:T(8,128)(2,1)} %attention.1), calls=%async_computation.2 | async-start | bytes 393216 | tf_op jit(solution)/shard_map/all_to_all | solution.py:511
  70.0 9.4 %copy-start.2 = (f32[192,512]{1,0:T(8,128)S(1)}, f32[192,512]{1,0:T(8,128)}, u32[]{:S(2)}) copy-start(f32[192,512]{1,0:T(8,128)} %get-tuple-element.29.gate_ref) | copy-start | bytes 1179652
  70.1 23.8 %copy-start.1 = (bf16[3,96,768]{2,1,0:T(8,128)(2,1)}, bf16[3,96,768]{2,1,0:T(8,128)(2,1)S(1)}, u32[]{:S(2)}) copy-start(bf16[3,96,768]{2,1,0:T(8,128)(2,1)S(1)} %get-tuple-element.51.wa) | copy-start | bytes 1327108
  70.1 23.8 %copy-start.3 = (bf16[128,768]{1,0:T(8,128)(2,1)}, bf16[128,768]{1,0:T(8,128)(2,1)S(1)}, u32[]{:S(2)}) copy-start(bf16[128,768]{1,0:T(8,128)(2,1)S(1)} %get-tuple-element.52.t0) | copy-start | bytes 589828
  70.1 16.0 %collective-permute-start.13 = (bf16[3,96,768]{2,1,0:T(8,128)(2,1)S(1)}, bf16[3,96,768]{2,1,0:T(8,128)(2,1)S(1)}, u32[]{:S(2)}, u32[]{:S(2)}) collective-permute-start(bf16[3,96,768]{2,1,0:T(8,128)(2,1)S(1)} %get-tuple-element.51.wa), channel_id=1, source_target_pairs={{0,1},{1,0},{2,3},{3,2},{4,5},{5,4},{6,7},{7,6},{8,9},{9,8},{10,11... | collective-permute-start | bytes 1327112 | tf_op jit(solution)/shard_map/ppermute | solution.py:444
  71.4 10.8 %collective-permute-start.14 = (bf16[128,768]{1,0:T(8,128)(2,1)S(1)}, bf16[128,768]{1,0:T(8,128)(2,1)S(1)}, u32[]{:S(2)}, u32[]{:S(2)}) collective-permute-start(bf16[128,768]{1,0:T(8,128)(2,1)S(1)} %get-tuple-element.52.t0), channel_id=1, source_target_pairs={{0,12},{4,0},{8,4},{12,8},{1,13},{5,1},{9,5},{13,9},{2,14},{6,2},{... | collective-permute-start | bytes 589832 | tf_op jit(solution)/shard_map/ppermute | solution.py:448
  73.6 8.9 %collective-permute-start.15 = (bf16[128,768]{1,0:T(8,128)(2,1)S(1)}, bf16[128,768]{1,0:T(8,128)(2,1)S(1)}, u32[]{:S(2)}, u32[]{:S(2)}) collective-permute-start(bf16[128,768]{1,0:T(8,128)(2,1)S(1)} %get-tuple-element.52.t0), channel_id=1, source_target_pairs={{0,8},{4,12},{8,0},{12,4},{1,9},{5,13},{9,1},{13,5},{2,10},{6,14},... | collective-permute-start | bytes 589832 | tf_op jit(solution)/shard_map/ppermute | solution.py:448
  74.1 12.1 %collective-permute-start.16 = (bf16[128,768]{1,0:T(8,128)(2,1)S(1)}, bf16[128,768]{1,0:T(8,128)(2,1)S(1)}, u32[]{:S(2)}, u32[]{:S(2)}) collective-permute-start(bf16[128,768]{1,0:T(8,128)(2,1)S(1)} %get-tuple-element.52.t0), channel_id=1, source_target_pairs={{0,4},{4,8},{8,12},{12,0},{1,5},{5,9},{9,13},{13,1},{2,6},{6,10},{... | collective-permute-start | bytes 589832 | tf_op jit(solution)/shard_map/ppermute | solution.py:448
  79.4 14.6 %copy-start = (bf16[192,512]{1,0:T(8,128)(2,1)}, bf16[192,512]{1,0:T(8,128)(2,1)S(1)}, u32[]{:S(2)}) copy-start(bf16[192,512]{1,0:T(8,128)(2,1)S(1)} %mix.1.m0) | copy-start | bytes 589828
  79.4 6.8 %collective-permute-start.7 = (bf16[192,512]{1,0:T(8,128)(2,1)S(1)}, bf16[192,512]{1,0:T(8,128)(2,1)S(1)}, u32[]{:S(2)}, u32[]{:S(2)}) collective-permute-start(bf16[192,512]{1,0:T(8,128)(2,1)S(1)} %mix.1.m0), channel_id=1, source_target_pairs={{0,12},{4,0},{8,4},{12,8},{1,13},{5,1},{9,5},{13,9},{2,14},{6,2},{... | collective-permute-start | bytes 589832 | tf_op jit(solution)/shard_map/ppermute | solution.py:448
  82.2 11.7 %copy-start.11 = (bf16[128,768]{1,0:T(8,128)(2,1)}, bf16[128,768]{1,0:T(8,128)(2,1)S(1)}, u32[]{:S(2)}) copy-start(bf16[128,768]{1,0:T(8,128)(2,1)S(1)} %collective-permute-done.14.t1) | copy-start | bytes 589828
  82.2 6.1 %collective-permute-start.8 = (bf16[192,512]{1,0:T(8,128)(2,1)S(1)}, bf16[192,512]{1,0:T(8,128)(2,1)S(1)}, u32[]{:S(2)}, u32[]{:S(2)}) collective-permute-start(bf16[192,512]{1,0:T(8,128)(2,1)S(1)} %mix.1.m0), channel_id=1, source_target_pairs={{0,8},{4,12},{8,0},{12,4},{1,9},{5,13},{9,1},{13,5},{2,10},{6,14},... | collective-permute-start | bytes 589832 | tf_op jit(solution)/shard_map/ppermute | solution.py:448
  82.5 11.4 %copy-start.12 = (bf16[128,768]{1,0:T(8,128)(2,1)}, bf16[128,768]{1,0:T(8,128)(2,1)S(1)}, u32[]{:S(2)}) copy-start(bf16[128,768]{1,0:T(8,128)(2,1)S(1)} %collective-permute-done.15.t2) | copy-start | bytes 589828
  82.5 11.4 %collective-permute-start.9 = (bf16[192,512]{1,0:T(8,128)(2,1)S(1)}, bf16[192,512]{1,0:T(8,128)(2,1)S(1)}, u32[]{:S(2)}, u32[]{:S(2)}) collective-permute-start(bf16[192,512]{1,0:T(8,128)(2,1)S(1)} %mix.1.m0), channel_id=1, source_target_pairs={{0,4},{4,8},{8,12},{12,0},{1,5},{5,9},{9,13},{13,1},{2,6},{6,10},{... | collective-permute-start | bytes 589832 | tf_op jit(solution)/shard_map/ppermute | solution.py:448
  86.2 7.8 %copy-start.13 = (bf16[128,768]{1,0:T(8,128)(2,1)}, bf16[128,768]{1,0:T(8,128)(2,1)S(1)}, u32[]{:S(2)}) copy-start(bf16[128,768]{1,0:T(8,128)(2,1)S(1)} %collective-permute-done.16.t3) | copy-start | bytes 589828
  86.2 7.8 %copy-start.10 = (bf16[3,96,768]{2,1,0:T(8,128)(2,1)}, bf16[3,96,768]{2,1,0:T(8,128)(2,1)S(1)}, u32[]{:S(2)}) copy-start(bf16[3,96,768]{2,1,0:T(8,128)(2,1)S(1)} %collective-permute-done.13.wb) | copy-start | bytes 1327108
  86.2 7.8 %copy-start.14 = (bf16[192,512]{1,0:T(8,128)(2,1)}, bf16[192,512]{1,0:T(8,128)(2,1)S(1)}, u32[]{:S(2)}) copy-start(bf16[192,512]{1,0:T(8,128)(2,1)S(1)} %collective-permute-done.7.m1) | copy-start | bytes 589828
  88.3 5.7 %copy-start.15 = (bf16[192,512]{1,0:T(8,128)(2,1)}, bf16[192,512]{1,0:T(8,128)(2,1)S(1)}, u32[]{:S(2)}) copy-start(bf16[192,512]{1,0:T(8,128)(2,1)S(1)} %collective-permute-done.8.m2) | copy-start | bytes 589828
  94.0 0.7 copy-start.16
